TPU v7x, 32 devices: a whole 2x2x4 slice. The times are simulated.
32 devices in a mesh: groups: 2 (over x), seq: 16 (over z, y, core).
Axes of the slice: x: 2, y: 2, z: 4, core: 2. Of those that a mesh axis runs over, the one named last changes fastest.
Arguments:
- spectral: bfloat16 [8192, 4096], P(('groups', 'seq')), parts along dimension 0, may hold values from -25 to 25
- recording_lengths: int32 [8], P('groups'), parts along dimension 0, may hold values from 1 to 1024, as said below
- expert_ids: int32 [4096, 8], P(('groups', 'seq')), parts along dimension 0, may hold values from 0 to 15, all different within a row; in each aligned block of 128 rows (0 to 127, 128 to 255, ...) at most 65 rows name the same one
- gate_weights: float32 [4096, 8], P(('groups', 'seq')), parts along dimension 0, may hold values from 0.05 to 0.5
- conv_weight: bfloat16 [2304, 256], P('seq'), may hold values from -0.125 to 0.125
- conv_proj: bfloat16 [2048, 1280], P('seq'), may hold values from -0.125 to 0.125
- ln_gain: float32 [1280], replicated, may hold values from 0.25 to 1.75
- attn_in: bfloat16 [1280, 1920], P('seq'), may hold values from -8 to 8
- attn_out: bfloat16 [640, 1280], P('seq'), may hold values from -0.25 to 0.25
- audio_proj: bfloat16 [1280, 2048], P('seq'), may hold values from -0.15625 to 0.15625
- rms_gain: float32 [2048], replicated, may hold values from 0.25 to 1.75
- w_gate_up: bfloat16 [16, 2048, 1536], P('seq'), may hold values from -0.125 to 0.125
- w_down: bfloat16 [16, 768, 2048], P('seq'), may hold values from -0.21875 to 0.21875
Outputs:
- thinker_out: bfloat16 [4096, 2048], P(('groups', 'seq')), parts along dimension 0
There are 2 independent parts, one for each index of `groups`. A program takes and returns all parts, laid end to end along the dimension named above; an argument that names none is the same for every part. Nothing has to cross between parts.
Inputs may be any that keep to these rules, and one draw needn't show every extreme that they name: `expert_ids`: each row names 8 different experts; in each aligned block of 128 rows (the rows of one device) no expert is named by more than 65 rows, a bound that some block reaches. `recording_lengths`: the lengths sum to 2048; the second recording is the longest, exactly 1024 tokens.
All inputs are finite; a program needn't handle non-finite values.
Results may differ from a plain program's by a relative error of at most 0.017.
Values may be sent and summed in bfloat16 or wider, within the bound.
No kernel may reach another device: no remote copies, remote signals or barrier semaphores. Data moves between devices by JAX's collectives and lax.ppermute only.
A program may use at most 128 MiB of HBM per device.

v0:
```python
import functools

import jax
import jax.numpy as jnp
from jax import lax
from jax.experimental import pallas as pl
from jax.experimental.pallas import tpu as pltpu
from jax.sharding import PartitionSpec as P

HEADS = 10
HDIM = 64
WIN = 128


def shifted(block, axis, distance):
    devices = range(lax.axis_size(axis))
    route = [(i - distance, i) for i in devices if i - distance in devices]
    return lax.ppermute(block, axis, route)


def padded(cells, sides, width):
    for axis, dim in sides:
        count = lax.axis_size(axis)
        ends = count - 1
        head = lax.slice_in_dim(cells, 0, width, axis=dim)
        tail = lax.slice_in_dim(cells, cells.shape[dim] - width, cells.shape[dim], axis=dim)
        cells = jnp.concatenate(
            [
                lax.ppermute(tail, axis, [(i, (i + 1) % count) for i in range(ends)]),
                cells,
                lax.ppermute(head, axis, [((i + 1) % count, i) for i in range(ends)]),
            ],
            axis=dim,
        )
    return cells


def layer_norm(values):
    mean = jnp.mean(values, -1, keepdims=True)
    centered = values - mean
    variance = jnp.mean(centered * centered, -1, keepdims=True)
    return centered * lax.rsqrt(variance + 1e-05)


def rms_norm(values, gain):
    scaled = values.astype(jnp.float32)
    power = jnp.mean(scaled * scaled, -1, keepdims=True)
    return (scaled * lax.rsqrt(power + 1e-06) * gain).astype(jnp.bfloat16)


def recording_of(positions, ends):
    return jnp.sum((positions[:, None] >= ends[None, :]).astype(jnp.int32), 1)


def attend(query_rows, key_rows, query_pos, key_pos, ends, total):
    width = HEADS * HDIM
    count = query_rows.shape[0]
    keys_count = key_rows.shape[0]
    query = query_rows.reshape(count, HEADS, HDIM)
    keys = key_rows[:, :width].reshape(keys_count, HEADS, HDIM)
    values = key_rows[:, width:].reshape(keys_count, HEADS, HDIM)
    scores = jnp.einsum("qhd,khd->hqk", query, keys, preferred_element_type=jnp.float32) * HDIM ** (
        -0.5
    )
    same = recording_of(query_pos, ends)[:, None] == recording_of(key_pos, ends)[None, :]
    near = jnp.abs(query_pos[:, None] - key_pos[None, :]) <= WIN
    inside = (key_pos >= 0) & (key_pos < total)
    valid = same & near & inside[None, :]
    scores = jnp.where(valid[None], scores, -1e30)
    top = jnp.max(scores, -1, keepdims=True)
    weights = jnp.exp(scores - top)
    probs = (weights / jnp.sum(weights, -1, keepdims=True)).astype(jnp.bfloat16)
    context = jnp.einsum("hqk,khd->qhd", probs, values, preferred_element_type=jnp.float32)
    return context.reshape(count, width).astype(jnp.bfloat16)


def expert_ffn(rows, gate_up, down):
    both = jnp.dot(rows, gate_up, preferred_element_type=jnp.float32)
    inner = down.shape[0]
    hidden = (jax.nn.silu(both[:, :inner]) * both[:, inner:]).astype(jnp.bfloat16)
    return jnp.dot(hidden, down, preferred_element_type=jnp.float32).astype(jnp.bfloat16)


def fold_with(left, piece):
    return jnp.dot(left, piece, preferred_element_type=jnp.float32)


def ring_step(block, stride, size):
    route = []
    for i in range(lax.axis_size("seq")):
        place = i // stride % size
        route.append((i, i + ((place + 1) % size - place) * stride))
    return lax.ppermute(block, "seq", route)


def levels(devices):
    core = 2
    rest = devices // core
    y = 1
    while (2 * y) * (2 * y) <= rest:
        y *= 2
    return rest // y, y, core


def gate_table(expert_ids, gate_weights, experts):
    named = expert_ids[None] == jnp.arange(experts, dtype=jnp.int32)[:, None, None]
    return jnp.sum(jnp.where(named, gate_weights[None], 0.0), -1)


def spread_gates(table):
    zs, ys, cores = levels(lax.axis_size("seq"))
    blocks = [table]
    for _ in range(zs - 1):
        blocks.append(ring_step(blocks[-1], ys * cores, zs))
    line = [jnp.stack(blocks)]
    for _ in range(ys - 1):
        line.append(ring_step(line[-1], cores, ys))
    both = jnp.stack(line)
    both = jnp.stack([both, ring_step(both, 1, cores)])
    mine = lax.dynamic_index_in_dim(both, lax.axis_index("seq"), 3, keepdims=False)
    return [mine[:, :, k].reshape(-1) for k in range(zs)]


def dense_experts(audio_embed, scaled, gates, fused, down):
    devices = lax.axis_size("seq")
    zs, ys, cores = levels(devices)
    tokens = scaled.shape[0]
    inner = down.shape[0]
    width = down.shape[1]
    blocks = [scaled]
    for _ in range(zs - 1):
        blocks.append(ring_step(blocks[-1], ys * cores, zs))
    chunks = []
    for block in blocks:
        line = [block]
        for _ in range(ys - 1):
            line.append(ring_step(line[-1], cores, ys))
        pair = jnp.stack(line)
        chunks.append(jnp.stack([pair, ring_step(pair, 1, cores)]))
    carry = None
    crossed = []
    columns = {}
    for k in list(range(1, zs)) + [0]:
        rows = chunks[k].reshape(-1, scaled.shape[1])
        weight = gates[k][:, None]
        both = jnp.dot(rows, fused, preferred_element_type=jnp.float32)
        hidden = (jax.nn.silu(both[:, :inner]) * both[:, inner:] * weight).astype(jnp.bfloat16)
        sums = jnp.dot(hidden, down, preferred_element_type=jnp.float32).astype(jnp.bfloat16)
        sums = sums.reshape(cores, ys, tokens, width)
        theirs = ring_step(sums[1], 1, cores)
        crossed.append(theirs)
        chip = sums[0].astype(jnp.float32) + theirs.astype(jnp.float32)
        column = chip[1 % ys]
        for dy in range(1, ys):
            moved = ring_step(column.astype(jnp.bfloat16), cores, ys)
            column = moved.astype(jnp.float32) + chip[(dy + 1) % ys]
        columns[k] = column
    for k in list(range(1, zs)) + [0]:
        column = columns[k]
        if carry is not None:
            column = column + carry.astype(jnp.float32)
        if k:
            carry = ring_step(column.astype(jnp.bfloat16), ys * cores, zs)
    return (audio_embed.astype(jnp.float32) + column).astype(jnp.bfloat16)


def hop(block, stride, size, distance):
    route = []
    for i in range(lax.axis_size("seq")):
        place = i // stride % size
        route.append((i, i + ((place + distance) % size - place) * stride))
    return lax.ppermute(block, "seq", route)


def after(block, *others):
    return lax.optimization_barrier((block, *others))[0]


def spread(block, halves=1, late=None):
    zs, ys, cores = levels(lax.axis_size("seq"))
    if halves > 1:
        rows = block.shape[0] // halves
        block = lax.dynamic_slice_in_dim(block, lax.axis_index("groups") * rows, rows, 0)
    far = [hop(block, ys * cores, zs, k) for k in range(1, zs)]
    side = [hop(block, cores, ys, j) for j in range(1, ys)]
    stacks = [jnp.stack([block, *side, *far])]
    names = [[(0, j, 0, 0) for j in range(ys)] + [(k, 0, 0, 0) for k in range(1, zs)]]
    for j in range(1, ys):
        stacks.append(hop(stacks[0][ys:], cores, ys, j))
        names.append([(k, j, 0, 0) for k in range(1, zs)])
    if halves > 1:
        for i in range(len(stacks)):
            stacks.append(lax.ppermute(stacks[i], "groups", [(0, 1), (1, 0)]))
            names.append([(k, j, 0, 1) for k, j, _, _ in names[i]])
    for i in range(len(stacks)):
        sent = stacks[i] if late is None else after(stacks[i], late())
        stacks.append(hop(sent, 1, cores, 1))
        names.append([(k, j, 1, dx) for k, j, _, dx in names[i]])
    return stacks, names


def put_in_place(names, place, pieces, full, sems):
    halves = 1 + max(name[3] for stack in names for name in stack)
    rows = pieces[0].shape[1]
    zs, ys, cores = levels(full.shape[0] // (halves * rows))
    z, y, core, group = place[0], place[1], place[2], place[3]
    copies = []
    for piece, stack in zip(pieces, names):
        for i, (k, dy, dc, dx) in enumerate(stack):
            index = lax.rem(z - k + zs, zs) * ys + lax.rem(y - dy + ys, ys)
            index = index * cores + lax.rem(core - dc + cores, cores)
            start = index * (rows * halves)
            if halves > 1:
                start = start + lax.rem(group - dx + halves, halves) * rows
            copies.append(
                pltpu.make_async_copy(
                    piece.at[i],
                    full.at[pl.ds(pl.multiple_of(start, rows), rows)],
                    sems.at[len(copies)],
                )
            )
    for copy in copies:
        copy.start()
    for copy in copies:
        copy.wait()


def norm_rows(values):
    mean = jnp.mean(values, -1, keepdims=True)
    centered = values - mean
    variance = jnp.mean(centered * centered, -1, keepdims=True)
    return centered * lax.rsqrt(variance + 1e-05)


def conv_kernel(names, place, frames, rim, *refs):
    pieces, (out, taps, weight, sems) = refs[: len(names)], refs[-4:]
    tokens = out.shape[0]
    channels = weight.shape[1]
    bins = out.shape[1] // channels
    row = lax.broadcasted_iota(jnp.int32, (tokens, 2 * tokens), 0)
    column = lax.broadcasted_iota(jnp.int32, (tokens, 2 * tokens), 1)
    first = lax.broadcasted_iota(jnp.int32, (tokens, 2 * channels), 0) == 0
    for a in range(3):
        pick = jnp.where(column == 2 * row + a - 1, 1.0, 0.0).astype(jnp.bfloat16)
        taps[a, :tokens, :] = jnp.zeros((tokens, 2 * channels), jnp.bfloat16)
        for f in range(bins):
            span = slice(2 * f * channels, 2 * (f + 1) * channels)
            part = jnp.dot(pick, frames[:, span], preferred_element_type=jnp.float32)
            if a == 0:
                part = jnp.where(first, rim[:, span].astype(jnp.float32), part)
            taps[a, (f + 1) * tokens : (f + 2) * tokens, :] = part.astype(jnp.bfloat16)
    put_in_place(names, place, pieces, weight, sems)
    half = bins // 2 * tokens
    for part in range(2):
        total = jnp.zeros((half, channels), jnp.float32)
        low = part * half
        for a in range(3):
            base = 3 * a * channels
            total += jnp.dot(
                taps[a, low + tokens : low + tokens + half, :],
                weight[base + channels : base + 3 * channels],
                preferred_element_type=jnp.float32,
            )
            total += jnp.dot(
                taps[a, low : low + half, channels:],
                weight[base : base + channels],
                preferred_element_type=jnp.float32,
            )
        act = (0.5 * total * (1.0 + lax.erf(total * 0.7071067811865476))).astype(jnp.bfloat16)
        for f in range(bins // 2):
            where = (part * (bins // 2) + f) * channels
            out[:, where : where + channels] = act[f * tokens : (f + 1) * tokens]


def fetch(gathered, rows, first, full, sems):
    copies = [
        pltpu.make_async_copy(
            gathered.at[i, :rows, first : first + full.shape[1]],
            full.at[i * rows : (i + 1) * rows],
            sems.at[i],
        )
        for i in range(gathered.shape[0])
    ]
    for copy in copies:
        copy.start()
    for copy in copies:
        copy.wait()


def embed_kernel(rows, act, gain, gathered, embed, normed, weight, sems):
    fetch(gathered, rows, 0, weight, sems)
    step = 256
    for low in range(0, embed.shape[1], step):
        span = slice(low, low + step)
        sums = jnp.dot(act[...], weight[:, span], preferred_element_type=jnp.float32)
        embed[:, span] = sums.astype(jnp.bfloat16)
    kept = embed[...].astype(jnp.float32)
    normed[...] = (norm_rows(kept) * gain[...]).astype(jnp.bfloat16)


def qkv_kernel(first, normed, gathered, query, key_rows, weight, sems):
    fetch(gathered, weight.shape[0] // gathered.shape[0], first, weight, sems)
    width = query.shape[1]
    query[...] = jnp.dot(
        normed[...], weight[:, :width], preferred_element_type=jnp.float32
    ).astype(jnp.bfloat16)
    key_rows[...] = jnp.dot(
        normed[...], weight[:, width:], preferred_element_type=jnp.float32
    ).astype(jnp.bfloat16)


def attend_kernel(total, ends, first, query, left, own, right, embed, out_proj, *refs):
    encoded, post, ctx = refs[-3:]
    tokens, width = query.shape
    reach = left.shape[0]
    keys = tokens + 2 * reach
    query_pos = first[0] + lax.broadcasted_iota(jnp.int32, (tokens, keys), 0)
    key_pos = first[0] - reach + lax.broadcasted_iota(jnp.int32, (tokens, keys), 1)
    query_rec = jnp.zeros((tokens, keys), jnp.int32)
    key_rec = jnp.zeros((tokens, keys), jnp.int32)
    for r in range(ends.shape[0]):
        query_rec += (query_pos >= ends[r]).astype(jnp.int32)
        key_rec += (key_pos >= ends[r]).astype(jnp.int32)
    near = jnp.abs(query_pos - key_pos) <= WIN
    valid = (query_rec == key_rec) & near & (key_pos >= 0) & (key_pos < total)
    low = lax.broadcasted_iota(jnp.int32, (tokens, 2 * HDIM), 1) < HDIM
    sides = (left, own, right)
    for pair in range(HEADS // 2):
        span = slice(pair * 2 * HDIM, (pair + 1) * 2 * HDIM)
        values = slice(width + span.start, width + span.stop)
        both = query[:, span].astype(jnp.float32)
        mixed = []
        for head in range(2):
            mine = low if head == 0 else jnp.logical_not(low)
            one = jnp.where(mine, both, 0.0).astype(jnp.bfloat16)
            scores = jnp.concatenate(
                [
                    lax.dot_general(
                        one,
                        side[:, span],
                        (((1,), (1,)), ((), ())),
                        preferred_element_type=jnp.float32,
                    )
                    for side in sides
                ],
                1,
            )
            scores = jnp.where(valid, scores * HDIM ** (-0.5), -1e30)
            weights = jnp.exp(scores - jnp.max(scores, -1, keepdims=True))
            probs = (weights / jnp.sum(weights, -1, keepdims=True)).astype(jnp.bfloat16)
            context = jnp.zeros((tokens, 2 * HDIM), jnp.float32)
            start = 0
            for side in sides:
                stop = start + side.shape[0]
                context += jnp.dot(
                    probs[:, start:stop], side[:, values], preferred_element_type=jnp.float32
                )
                start = stop
            mixed.append(context)
        ctx[:, span] = jnp.where(low, mixed[0], mixed[1]).astype(jnp.bfloat16)
    branch = jnp.dot(ctx[...], out_proj[...], preferred_element_type=jnp.float32)
    kept = (embed[...].astype(jnp.float32) + branch).astype(jnp.bfloat16)
    encoded[...] = kept
    post[...] = norm_rows(kept.astype(jnp.float32)).astype(jnp.bfloat16)


SMEM = pl.BlockSpec(memory_space=pltpu.SMEM)
VMEM = pl.BlockSpec(memory_space=pltpu.VMEM)
ANY = pl.BlockSpec(memory_space=pl.ANY)
HBM = pl.BlockSpec(memory_space=pltpu.HBM)


def room(mib):
    return pltpu.CompilerParams(vmem_limit_bytes=mib * 2**20)


def rows_of(*shape):
    return jax.ShapeDtypeStruct(shape, jnp.bfloat16)


def with_pieces(kernel, mib, place, operands, spreads, full, outs, scratch=(), first=()):
    flops = 2 * operands[0].shape[0] * full[0] * full[1]
    pieces, names = spreads
    copies = sum(len(stack) for stack in names)
    return pl.pallas_call(
        functools.partial(kernel, names),
        out_shape=outs,
        in_specs=[SMEM] + [VMEM] * len(operands) + [ANY] * (len(pieces) + len(first)),
        out_specs=jax.tree.map(lambda _: VMEM, outs),
        scratch_shapes=[
            *scratch,
            pltpu.VMEM(full, jnp.bfloat16),
            pltpu.SemaphoreType.DMA((copies,)),
        ],
        compiler_params=room(mib),
        cost_estimate=pl.CostEstimate(
            flops=4 * flops, bytes_accessed=4 * full[0] * full[1], transcendentals=0
        ),
    )(place, *operands, *pieces, *first)


def dense_device(
    spectral,
    recording_lengths,
    expert_ids,
    gate_weights,
    conv_weight,
    conv_proj,
    ln_gain,
    attn_in,
    attn_out,
    audio_proj,
    rms_gain,
    w_gate_up,
    w_down,
):
    devices = lax.axis_size("seq")
    zs, ys, cores = levels(devices)
    tokens = expert_ids.shape[0]
    experts = devices * w_down.shape[0]
    width = HEADS * HDIM
    channels = conv_weight.shape[1]
    bins = spectral.shape[1] // channels // 2
    me = lax.axis_index("seq")
    place = jnp.stack(
        [me // (ys * cores), me // cores % ys, me % cores, lax.axis_index("groups")]
    ).astype(jnp.int32)
    rim = shifted(spectral[-1:], "seq", 1)
    rows, wide, dim = attn_in.shape[0], attn_in.shape[1], conv_proj.shape[1]
    high, thin, broad = conv_proj.shape[0], attn_out.shape[0], audio_proj.shape[1]
    deep = -(-max(high + thin, 2 * rows) // 16) * 16
    packed = jnp.concatenate(
        [
            jnp.pad(jnp.concatenate([conv_proj, attn_out]), ((0, deep - high - thin), (0, 0))),
            jnp.pad(
                jnp.concatenate([jnp.pad(attn_in, ((0, 0), (0, broad - wide))), audio_proj]),
                ((0, deep - 2 * rows), (0, 0)),
            ),
        ],
        1,
    )
    late_full = lax.all_gather(packed, "seq", axis=0)
    audio_full = late_full[:, rows : 2 * rows, dim:].reshape(-1, broad)
    out_full = late_full[:, high : high + thin, :dim].reshape(-1, dim)
    conv_pieces = spread(conv_weight)
    gates = spread_gates(gate_table(expert_ids, gate_weights, experts))
    conv_act = with_pieces(
        conv_kernel,
        16,
        place,
        [spectral, rim],
        conv_pieces,
        (devices * conv_weight.shape[0], channels),
        rows_of(tokens, bins * channels),
        [pltpu.VMEM((3, (bins + 1) * tokens, 2 * channels), jnp.bfloat16)],
        gates,
    )
    embed, normed = pl.pallas_call(
        functools.partial(embed_kernel, high),
        out_shape=(rows_of(tokens, dim), rows_of(tokens, dim)),
        in_specs=[VMEM, VMEM, HBM],
        out_specs=(VMEM, VMEM),
        scratch_shapes=[
            pltpu.VMEM((devices * high, dim), jnp.bfloat16),
            pltpu.SemaphoreType.DMA((devices,)),
        ],
        compiler_params=room(46),
        cost_estimate=pl.CostEstimate(
            flops=4 * 10**9, bytes_accessed=5 * 10**6, transcendentals=0
        ),
    )(conv_act, ln_gain[None], late_full)
    query, key_rows = pl.pallas_call(
        functools.partial(qkv_kernel, dim),
        out_shape=(rows_of(tokens, width), rows_of(tokens, 2 * width)),
        in_specs=[VMEM, HBM],
        out_specs=(VMEM, VMEM),
        scratch_shapes=[
            pltpu.VMEM((devices * rows, wide), jnp.bfloat16),
            pltpu.SemaphoreType.DMA((devices,)),
        ],
        compiler_params=room(46),
        cost_estimate=pl.CostEstimate(
            flops=4 * 10**9, bytes_accessed=5 * 10**6, transcendentals=0
        ),
    )(normed, late_full)
    left = shifted(key_rows[-WIN:], "seq", 1)
    right = shifted(key_rows[:WIN], "seq", -1)
    ends = jnp.cumsum(recording_lengths).astype(jnp.int32)
    weighted = (w_gate_up[0] * rms_gain[:, None]).astype(jnp.bfloat16)
    fused = jnp.dot(audio_full, weighted, preferred_element_type=jnp.float32)
    fused = fused.astype(jnp.bfloat16)
    encoded, post = pl.pallas_call(
        functools.partial(attend_kernel, devices * tokens),
        out_shape=(rows_of(tokens, dim), rows_of(tokens, dim)),
        in_specs=[SMEM, SMEM] + [VMEM] * 6 + [ANY],
        out_specs=(VMEM, VMEM),
        scratch_shapes=[pltpu.VMEM((tokens, width), jnp.bfloat16)],
        compiler_params=room(8),
        cost_estimate=pl.CostEstimate(
            flops=4 * 10**9, bytes_accessed=4 * 10**6, transcendentals=0
        ),
    )(ends, (me * tokens)[None].astype(jnp.int32), query, left, key_rows, right, embed, out_full, fused)
    audio_sum = jnp.dot(post, audio_full, preferred_element_type=jnp.float32)
    audio_embed = audio_sum.astype(jnp.bfloat16)
    power = jnp.mean(jnp.square(audio_embed.astype(jnp.float32)), -1, keepdims=True)
    scaled = (post.astype(jnp.float32) * lax.rsqrt(power + 1e-06)).astype(jnp.bfloat16)
    return dense_experts(audio_embed, scaled, gates, fused, w_down[0])


def routed_device(
    spectral,
    recording_lengths,
    expert_ids,
    gate_weights,
    conv_weight,
    conv_proj,
    ln_gain,
    attn_in,
    attn_out,
    audio_proj,
    rms_gain,
    w_gate_up,
    w_down,
):
    devices = lax.axis_size("seq")
    local_tokens = expert_ids.shape[0]
    topk = expert_ids.shape[1]
    experts = devices * w_down.shape[0]
    slots = local_tokens * topk // experts + 1
    width = HEADS * HDIM
    channels = conv_weight.shape[1]
    freq_in = spectral.shape[1] // channels
    freq_out = freq_in // 2
    thinker_width = audio_proj.shape[1]
    proj_full = lax.all_gather(audio_proj, "seq", axis=0, tiled=True)
    frame_rim = shifted(spectral[-1:], "seq", 1)
    extended = jnp.concatenate([frame_rim, spectral], 0).reshape(
        2 * local_tokens + 1, freq_in, channels
    )
    extended = jnp.pad(extended, ((0, 0), (1, 0), (0, 0)))
    tap_list = []
    for across in range(3):
        row_set = extended[across : across + 2 * local_tokens : 2]
        for along in range(3):
            tap_list.append(row_set[:, along : along + freq_in : 2, :])
    patches = jnp.concatenate(tap_list, 2).reshape(local_tokens * freq_out, 9 * channels)
    conv_sum = fold_with(patches, lax.all_gather(conv_weight, "seq", axis=0, tiled=True))
    conv_act = (
        jax.nn.gelu(conv_sum, approximate=False)
        .astype(jnp.bfloat16)
        .reshape(local_tokens, freq_out * channels)
    )
    embed_sum = fold_with(conv_act, lax.all_gather(conv_proj, "seq", axis=0, tiled=True))
    embed = embed_sum.astype(jnp.bfloat16)
    normed = (layer_norm(embed.astype(jnp.float32)) * ln_gain).astype(jnp.bfloat16)
    qkv_sum = fold_with(normed, lax.all_gather(attn_in, "seq", axis=0, tiled=True))
    qkv = qkv_sum.astype(jnp.bfloat16)
    key_rows = padded(qkv[:, width:], (("seq", 0),), WIN)
    ends = jnp.cumsum(recording_lengths)
    first = lax.axis_index("seq") * local_tokens
    query_pos = first + jnp.arange(local_tokens, dtype=jnp.int32)
    key_pos = first - WIN + jnp.arange(local_tokens + 2 * WIN, dtype=jnp.int32)
    context = attend(qkv[:, :width], key_rows, query_pos, key_pos, ends, devices * local_tokens)
    branch_sum = fold_with(context, lax.all_gather(attn_out, "seq", axis=0, tiled=True))
    encoded = (embed.astype(jnp.float32) + branch_sum).astype(jnp.bfloat16)
    post = layer_norm(encoded.astype(jnp.float32)).astype(jnp.bfloat16)
    audio_embed = jnp.dot(post, proj_full, preferred_element_type=jnp.float32).astype(jnp.bfloat16)
    flat_ids = expert_ids.reshape(-1)
    onehot = (flat_ids[:, None] == jnp.arange(experts, dtype=jnp.int32)[None, :]).astype(jnp.int32)
    before = jnp.cumsum(onehot, 0) - onehot
    position = jnp.sum(before * onehot, 1)
    slot_index = flat_ids * slots + position
    owner = jnp.full((experts * slots,), local_tokens * topk, jnp.int32)
    owner = owner.at[slot_index].set(jnp.arange(local_tokens * topk, dtype=jnp.int32))
    owner_rows = owner // topk
    gate_up_local = w_gate_up[0]
    down_local = w_down[0]
    sent_rows = rms_norm(audio_embed, rms_gain)
    padded_rows = jnp.concatenate([sent_rows, jnp.zeros((1, sent_rows.shape[1]), jnp.bfloat16)], 0)
    send_buffer = padded_rows[owner_rows].reshape(experts, slots, sent_rows.shape[1])
    received = lax.all_to_all(send_buffer, "seq", split_axis=0, concat_axis=0, tiled=True)
    rows = received.reshape(-1, received.shape[-1])
    result = expert_ffn(rows, gate_up_local, down_local)
    results = result.reshape(received.shape[0], received.shape[1], thinker_width)
    returned = lax.all_to_all(results, "seq", split_axis=0, concat_axis=0, tiled=True)
    picked = returned.reshape(experts * slots, thinker_width)[slot_index].reshape(
        local_tokens, topk, thinker_width
    )
    expert_sum = jnp.sum(picked * gate_weights[:, :, None], 1)
    return (audio_embed.astype(jnp.float32) + expert_sum).astype(jnp.bfloat16)


def on_device(*arrays):
    devices = lax.axis_size("seq")
    experts, topk = devices * arrays[12].shape[0], arrays[2].shape[1]
    if experts <= 2 * topk and devices % 2 == 0:
        return dense_device(*arrays)
    return routed_device(*arrays)


def solution(mesh):
    placed = (
        P(("groups", "seq"), None),
        P("groups"),
        P(("groups", "seq"), None),
        P(("groups", "seq"), None),
        P("seq", None),
        P("seq", None),
        P(),
        P("seq", None),
        P("seq", None),
        P("seq", None),
        P(),
        P("seq", None, None),
        P("seq", None, None),
    )
    return jax.shard_map(
        on_device, mesh=mesh, in_specs=placed, out_specs=P(("groups", "seq"), None), check_vma=False
    )
```

profile of v0, /device:TPU:0, one launch (start us, length us, event | category | flops | bytes accessed | tf_op | source)
XLA Modules:
  0.0 276.8 jit_solution(7677985856568257122)
XLA Ops:
  6.5 1.2 fusion.66
  7.8 1.1 fusion.61
  8.9 1.1 fusion.34
  10.1 3.1 %collective-permute-start.8 = (f32[16,128]{1,0:T(8,128)S(1)}, f32[16,128]{1,0:T(8,128)S(1)}, u32[]{:S(2)}, u32[]{:S(2)}) collective-permute-start(f32[16,128]{1,0:T(8,128)S(1)} %select_reduce_fusion), channel_id=1, source_target_pairs={{0,4},{1,5},{2,6},{3,7},{4,8},{5,9},{6,10},{7,11},{8,12},{9,13},{1... | collective-permute-start | bytes 24584 | tf_op jit(solution)/shard_map/ppermute | solution.py:93
  13.2 3.7 %collective-permute-done.8 = f32[16,128]{1,0:T(8,128)S(1)} collective-permute-done((f32[16,128]{1,0:T(8,128)S(1)}, f32[16,128]{1,0:T(8,128)S(1)}, u32[]{:S(2)}, u32[]{:S(2)}) %collective-permute-start.8) | collective-permute-done | bytes 8224 | tf_op jit(solution)/shard_map/ppermute | solution.py:93
  16.8 5.6 %collective-permute-done.9 = f32[16,128]{1,0:T(8,128)S(1)} collective-permute-done((f32[16,128]{1,0:T(8,128)S(1)}, f32[16,128]{1,0:T(8,128)S(1)}, u32[]{:S(2)}, u32[]{:S(2)}) %collective-permute-start.9) | collective-permute-done | bytes 8224 | tf_op jit(solution)/shard_map/ppermute | solution.py:93
  22.4 1.7 collective-permute-start.1
  24.1 3.9 %collective-permute-start.4 = (bf16[144,256]{1,0:T(8,128)(2,1)}, bf16[144,256]{1,0:T(8,128)(2,1)}, u32[]{:S(2)}, u32[]{:S(2)}) collective-permute-start(bf16[144,256]{1,0:T(8,128)(2,1)} %param.17), channel_id=1, source_target_pairs={{0,12},{1,13},{2,14},{3,15},{4,0},{5,1},{6,2},{7,3},{8,4},{9,5},{1... | collective-permute-start | bytes 221192 | tf_op jit(solution)/shard_map/ppermute | solution.py:172
  29.1 1.3 collective-permute-start.11
  30.4 0.9 bitcast_dynamic-update-slice_fusion.1
  31.3 1.5 slice.107
  32.7 1.3 collective-permute-done.11
  34.0 1.9 collective-permute-start
  35.9 1.4 pad_maximum_fusion.9
  37.3 1.4 collective-permute-start.12
  38.8 1.7 pad_maximum_fusion.8
  40.4 1.5 collective-permute-start.5
  42.0 0.9 bitcast_dynamic-update-slice_fusion
  42.9 0.9 constant_dynamic-update-slice_fusion.2
  43.8 0.9 constant_dynamic-update-slice_fusion.1
  44.7 0.9 constant_dynamic-update-slice_fusion.refs_0_
  47.3 6.1 %collective-permute-done.5.refs_1_ = bf16[3,144,256]{2,1,0:T(8,128)(2,1)} collective-permute-done((bf16[3,144,256]{2,1,0:T(8,128)(2,1)}, bf16[3,144,256]{2,1,0:T(8,128)(2,1)}, u32[]{:S(2)}, u32[]{:S(2)}) %collective-permute-start.5) | collective-permute-done | bytes 221216 | tf_op jit(solution)/shard_map/ppermute | solution.py:172
  53.5 1.7 collective-permute-done.7.refs_3_
  55.2 1.7 copy-done.3
  56.9 4.9 %shard_map.127.act = bf16[128,2048]{1,0:T(8,128)(2,1)S(1)} custom-call(s32[4]{0:T(128)S(1)} %pad_add_fusion.place, bf16[256,4096]{1,0:T(8,128)(2,1)S(1)} %copy-done.3, bf16[1,4096]{1,0:T(2,128)(2,1)} %collective-permute-done.rim, bf16[5,144,256]{2,1,0:T(8,128)(2,1)S(1)} %constant_dynamic-update-slice_fusion.refs_0_, ...), custom_call_target="tpu_custom_call" | custom-call | flops 1207959552 | bytes 2359296 | tf_op jit(solution)/shard_map/pallas_call | solution.py:385
  62.6 55.5 %all-gather.3.cloned.1.call-done = bf16[2816,3328]{1,0:T(8,128)(2,1)} async-done(((bf16[176,3328]{1,0:T(8,128)(2,1)}), bf16[2816,3328]{1,0:T(8,128)(2,1)}) %all-gather.3.cloned.1.call-update) | async-done | bytes 18743312 | tf_op jit(solution)/shard_map/all_gather | solution.py:442
  118.1 1.0 copy-done.2
  119.1 3.9 %shard_map.128 = (bf16[128,1280]{1,0:T(8,128)(2,1)S(1)}, bf16[128,1280]{1,0:T(8,128)(2,1)S(1)}) custom-call(bf16[128,2048]{1,0:T(8,128)(2,1)S(1)} %copy-done.2, f32[1,1280]{1,0:T(1,128)S(1)} %broadcast_in_dim.26.gain, bf16[16,176,3328]{2,1,0:T(8,128)(2,1)} %bitcast.153), custom_call_target="tpu_custom_call" | custom-call | flops 4000000000 | bytes 5000000 | tf_op jit(solution)/shard_map/pallas_call | solution.py:458
  123.0 3.5 %shard_map.129 = (bf16[128,640]{1,0:T(8,128)(2,1)S(1)}, bf16[128,1280]{1,0:T(8,128)(2,1)S(1)}) custom-call(bf16[128,1280]{1,0:T(8,128)(2,1)S(1)} %get-tuple-element.10.normed, bf16[16,176,3328]{2,1,0:T(8,128)(2,1)} %bitcast.154), custom_call_target="tpu_custom_call" | custom-call | flops 4000000000 | bytes 5000000 | tf_op jit(solution)/shard_map/pallas_call | solution.py:472
  126.5 1.3 collective-permute-start.14
  127.8 3.2 %collective-permute-start.13 = (bf16[128,1280]{1,0:T(8,128)(2,1)S(1)}, bf16[128,1280]{1,0:T(8,128)(2,1)S(1)}, u32[]{:S(2)}, u32[]{:S(2)}) collective-permute-start(bf16[128,1280]{1,0:T(8,128)(2,1)S(1)} %get-tuple-element.12.own), channel_id=1, source_target_pairs={{0,1},{1,2},{2,3},{3,4},{4,5},{5,6},{6,7},{7,8},{8,9},{9,10},{10,1... | collective-permute-start | bytes 983048 | tf_op jit(solution)/shard_map/ppermute | solution.py:18
  131.0 3.0 %slice.143 = bf16[16,80,2048]{2,1,0:T(8,128)(2,1)S(1)} slice(bf16[16,176,3328]{2,1,0:T(8,128)(2,1)} %bitcast.155), slice={[0:16], [80:160], [1280:3328]} | slice | bytes 10485760 | tf_op jit(solution)/shard_map/slice | solution.py:443
  134.0 8.9 %convolution_convert_fusion.refs_0_ = bf16[1280,1536]{1,0:T(8,128)(2,1)S(1)} fusion(bf16[1280,2048]{1,0:T(8,128)(2,1)S(1)} %bitcast.157, bf16[1,2048,1536]{2,1,0:T(8,128)(2,1)S(1)} %bitcast.188, f32[2048]{0:T(1024)S(1)} %copy-done.7), kind=kOutput, calls=%fused_computation.1 | convolution fusion | flops 8064466944 | bytes 15474688 | tf_op jit(solution)/shard_map/dot_general | solution.py:490
  142.9 1.6 slice.142
  144.5 5.5 %shard_map.130 = (bf16[128,1280]{1,0:T(8,128)(2,1)}, bf16[128,1280]{1,0:T(8,128)(2,1)S(1)}) custom-call(s32[4]{0:T(128)S(1)} %bitcast.152, s32[1]{0:T(128)} %bitcast.2.first, bf16[128,640]{1,0:T(8,128)(2,1)S(1)} %get-tuple-element.11.query, bf16[128,1280]{1,0:T(8,128)(2,1)S(1)} %collective-permute-done.13.left, bf16[128,1280]{1,0:T(8,128)(2,1)S(1)} %get-tuple-element.12.own, ...), custom_call_target="tpu_custom_call" | custom-call | flops 4000000000 | bytes 4000000 | tf_op jit(solution)/shard_map/pallas_call | solution.py:492
  150.0 0.9 multiply_reduce_fusion
  151.1 1.6 collective-permute-start.19
  152.6 1.0 collective-permute-start.15
  153.7 9.2 %collective-permute-done.19 = bf16[128,1280]{1,0:T(8,128)(2,1)S(1)} collective-permute-done((bf16[128,1280]{1,0:T(8,128)(2,1)S(1)}, bf16[128,1280]{1,0:T(8,128)(2,1)S(1)}, u32[]{:S(2)}, u32[]{:S(2)}) %collective-permute-start.19) | collective-permute-done | bytes 327712 | tf_op jit(solution)/shard_map/ppermute | solution.py:93
  163.2 1.2 collective-permute-start.30
  164.8 10.0 %collective-permute-done.20 = bf16[128,1280]{1,0:T(8,128)(2,1)S(1)} collective-permute-done((bf16[128,1280]{1,0:T(8,128)(2,1)S(1)}, bf16[128,1280]{1,0:T(8,128)(2,1)S(1)}, u32[]{:S(2)}, u32[]{:S(2)}) %collective-permute-start.20) | collective-permute-done | bytes 327712 | tf_op jit(solution)/shard_map/ppermute | solution.py:93
  174.8 1.4 collective-permute-start.26
  176.6 7.4 %collective-permute-done.26 = bf16[128,1280]{1,0:T(8,128)(2,1)S(1)} collective-permute-done((bf16[128,1280]{1,0:T(8,128)(2,1)S(1)}, bf16[128,1280]{1,0:T(8,128)(2,1)S(1)}, u32[]{:S(2)}, u32[]{:S(2)}) %collective-permute-start.26) | collective-permute-done | bytes 327712 | tf_op jit(solution)/shard_map/ppermute | solution.py:93
  184.3 2.2 fusion.83
  186.5 2.0 fusion.11
  188.6 1.5 collective-permute-start.22
  190.5 8.2 %collective-permute-done.22 = bf16[128,1280]{1,0:T(8,128)(2,1)S(1)} collective-permute-done((bf16[128,1280]{1,0:T(8,128)(2,1)S(1)}, bf16[128,1280]{1,0:T(8,128)(2,1)S(1)}, u32[]{:S(2)}, u32[]{:S(2)}) %collective-permute-start.22) | collective-permute-done | bytes 327712 | tf_op jit(solution)/shard_map/ppermute | solution.py:93
  199.1 2.2 fusion.86
  201.3 2.0 fusion.20
  204.2 2.2 fusion.85
  206.4 2.0 fusion.17
  208.9 2.2 fusion.84
  211.1 2.3 fusion.14
  214.5 1.5 collective-permute-start.33
  217.1 12.3 %collective-permute-done.33 = bf16[128,2048]{1,0:T(8,128)(2,1)S(1)} collective-permute-done((bf16[128,2048]{1,0:T(8,128)(2,1)S(1)}, bf16[128,2048]{1,0:T(8,128)(2,1)S(1)}, u32[]{:S(2)}, u32[]{:S(2)}) %collective-permute-start.33) | collective-permute-done | bytes 524320 | tf_op jit(solution)/shard_map/ppermute | solution.py:93
  229.9 1.5 collective-permute-start.25
  231.5 9.1 %collective-permute-done.29 = bf16[128,2048]{1,0:T(8,128)(2,1)S(1)} collective-permute-done((bf16[128,2048]{1,0:T(8,128)(2,1)S(1)}, bf16[128,2048]{1,0:T(8,128)(2,1)S(1)}, u32[]{:S(2)}, u32[]{:S(2)}) %collective-permute-start.29) | collective-permute-done | bytes 524320 | tf_op jit(solution)/shard_map/ppermute | solution.py:93
  240.6 2.8 %collective-permute-done.34 = bf16[128,2048]{1,0:T(8,128)(2,1)S(1)} collective-permute-done((bf16[128,2048]{1,0:T(8,128)(2,1)S(1)}, bf16[128,2048]{1,0:T(8,128)(2,1)S(1)}, u32[]{:S(2)}, u32[]{:S(2)}) %collective-permute-start.34) | collective-permute-done | bytes 524320 | tf_op jit(solution)/shard_map/ppermute | solution.py:93
  244.1 1.5 collective-permute-start.18
  245.6 6.1 %collective-permute-done.25 = bf16[128,2048]{1,0:T(8,128)(2,1)S(1)} collective-permute-done((bf16[128,2048]{1,0:T(8,128)(2,1)S(1)}, bf16[128,2048]{1,0:T(8,128)(2,1)S(1)}, u32[]{:S(2)}, u32[]{:S(2)}) %collective-permute-start.25) | collective-permute-done | bytes 524320 | tf_op jit(solution)/shard_map/ppermute | solution.py:93
  251.8 4.8 %collective-permute-done.35 = bf16[128,2048]{1,0:T(8,128)(2,1)S(1)} collective-permute-done((bf16[128,2048]{1,0:T(8,128)(2,1)S(1)}, bf16[128,2048]{1,0:T(8,128)(2,1)S(1)}, u32[]{:S(2)}, u32[]{:S(2)}) %collective-permute-start.35) | collective-permute-done | bytes 524320 | tf_op jit(solution)/shard_map/ppermute | solution.py:93
  256.8 5.2 %collective-permute-done.18 = bf16[128,2048]{1,0:T(8,128)(2,1)S(1)} collective-permute-done((bf16[128,2048]{1,0:T(8,128)(2,1)S(1)}, bf16[128,2048]{1,0:T(8,128)(2,1)S(1)}, u32[]{:S(2)}, u32[]{:S(2)}) %collective-permute-start.18) | collective-permute-done | bytes 524320 | tf_op jit(solution)/shard_map/ppermute | solution.py:93
  262.1 6.8 %collective-permute-done.36 = bf16[128,2048]{1,0:T(8,128)(2,1)S(1)} collective-permute-done((bf16[128,2048]{1,0:T(8,128)(2,1)S(1)}, bf16[128,2048]{1,0:T(8,128)(2,1)S(1)}, u32[]{:S(2)}, u32[]{:S(2)}) %collective-permute-start.36) | collective-permute-done | bytes 524320 | tf_op jit(solution)/shard_map/ppermute | solution.py:93
  268.9 1.1 fusion.46
  (95 shorter events, 10.9 us)
Async XLA Ops:
  6.5 180.0 %copy-start = (bf16[1,768,2048]{2,1,0:T(8,128)(2,1)S(1)}, bf16[1,768,2048]{2,1,0:T(8,128)(2,1)}, u32[]{:S(2)}) copy-start(bf16[1,768,2048]{2,1,0:T(8,128)(2,1)} %param.25) | copy-start | bytes 9437188
  6.5 111.5 %all-gather.3.cloned.1.call-start = ((), (), s32[]{:S(2)}) async-start(), calls=%async_computation | async-start | bytes 19914752 | tf_op jit(solution)/shard_map/all_gather | solution.py:442
  7.7 2.3 copy-start.5
  7.8 2.3 copy-start.6
  8.9 37.6 %copy-start.4 = (f32[1280]{0:T(1024)S(1)}, f32[1280]{0:T(1024)}, u32[]{:S(2)}) copy-start(f32[1280]{0:T(1024)} %param.19) | copy-start | bytes 15364
  10.1 6.7 %collective-permute-start.8 = (f32[16,128]{1,0:T(8,128)S(1)}, f32[16,128]{1,0:T(8,128)S(1)}, u32[]{:S(2)}, u32[]{:S(2)}) collective-permute-start(f32[16,128]{1,0:T(8,128)S(1)} %select_reduce_fusion), channel_id=1, source_target_pairs={{0,4},{1,5},{2,6},{3,7},{4,8},{5,9},{6,10},{7,11},{8,12},{9,13},{1... | collective-permute-start | bytes 24584 | tf_op jit(solution)/shard_map/ppermute | solution.py:93
  16.8 5.6 %collective-permute-start.9 = (f32[16,128]{1,0:T(8,128)S(1)}, f32[16,128]{1,0:T(8,128)S(1)}, u32[]{:S(2)}, u32[]{:S(2)}) collective-permute-start(f32[16,128]{1,0:T(8,128)S(1)} %collective-permute-done.8), channel_id=1, source_target_pairs={{0,4},{1,5},{2,6},{3,7},{4,8},{5,9},{6,10},{7,11},{8,12},{9,13},{1... | collective-permute-start | bytes 24584 | tf_op jit(solution)/shard_map/ppermute | solution.py:93
  22.4 6.1 %collective-permute-start.10 = (f32[16,128]{1,0:T(8,128)S(1)}, f32[16,128]{1,0:T(8,128)S(1)}, u32[]{:S(2)}, u32[]{:S(2)}) collective-permute-start(f32[16,128]{1,0:T(8,128)S(1)} %collective-permute-done.9), channel_id=1, source_target_pairs={{0,4},{1,5},{2,6},{3,7},{4,8},{5,9},{6,10},{7,11},{8,12},{9,13},{1... | collective-permute-start | bytes 24584 | tf_op jit(solution)/shard_map/ppermute | solution.py:93
  22.4 15.0 %collective-permute-start.2 = (bf16[144,256]{1,0:T(8,128)(2,1)}, bf16[144,256]{1,0:T(8,128)(2,1)}, u32[]{:S(2)}, u32[]{:S(2)}) collective-permute-start(bf16[144,256]{1,0:T(8,128)(2,1)} %param.17), channel_id=1, source_target_pairs={{0,4},{1,5},{2,6},{3,7},{4,8},{5,9},{6,10},{7,11},{8,12},{9,13},{1... | collective-permute-start | bytes 221192 | tf_op jit(solution)/shard_map/ppermute | solution.py:172
  22.4 19.6 %collective-permute-start.1 = (bf16[144,256]{1,0:T(8,128)(2,1)}, bf16[144,256]{1,0:T(8,128)(2,1)}, u32[]{:S(2)}, u32[]{:S(2)}) collective-permute-start(bf16[144,256]{1,0:T(8,128)(2,1)} %param.17), channel_id=1, source_target_pairs={{0,2},{1,3},{2,0},{3,1},{4,6},{5,7},{6,4},{7,5},{8,10},{9,11},{10,... | collective-permute-start | bytes 221192 | tf_op jit(solution)/shard_map/ppermute | solution.py:172
  24.1 14.6 %collective-permute-start.4 = (bf16[144,256]{1,0:T(8,128)(2,1)}, bf16[144,256]{1,0:T(8,128)(2,1)}, u32[]{:S(2)}, u32[]{:S(2)}) collective-permute-start(bf16[144,256]{1,0:T(8,128)(2,1)} %param.17), channel_id=1, source_target_pairs={{0,12},{1,13},{2,14},{3,15},{4,0},{5,1},{6,2},{7,3},{8,4},{9,5},{1... | collective-permute-start | bytes 221192 | tf_op jit(solution)/shard_map/ppermute | solution.py:172
  28.0 10.8 %collective-permute-start.3 = (bf16[144,256]{1,0:T(8,128)(2,1)}, bf16[144,256]{1,0:T(8,128)(2,1)}, u32[]{:S(2)}, u32[]{:S(2)}) collective-permute-start(bf16[144,256]{1,0:T(8,128)(2,1)} %param.17), channel_id=1, source_target_pairs={{0,8},{1,9},{2,10},{3,11},{4,12},{5,13},{6,14},{7,15},{8,0},{9,1},... | collective-permute-start | bytes 221192 | tf_op jit(solution)/shard_map/ppermute | solution.py:172
  29.1 4.9 %collective-permute-start.11 = (f32[4,16,128]{2,1,0:T(8,128)}, f32[4,16,128]{2,1,0:T(8,128)}, u32[]{:S(2)}, u32[]{:S(2)}) collective-permute-start(f32[4,16,128]{2,1,0:T(8,128)} %get-tuple-element.34), channel_id=1, source_target_pairs={{0,2},{1,3},{2,0},{3,1},{4,6},{5,7},{6,4},{7,5},{8,10},{9,11},{10,... | collective-permute-start | bytes 98312 | tf_op jit(solution)/shard_map/ppermute | solution.py:93
  34.0 19.4 %collective-permute-start = (bf16[1,4096]{1,0:T(2,128)(2,1)}, bf16[1,4096]{1,0:T(2,128)(2,1)}, u32[]{:S(2)}, u32[]{:S(2)}) collective-permute-start(bf16[1,4096]{1,0:T(2,128)(2,1)} %slice.107), channel_id=1, source_target_pairs={{0,1},{1,2},{2,3},{3,4},{4,5},{5,6},{6,7},{7,8},{8,9},{9,10},{10,1... | collective-permute-start | bytes 24584 | tf_op jit(solution)/shard_map/ppermute | solution.py:18
  37.3 9.1 %collective-permute-start.12 = (f32[2,4,16,128]{3,2,1,0:T(8,128)}, f32[2,4,16,128]{3,2,1,0:T(8,128)}, u32[]{:S(2)}, u32[]{:S(2)}) collective-permute-start(f32[2,4,16,128]{3,2,1,0:T(8,128)} %get-tuple-element.31), channel_id=1, source_target_pairs={{0,1},{1,0},{2,3},{3,2},{4,5},{5,4},{6,7},{7,6},{8,9},{9,8},{10,11... | collective-permute-start | bytes 196616 | tf_op jit(solution)/shard_map/ppermute | solution.py:93
  40.4 13.0 %collective-permute-start.5 = (bf16[3,144,256]{2,1,0:T(8,128)(2,1)}, bf16[3,144,256]{2,1,0:T(8,128)(2,1)}, u32[]{:S(2)}, u32[]{:S(2)}) collective-permute-start(bf16[3,144,256]{2,1,0:T(8,128)(2,1)} %pad_maximum_fusion.8), channel_id=1, source_target_pairs={{0,2},{1,3},{2,0},{3,1},{4,6},{5,7},{6,4},{7,5},{8,10},{9,11},{10,... | collective-permute-start | bytes 663560 | tf_op jit(solution)/shard_map/ppermute | solution.py:172
  45.6 7.9 %collective-permute-start.6 = (bf16[5,144,256]{2,1,0:T(8,128)(2,1)S(1)}, bf16[5,144,256]{2,1,0:T(8,128)(2,1)}, u32[]{:S(2)}, u32[]{:S(2)}) collective-permute-start(bf16[5,144,256]{2,1,0:T(8,128)(2,1)S(1)} %constant_dynamic-update-slice_fusion.refs_0_), channel_id=1, source_target_pairs={{0,1},{1,0},{2,3},{3,2},{4,5},{5,4},{6,7},{7,6},{8,9},{9,8},{10,11... | collective-permute-start | bytes 1105928 | tf_op jit(solution)/shard_map/ppermute | solution.py:172
  53.4 1.8 collective-permute-start.7
  55.2 1.7 copy-start.3
  61.8 0.8 copy-start.1
  118.1 1.0 copy-start.2
  119.1 14.9 %slice-start = ((s8[6291456]{0:T(1024)(128)(4,1)}), s8[2097152]{0:T(1024)(128)(4,1)S(1)}, s32[]{:S(2)}) async-start(s8[6291456]{0:T(1024)(128)(4,1)} %bitcast.187), calls=%async_computation.1 | async-start | bytes 4194304
  123.0 11.0 %slice-start.1 = ((s8[6291456]{0:T(1024)(128)(4,1)}), s8[4194304]{0:T(1024)(128)(4,1)S(1)}, s32[]{:S(2)}) async-start(s8[6291456]{0:T(1024)(128)(4,1)} %bitcast.187), calls=%async_computation.2 | async-start | bytes 8388608
  126.5 7.5 %copy-start.7 = (f32[2048]{0:T(1024)S(1)}, f32[2048]{0:T(1024)}, u32[]{:S(2)}) copy-start(f32[2048]{0:T(1024)} %param.23) | copy-start | bytes 24580
  126.5 18.0 %collective-permute-start.14 = (bf16[128,1280]{1,0:T(8,128)(2,1)S(1)}, bf16[128,1280]{1,0:T(8,128)(2,1)S(1)}, u32[]{:S(2)}, u32[]{:S(2)}) collective-permute-start(bf16[128,1280]{1,0:T(8,128)(2,1)S(1)} %get-tuple-element.12.own), channel_id=1, source_target_pairs={{1,0},{2,1},{3,2},{4,3},{5,4},{6,5},{7,6},{8,7},{9,8},{10,9},{11,1... | collective-permute-start | bytes 983048 | tf_op jit(solution)/shard_map/ppermute | solution.py:18
  127.8 16.7 %collective-permute-start.13 = (bf16[128,1280]{1,0:T(8,128)(2,1)S(1)}, bf16[128,1280]{1,0:T(8,128)(2,1)S(1)}, u32[]{:S(2)}, u32[]{:S(2)}) collective-permute-start(bf16[128,1280]{1,0:T(8,128)(2,1)S(1)} %get-tuple-element.12.own), channel_id=1, source_target_pairs={{0,1},{1,2},{2,3},{3,4},{4,5},{5,6},{6,7},{7,8},{8,9},{9,10},{10,1... | collective-permute-start | bytes 983048 | tf_op jit(solution)/shard_map/ppermute | solution.py:18
  151.1 11.8 %collective-permute-start.19 = (bf16[128,1280]{1,0:T(8,128)(2,1)S(1)}, bf16[128,1280]{1,0:T(8,128)(2,1)S(1)}, u32[]{:S(2)}, u32[]{:S(2)}) collective-permute-start(bf16[128,1280]{1,0:T(8,128)(2,1)S(1)} %multiply_convert_fusion.1), channel_id=1, source_target_pairs={{0,4},{1,5},{2,6},{3,7},{4,8},{5,9},{6,10},{7,11},{8,12},{9,13},{1... | collective-permute-start | bytes 983048 | tf_op jit(solution)/shard_map/ppermute | solution.py:93
  152.6 11.7 %collective-permute-start.15 = (bf16[128,1280]{1,0:T(8,128)(2,1)S(1)}, bf16[128,1280]{1,0:T(8,128)(2,1)S(1)}, u32[]{:S(2)}, u32[]{:S(2)}) collective-permute-start(bf16[128,1280]{1,0:T(8,128)(2,1)S(1)} %multiply_convert_fusion.1), channel_id=1, source_target_pairs={{0,2},{1,3},{2,0},{3,1},{4,6},{5,7},{6,4},{7,5},{8,10},{9,11},{10,... | collective-permute-start | bytes 983048 | tf_op jit(solution)/shard_map/ppermute | solution.py:93
  162.9 11.9 %collective-permute-start.20 = (bf16[128,1280]{1,0:T(8,128)(2,1)S(1)}, bf16[128,1280]{1,0:T(8,128)(2,1)S(1)}, u32[]{:S(2)}, u32[]{:S(2)}) collective-permute-start(bf16[128,1280]{1,0:T(8,128)(2,1)S(1)} %collective-permute-done.19), channel_id=1, source_target_pairs={{0,4},{1,5},{2,6},{3,7},{4,8},{5,9},{6,10},{7,11},{8,12},{9,13},{1... | collective-permute-start | bytes 983048 | tf_op jit(solution)/shard_map/ppermute | solution.py:93
  163.2 13.0 %collective-permute-start.30 = (bf16[128,1280]{1,0:T(8,128)(2,1)S(1)}, bf16[128,1280]{1,0:T(8,128)(2,1)S(1)}, u32[]{:S(2)}, u32[]{:S(2)}) collective-permute-start(bf16[128,1280]{1,0:T(8,128)(2,1)S(1)} %collective-permute-done.19), channel_id=1, source_target_pairs={{0,2},{1,3},{2,0},{3,1},{4,6},{5,7},{6,4},{7,5},{8,10},{9,11},{10,... | collective-permute-start | bytes 983048 | tf_op jit(solution)/shard_map/ppermute | solution.py:93
  164.5 19.7 %collective-permute-start.16 = (bf16[2,128,1280]{2,1,0:T(8,128)(2,1)S(1)}, bf16[2,128,1280]{2,1,0:T(8,128)(2,1)S(1)}, u32[]{:S(2)}, u32[]{:S(2)}) collective-permute-start(bf16[2,128,1280]{2,1,0:T(8,128)(2,1)S(1)} %get-tuple-element.30), channel_id=1, source_target_pairs={{0,1},{1,0},{2,3},{3,2},{4,5},{5,4},{6,7},{7,6},{8,9},{9,8},{10,11... | collective-permute-start | bytes 1966088 | tf_op jit(solution)/shard_map/ppermute | solution.py:93
  174.8 9.3 %collective-permute-start.26 = (bf16[128,1280]{1,0:T(8,128)(2,1)S(1)}, bf16[128,1280]{1,0:T(8,128)(2,1)S(1)}, u32[]{:S(2)}, u32[]{:S(2)}) collective-permute-start(bf16[128,1280]{1,0:T(8,128)(2,1)S(1)} %collective-permute-done.20), channel_id=1, source_target_pairs={{0,2},{1,3},{2,0},{3,1},{4,6},{5,7},{6,4},{7,5},{8,10},{9,11},{10,... | collective-permute-start | bytes 983048 | tf_op jit(solution)/shard_map/ppermute | solution.py:93
  176.2 22.7 %collective-permute-start.31 = (bf16[2,128,1280]{2,1,0:T(8,128)(2,1)S(1)}, bf16[2,128,1280]{2,1,0:T(8,128)(2,1)S(1)}, u32[]{:S(2)}, u32[]{:S(2)}) collective-permute-start(bf16[2,128,1280]{2,1,0:T(8,128)(2,1)S(1)} %get-tuple-element.24), channel_id=1, source_target_pairs={{0,1},{1,0},{2,3},{3,2},{4,5},{5,4},{6,7},{7,6},{8,9},{9,8},{10,11... | collective-permute-start | bytes 1966088 | tf_op jit(solution)/shard_map/ppermute | solution.py:93
  176.3 12.3 %collective-permute-start.21 = (bf16[128,1280]{1,0:T(8,128)(2,1)S(1)}, bf16[128,1280]{1,0:T(8,128)(2,1)S(1)}, u32[]{:S(2)}, u32[]{:S(2)}) collective-permute-start(bf16[128,1280]{1,0:T(8,128)(2,1)S(1)} %collective-permute-done.20), channel_id=1, source_target_pairs={{0,4},{1,5},{2,6},{3,7},{4,8},{5,9},{6,10},{7,11},{8,12},{9,13},{1... | collective-permute-start | bytes 983048 | tf_op jit(solution)/shard_map/ppermute | solution.py:93
  184.1 20.0 %collective-permute-start.27 = (bf16[2,128,1280]{2,1,0:T(8,128)(2,1)S(1)}, bf16[2,128,1280]{2,1,0:T(8,128)(2,1)S(1)}, u32[]{:S(2)}, u32[]{:S(2)}) collective-permute-start(bf16[2,128,1280]{2,1,0:T(8,128)(2,1)S(1)} %get-tuple-element.26), channel_id=1, source_target_pairs={{0,1},{1,0},{2,3},{3,2},{4,5},{5,4},{6,7},{7,6},{8,9},{9,8},{10,11... | collective-permute-start | bytes 1966088 | tf_op jit(solution)/shard_map/ppermute | solution.py:93
  188.6 10.2 %collective-permute-start.22 = (bf16[128,1280]{1,0:T(8,128)(2,1)S(1)}, bf16[128,1280]{1,0:T(8,128)(2,1)S(1)}, u32[]{:S(2)}, u32[]{:S(2)}) collective-permute-start(bf16[128,1280]{1,0:T(8,128)(2,1)S(1)} %collective-permute-done.21), channel_id=1, source_target_pairs={{0,2},{1,3},{2,0},{3,1},{4,6},{5,7},{6,4},{7,5},{8,10},{9,11},{10,... | collective-permute-start | bytes 983048 | tf_op jit(solution)/shard_map/ppermute | solution.py:93
  190.3 53.4 %collective-permute-start.17 = (bf16[2,128,2048]{2,1,0:T(8,128)(2,1)S(1)}, bf16[2,128,2048]{2,1,0:T(8,128)(2,1)S(1)}, u32[]{:S(2)}, u32[]{:S(2)}) collective-permute-start(bf16[2,128,2048]{2,1,0:T(8,128)(2,1)S(1)} %bitcast.167), channel_id=1, source_target_pairs={{0,1},{1,0},{2,3},{3,2},{4,5},{5,4},{6,7},{7,6},{8,9},{9,8},{10,11... | collective-permute-start | bytes 3145736 | tf_op jit(solution)/shard_map/ppermute | solution.py:93
  198.9 9.9 %collective-permute-start.23 = (bf16[2,128,1280]{2,1,0:T(8,128)(2,1)S(1)}, bf16[2,128,1280]{2,1,0:T(8,128)(2,1)S(1)}, u32[]{:S(2)}, u32[]{:S(2)}) collective-permute-start(bf16[2,128,1280]{2,1,0:T(8,128)(2,1)S(1)} %get-tuple-element.28), channel_id=1, source_target_pairs={{0,1},{1,0},{2,3},{3,2},{4,5},{5,4},{6,7},{7,6},{8,9},{9,8},{10,11... | collective-permute-start | bytes 1966088 | tf_op jit(solution)/shard_map/ppermute | solution.py:93
  203.5 10.5 %collective-permute-start.32 = (bf16[2,128,2048]{2,1,0:T(8,128)(2,1)S(1)}, bf16[2,128,2048]{2,1,0:T(8,128)(2,1)S(1)}, u32[]{:S(2)}, u32[]{:S(2)}) collective-permute-start(bf16[2,128,2048]{2,1,0:T(8,128)(2,1)S(1)} %bitcast.168), channel_id=1, source_target_pairs={{0,1},{1,0},{2,3},{3,2},{4,5},{5,4},{6,7},{7,6},{8,9},{9,8},{10,11... | collective-permute-start | bytes 3145736 | tf_op jit(solution)/shard_map/ppermute | solution.py:93
  208.6 7.4 %collective-permute-start.28 = (bf16[2,128,2048]{2,1,0:T(8,128)(2,1)S(1)}, bf16[2,128,2048]{2,1,0:T(8,128)(2,1)S(1)}, u32[]{:S(2)}, u32[]{:S(2)}) collective-permute-start(bf16[2,128,2048]{2,1,0:T(8,128)(2,1)S(1)} %bitcast.170), channel_id=1, source_target_pairs={{0,1},{1,0},{2,3},{3,2},{4,5},{5,4},{6,7},{7,6},{8,9},{9,8},{10,11... | collective-permute-start | bytes 3145736 | tf_op jit(solution)/shard_map/ppermute | solution.py:93
  213.5 16.0 %collective-permute-start.24 = (bf16[2,128,2048]{2,1,0:T(8,128)(2,1)S(1)}, bf16[2,128,2048]{2,1,0:T(8,128)(2,1)S(1)}, u32[]{:S(2)}, u32[]{:S(2)}) collective-permute-start(bf16[2,128,2048]{2,1,0:T(8,128)(2,1)S(1)} %bitcast.169), channel_id=1, source_target_pairs={{0,1},{1,0},{2,3},{3,2},{4,5},{5,4},{6,7},{7,6},{8,9},{9,8},{10,11... | collective-permute-start | bytes 3145736 | tf_op jit(solution)/shard_map/ppermute | solution.py:93
  214.5 14.9 %collective-permute-start.33 = (bf16[128,2048]{1,0:T(8,128)(2,1)S(1)}, bf16[128,2048]{1,0:T(8,128)(2,1)S(1)}, u32[]{:S(2)}, u32[]{:S(2)}) collective-permute-start(bf16[128,2048]{1,0:T(8,128)(2,1)S(1)} %fusion.65), channel_id=1, source_target_pairs={{0,2},{1,3},{2,0},{3,1},{4,6},{5,7},{6,4},{7,5},{8,10},{9,11},{10,... | collective-permute-start | bytes 1572872 | tf_op jit(solution)/shard_map/ppermute | solution.py:93
  216.4 24.1 %collective-permute-start.29 = (bf16[128,2048]{1,0:T(8,128)(2,1)S(1)}, bf16[128,2048]{1,0:T(8,128)(2,1)S(1)}, u32[]{:S(2)}, u32[]{:S(2)}) collective-permute-start(bf16[128,2048]{1,0:T(8,128)(2,1)S(1)} %fusion.64), channel_id=1, source_target_pairs={{0,2},{1,3},{2,0},{3,1},{4,6},{5,7},{6,4},{7,5},{8,10},{9,11},{10,... | collective-permute-start | bytes 1572872 | tf_op jit(solution)/shard_map/ppermute | solution.py:93
  229.4 13.9 %collective-permute-start.34 = (bf16[128,2048]{1,0:T(8,128)(2,1)S(1)}, bf16[128,2048]{1,0:T(8,128)(2,1)S(1)}, u32[]{:S(2)}, u32[]{:S(2)}) collective-permute-start(bf16[128,2048]{1,0:T(8,128)(2,1)S(1)} %fusion.36), channel_id=1, source_target_pairs={{0,4},{1,5},{2,6},{3,7},{4,8},{5,9},{6,10},{7,11},{8,12},{9,13},{1... | collective-permute-start | bytes 1572872 | tf_op jit(solution)/shard_map/ppermute | solution.py:93
  229.9 21.8 %collective-permute-start.25 = (bf16[128,2048]{1,0:T(8,128)(2,1)S(1)}, bf16[128,2048]{1,0:T(8,128)(2,1)S(1)}, u32[]{:S(2)}, u32[]{:S(2)}) collective-permute-start(bf16[128,2048]{1,0:T(8,128)(2,1)S(1)} %fusion.63), channel_id=1, source_target_pairs={{0,2},{1,3},{2,0},{3,1},{4,6},{5,7},{6,4},{7,5},{8,10},{9,11},{10,... | collective-permute-start | bytes 1572872 | tf_op jit(solution)/shard_map/ppermute | solution.py:93
  243.6 13.0 %collective-permute-start.35 = (bf16[128,2048]{1,0:T(8,128)(2,1)S(1)}, bf16[128,2048]{1,0:T(8,128)(2,1)S(1)}, u32[]{:S(2)}, u32[]{:S(2)}) collective-permute-start(bf16[128,2048]{1,0:T(8,128)(2,1)S(1)} %fusion.39), channel_id=1, source_target_pairs={{0,4},{1,5},{2,6},{3,7},{4,8},{5,9},{6,10},{7,11},{8,12},{9,13},{1... | collective-permute-start | bytes 1572872 | tf_op jit(solution)/shard_map/ppermute | solution.py:93
  244.1 18.0 %collective-permute-start.18 = (bf16[128,2048]{1,0:T(8,128)(2,1)S(1)}, bf16[128,2048]{1,0:T(8,128)(2,1)S(1)}, u32[]{:S(2)}, u32[]{:S(2)}) collective-permute-start(bf16[128,2048]{1,0:T(8,128)(2,1)S(1)} %fusion.62), channel_id=1, source_target_pairs={{0,2},{1,3},{2,0},{3,1},{4,6},{5,7},{6,4},{7,5},{8,10},{9,11},{10,... | collective-permute-start | bytes 1572872 | tf_op jit(solution)/shard_map/ppermute | solution.py:93
  256.8 12.1 %collective-permute-start.36 = (bf16[128,2048]{1,0:T(8,128)(2,1)S(1)}, bf16[128,2048]{1,0:T(8,128)(2,1)S(1)}, u32[]{:S(2)}, u32[]{:S(2)}) collective-permute-start(bf16[128,2048]{1,0:T(8,128)(2,1)S(1)} %fusion.42), channel_id=1, source_target_pairs={{0,4},{1,5},{2,6},{3,7},{4,8},{5,9},{6,10},{7,11},{8,12},{9,13},{1... | collective-permute-start | bytes 1572872 | tf_op jit(solution)/shard_map/ppermute | solution.py:93
Sparse Core Ops, SparseCore 0:
  10.2 107.8 all-gather.2
where the time goes:
time: 278 us; the launch traced here: 277 us
  waiting for transfers between devices  156 us (56%)
  starting transfers between devices  34.3 us (12%)
  matrix products  27 us (10%)
  Pallas kernels  17.8 us (6%)
  local copies, waits for them, and re-layouts  14.9 us (5%)
  between operations  13.9 us (5%)
  other arithmetic  12.9 us (5%)
    ppermute x27, waiting for transfers between devices, ring_step(): return lax.ppermute(block, 'seq', route)  92.5 us
    all_gather x1, waiting for transfers between devices, dense_device(): late_full = lax.all_gather(packed, 'seq', axis=0)  55.5 us
    ppermute x27, starting transfers between devices, ring_step(): return lax.ppermute(block, 'seq', route)  20.3 us
    dot_general x1, matrix products, dense_device(): fused = jnp.dot(audio_full, weighted, preferred_element_type=jnp.float32)  8.86 us
    dot_general x4, matrix products, dense_experts(): both = jnp.dot(rows, fused, preferred_element_type=jnp.float32)  8.77 us
    dot_general x4, matrix products, dense_experts(): jnp.dot(hidden, down, preferred_element_type=jnp.float32)  8.43 us
    ppermute x7, waiting for transfers between devices, hop(): return lax.ppermute(block, 'seq', route)  7.87 us
    ppermute x7, starting transfers between devices, hop(): return lax.ppermute(block, 'seq', route)  7.68 us
  transfers between devices with their start and end apart: 38, of which 17 were waited for; matrix products, arithmetic and copies ran while one was open for 17% of the time, Pallas kernels for 2%

commit v1 on v0

--- a/solution.py
+++ b/solution.py
@@ -121,6 +121,11 @@
     return [mine[:, :, k].reshape(-1) for k in range(zs)]
 
 
+def once(block, other):
+    zero = 0.0 * other[(0,) * other.ndim].astype(jnp.float32)
+    return (block.astype(jnp.float32) + zero).astype(block.dtype)
+
+
 def dense_experts(audio_embed, scaled, gates, fused, down):
     devices = lax.axis_size("seq")
     zs, ys, cores = levels(devices)
@@ -128,27 +133,29 @@
     inner = down.shape[0]
     width = down.shape[1]
     blocks = [scaled]
-    for _ in range(zs - 1):
-        blocks.append(ring_step(blocks[-1], ys * cores, zs))
-    chunks = []
-    for block in blocks:
+    for k in range(1, zs):
+        sent = once(blocks[-1], fused) if k == 2 else blocks[-1]
+        blocks.append(ring_step(sent, ys * cores, zs))
+    totals, columns, carry = {}, {}, None
+
+    def send(k):
+        block = blocks[k]
         line = [block]
         for _ in range(ys - 1):
             line.append(ring_step(line[-1], cores, ys))
         pair = jnp.stack(line)
-        chunks.append(jnp.stack([pair, ring_step(pair, 1, cores)]))
-    carry = None
-    crossed = []
-    columns = {}
-    for k in list(range(1, zs)) + [0]:
-        rows = chunks[k].reshape(-1, scaled.shape[1])
+        return jnp.stack([pair, ring_step(pair, 1, cores)])
+
+    theirs = None
+    for k in [*range(1, zs), 0]:
+        rows = send(k).reshape(-1, scaled.shape[1])
         weight = gates[k][:, None]
         both = jnp.dot(rows, fused, preferred_element_type=jnp.float32)
         hidden = (jax.nn.silu(both[:, :inner]) * both[:, inner:] * weight).astype(jnp.bfloat16)
         sums = jnp.dot(hidden, down, preferred_element_type=jnp.float32).astype(jnp.bfloat16)
+        totals[k] = sums
         sums = sums.reshape(cores, ys, tokens, width)
         theirs = ring_step(sums[1], 1, cores)
-        crossed.append(theirs)
         chip = sums[0].astype(jnp.float32) + theirs.astype(jnp.float32)
         column = chip[1 % ys]
         for dy in range(1, ys):
@@ -428,20 +435,21 @@
     rim = shifted(spectral[-1:], "seq", 1)
     rows, wide, dim = attn_in.shape[0], attn_in.shape[1], conv_proj.shape[1]
     high, thin, broad = conv_proj.shape[0], attn_out.shape[0], audio_proj.shape[1]
-    deep = -(-max(high + thin, 2 * rows) // 16) * 16
+    lanes = broad - wide
+    head = 2 * rows - high
+    spare = attn_out[head:].reshape(thin - head, -1, lanes).swapaxes(0, 1).reshape(rows, lanes)
     packed = jnp.concatenate(
         [
-            jnp.pad(jnp.concatenate([conv_proj, attn_out]), ((0, deep - high - thin), (0, 0))),
-            jnp.pad(
-                jnp.concatenate([jnp.pad(attn_in, ((0, 0), (0, broad - wide))), audio_proj]),
-                ((0, deep - 2 * rows), (0, 0)),
-            ),
+            jnp.concatenate([conv_proj, attn_out[:head]]),
+            jnp.concatenate([jnp.concatenate([attn_in, spare], 1), audio_proj]),
         ],
         1,
     )
     late_full = lax.all_gather(packed, "seq", axis=0)
     audio_full = late_full[:, rows : 2 * rows, dim:].reshape(-1, broad)
-    out_full = late_full[:, high : high + thin, :dim].reshape(-1, dim)
+    spare = late_full[:, :rows, dim + wide :].reshape(devices, -1, thin - head, lanes)
+    spare = spare.swapaxes(1, 2).reshape(devices, thin - head, dim)
+    out_full = jnp.concatenate([late_full[:, high : high + head, :dim], spare], 1).reshape(-1, dim)
     conv_pieces = spread(conv_weight)
     gates = spread_gates(gate_table(expert_ids, gate_weights, experts))
     conv_act = with_pieces(
@@ -492,14 +500,14 @@
     encoded, post = pl.pallas_call(
         functools.partial(attend_kernel, devices * tokens),
         out_shape=(rows_of(tokens, dim), rows_of(tokens, dim)),
-        in_specs=[SMEM, SMEM] + [VMEM] * 6 + [ANY],
+        in_specs=[SMEM, SMEM] + [VMEM] * 6,
         out_specs=(VMEM, VMEM),
         scratch_shapes=[pltpu.VMEM((tokens, width), jnp.bfloat16)],
         compiler_params=room(8),
         cost_estimate=pl.CostEstimate(
             flops=4 * 10**9, bytes_accessed=4 * 10**6, transcendentals=0
         ),
-    )(ends, (me * tokens)[None].astype(jnp.int32), query, left, key_rows, right, embed, out_full, fused)
+    )(ends, (me * tokens)[None].astype(jnp.int32), query, left, key_rows, right, embed, out_full)
     audio_sum = jnp.dot(post, audio_full, preferred_element_type=jnp.float32)
     audio_embed = audio_sum.astype(jnp.bfloat16)
     power = jnp.mean(jnp.square(audio_embed.astype(jnp.float32)), -1, keepdims=True)

time: 278 us -> 265 us (0.953)
  waiting for transfers between devices: 156 us -> 140 us
  local copies, waits for them, and re-layouts: 14.9 us -> 18.1 us
    all_gather x1, waiting for transfers between devices: 55.5 us -> 43.8 us  [dense_device(): late_full = lax.all_gather(packed, 'seq', axis=0)]
    ppermute x27, waiting for transfers between devices: 92.5 us -> 84.5 us  [ring_step(): return lax.ppermute(block, 'seq', route)]
    ppermute x7, waiting for transfers between devices: 7.87 us -> 11.6 us  [hop(): return lax.ppermute(block, 'seq', route)]
  transfers between devices with their start and end apart: 38 -> 38, of which waited for: 17 -> 20; matrix products, arithmetic and copies ran while one was open for 17% -> 18% of each run, Pallas kernels for 2% -> 2%
where the time goes in v1:
time: 265 us; the launch traced here: 264 us
  waiting for transfers between devices  140 us (53%)
  starting transfers between devices  34.9 us (13%)
  matrix products  26.9 us (10%)
  local copies, waits for them, and re-layouts  18.1 us (7%)
  Pallas kernels  17.5 us (7%)
  between operations  14.5 us (5%)
  other arithmetic  12 us (5%)
    ppermute x27, waiting for transfers between devices, ring_step(): return lax.ppermute(block, 'seq', route)  84.5 us
    all_gather x1, waiting for transfers between devices, dense_device(): late_full = lax.all_gather(packed, 'seq', axis=0)  43.8 us
    ppermute x27, starting transfers between devices, ring_step(): return lax.ppermute(block, 'seq', route)  21.9 us
    ppermute x7, waiting for transfers between devices, hop(): return lax.ppermute(block, 'seq', route)  11.6 us
    dot_general x1, matrix products, dense_device(): fused = jnp.dot(audio_full, weighted, preferred_element_type=jnp.float32)  8.87 us
    dot_general x4, matrix products, dense_experts(): both = jnp.dot(rows, fused, preferred_element_type=jnp.float32)  8.77 us
    dot_general x4, matrix products, dense_experts(): jnp.dot(hidden, down, preferred_element_type=jnp.float32)  8.3 us
    ppermute x7, starting transfers between devices, hop(): return lax.ppermute(block, 'seq', route)  7.67 us
  transfers between devices with their start and end apart: 38, of which 20 were waited for; matrix products, arithmetic and copies ran while one was open for 18% of the time, Pallas kernels for 2%

profile of v1, /device:TPU:0, one launch (start us, length us, event | category | flops | bytes accessed | tf_op | source)
XLA Modules:
  0.0 263.9 jit_solution(10019713371153201003)
XLA Ops:
  6.5 1.0 slice.124
  8.3 2.3 maximum_maximum_fusion
  10.7 3.1 %collective-permute-start.8 = (f32[16,128]{1,0:T(8,128)S(1)}, f32[16,128]{1,0:T(8,128)S(1)}, u32[]{:S(2)}, u32[]{:S(2)}) collective-permute-start(f32[16,128]{1,0:T(8,128)S(1)} %select_reduce_fusion), channel_id=1, source_target_pairs={{0,4},{1,5},{2,6},{3,7},{4,8},{5,9},{6,10},{7,11},{8,12},{9,13},{1... | collective-permute-start | bytes 24584 | tf_op jit(solution)/shard_map/ppermute | solution.py:93
  13.7 3.7 %collective-permute-done.8 = f32[16,128]{1,0:T(8,128)S(1)} collective-permute-done((f32[16,128]{1,0:T(8,128)S(1)}, f32[16,128]{1,0:T(8,128)S(1)}, u32[]{:S(2)}, u32[]{:S(2)}) %collective-permute-start.8) | collective-permute-done | bytes 8224 | tf_op jit(solution)/shard_map/ppermute | solution.py:93
  17.4 5.6 %collective-permute-done.9 = f32[16,128]{1,0:T(8,128)S(1)} collective-permute-done((f32[16,128]{1,0:T(8,128)S(1)}, f32[16,128]{1,0:T(8,128)S(1)}, u32[]{:S(2)}, u32[]{:S(2)}) %collective-permute-start.9) | collective-permute-done | bytes 8224 | tf_op jit(solution)/shard_map/ppermute | solution.py:93
  23.0 1.7 collective-permute-start.1
  24.7 4.4 %collective-permute-start.3 = (bf16[144,256]{1,0:T(8,128)(2,1)}, bf16[144,256]{1,0:T(8,128)(2,1)}, u32[]{:S(2)}, u32[]{:S(2)}) collective-permute-start(bf16[144,256]{1,0:T(8,128)(2,1)} %param.17), channel_id=1, source_target_pairs={{0,8},{1,9},{2,10},{3,11},{4,12},{5,13},{6,14},{7,15},{8,0},{9,1},... | collective-permute-start | bytes 221192 | tf_op jit(solution)/shard_map/ppermute | solution.py:179
  29.7 1.3 collective-permute-start.11
  31.0 0.9 bitcast_dynamic-update-slice_fusion.1
  31.9 1.5 slice.119
  33.3 1.3 collective-permute-done.11
  34.6 1.9 collective-permute-start
  36.5 1.4 pad_maximum_fusion.10
  37.9 1.4 collective-permute-start.12
  39.3 0.9 bitcast_dynamic-update-slice_fusion
  40.2 0.9 constant_dynamic-update-slice_fusion.2
  41.1 0.9 constant_dynamic-update-slice_fusion.1
  42.0 0.9 constant_dynamic-update-slice_fusion.refs_0_
  42.9 1.7 pad_maximum_fusion.9
  44.6 1.5 collective-permute-start.5
  47.9 9.9 %collective-permute-done.5.refs_1_ = bf16[3,144,256]{2,1,0:T(8,128)(2,1)} collective-permute-done((bf16[3,144,256]{2,1,0:T(8,128)(2,1)}, bf16[3,144,256]{2,1,0:T(8,128)(2,1)}, u32[]{:S(2)}, u32[]{:S(2)}) %collective-permute-start.5) | collective-permute-done | bytes 221216 | tf_op jit(solution)/shard_map/ppermute | solution.py:179
  57.8 1.7 collective-permute-done.7.refs_3_
  59.5 1.6 copy-done.3
  61.1 4.9 %shard_map.127.act = bf16[128,2048]{1,0:T(8,128)(2,1)S(1)} custom-call(s32[4]{0:T(128)S(1)} %pad_add_fusion.place, bf16[256,4096]{1,0:T(8,128)(2,1)S(1)} %copy-done.3, bf16[1,4096]{1,0:T(2,128)(2,1)} %collective-permute-done.rim, bf16[5,144,256]{2,1,0:T(8,128)(2,1)S(1)} %constant_dynamic-update-slice_fusion.refs_0_, ...), custom_call_target="tpu_custom_call" | custom-call | flops 1207959552 | bytes 2359296 | tf_op jit(solution)/shard_map/pallas_call | solution.py:392
  66.8 43.8 %all-gather.3.cloned.1.call-done = bf16[2560,3328]{1,0:T(8,128)(2,1)} async-done(((bf16[160,3328]{1,0:T(8,128)(2,1)}), bf16[2560,3328]{1,0:T(8,128)(2,1)}) %all-gather.3.cloned.1.call-update) | async-done | bytes 17039376 | tf_op jit(solution)/shard_map/all_gather | solution.py:448
  110.6 1.0 copy-done.2
  111.7 3.7 %shard_map.128 = (bf16[128,1280]{1,0:T(8,128)(2,1)S(1)}, bf16[128,1280]{1,0:T(8,128)(2,1)S(1)}) custom-call(bf16[128,2048]{1,0:T(8,128)(2,1)S(1)} %copy-done.2, f32[1,1280]{1,0:T(1,128)S(1)} %broadcast_in_dim.26.gain, bf16[16,160,3328]{2,1,0:T(8,128)(2,1)} %bitcast.166), custom_call_target="tpu_custom_call" | custom-call | flops 4000000000 | bytes 5000000 | tf_op jit(solution)/shard_map/pallas_call | solution.py:466
  115.4 3.4 %shard_map.129 = (bf16[128,640]{1,0:T(8,128)(2,1)S(1)}, bf16[128,1280]{1,0:T(8,128)(2,1)S(1)}) custom-call(bf16[128,1280]{1,0:T(8,128)(2,1)S(1)} %get-tuple-element.10.normed, bf16[16,160,3328]{2,1,0:T(8,128)(2,1)} %bitcast.167), custom_call_target="tpu_custom_call" | custom-call | flops 4000000000 | bytes 5000000 | tf_op jit(solution)/shard_map/pallas_call | solution.py:480
  118.7 2.2 collective-permute-start.13
  120.9 1.3 collective-permute-start.14
  122.2 1.0 slice_bitcast_fusion.4
  123.2 1.4 slice.158
  124.7 3.0 %slice.160 = bf16[16,80,2048]{2,1,0:T(8,128)(2,1)S(1)} slice(bf16[16,160,3328]{2,1,0:T(8,128)(2,1)} %bitcast.170), slice={[0:16], [80:160], [1280:3328]} | slice | bytes 10485760 | tf_op jit(solution)/shard_map/slice | solution.py:449
  127.8 5.5 %shard_map.130 = (bf16[128,1280]{1,0:T(8,128)(2,1)}, bf16[128,1280]{1,0:T(8,128)(2,1)S(1)}) custom-call(s32[4]{0:T(128)S(1)} %bitcast.165, s32[1]{0:T(128)} %bitcast.2.first, bf16[128,640]{1,0:T(8,128)(2,1)S(1)} %get-tuple-element.11.query, bf16[128,1280]{1,0:T(8,128)(2,1)S(1)} %collective-permute-done.13.left, bf16[128,1280]{1,0:T(8,128)(2,1)S(1)} %get-tuple-element.12.own, ...), custom_call_target="tpu_custom_call" | custom-call | flops 4000000000 | bytes 4000000 | tf_op jit(solution)/shard_map/pallas_call | solution.py:500
  133.3 1.0 multiply_reduce_fusion
  134.5 4.4 %collective-permute-start.19 = (bf16[128,1280]{1,0:T(8,128)(2,1)S(1)}, bf16[128,1280]{1,0:T(8,128)(2,1)S(1)}, u32[]{:S(2)}, u32[]{:S(2)}) collective-permute-start(bf16[128,1280]{1,0:T(8,128)(2,1)S(1)} %multiply_convert_fusion.1), channel_id=1, source_target_pairs={{0,4},{1,5},{2,6},{3,7},{4,8},{5,9},{6,10},{7,11},{8,12},{9,13},{1... | collective-permute-start | bytes 983048 | tf_op jit(solution)/shard_map/ppermute | solution.py:93
  138.8 8.9 %convolution_convert_fusion = bf16[1280,1536]{1,0:T(8,128)(2,1)S(1)} fusion(bf16[1280,2048]{1,0:T(8,128)(2,1)S(1)} %bitcast.172, bf16[1,2048,1536]{2,1,0:T(8,128)(2,1)S(1)} %bitcast.202, f32[2048]{0:T(1024)S(1)} %copy-done.7), kind=kOutput, calls=%fused_computation.1 | convolution fusion | flops 8064466944 | bytes 15474688 | tf_op jit(solution)/shard_map/dot_general | solution.py:498
  150.4 1.2 collective-permute-start.30
  151.6 7.9 %collective-permute-done.15 = bf16[128,1280]{1,0:T(8,128)(2,1)S(1)} collective-permute-done((bf16[128,1280]{1,0:T(8,128)(2,1)S(1)}, bf16[128,1280]{1,0:T(8,128)(2,1)S(1)}, u32[]{:S(2)}, u32[]{:S(2)}) %collective-permute-start.15) | collective-permute-done | bytes 327712 | tf_op jit(solution)/shard_map/ppermute | solution.py:93
  159.7 1.7 collective-permute-done.20
  161.3 1.2 collective-permute-start.26
  162.5 4.0 %collective-permute-done.30 = bf16[128,1280]{1,0:T(8,128)(2,1)S(1)} collective-permute-done((bf16[128,1280]{1,0:T(8,128)(2,1)S(1)}, bf16[128,1280]{1,0:T(8,128)(2,1)S(1)}, u32[]{:S(2)}, u32[]{:S(2)}) %collective-permute-start.30) | collective-permute-done | bytes 327712 | tf_op jit(solution)/shard_map/ppermute | solution.py:93
  166.7 1.6 collective-permute-start.21
  168.3 4.7 %collective-permute-done.26 = bf16[128,1280]{1,0:T(8,128)(2,1)S(1)} collective-permute-done((bf16[128,1280]{1,0:T(8,128)(2,1)S(1)}, bf16[128,1280]{1,0:T(8,128)(2,1)S(1)}, u32[]{:S(2)}, u32[]{:S(2)}) %collective-permute-start.26) | collective-permute-done | bytes 327712 | tf_op jit(solution)/shard_map/ppermute | solution.py:93
  173.2 2.2 fusion.76
  175.4 2.1 fusion.11
  179.2 2.2 fusion.79
  181.4 2.0 fusion.20
  183.7 4.2 %collective-permute-done.22 = bf16[128,1280]{1,0:T(8,128)(2,1)S(1)} collective-permute-done((bf16[128,1280]{1,0:T(8,128)(2,1)S(1)}, bf16[128,1280]{1,0:T(8,128)(2,1)S(1)}, u32[]{:S(2)}, u32[]{:S(2)}) %collective-permute-start.22) | collective-permute-done | bytes 327712 | tf_op jit(solution)/shard_map/ppermute | solution.py:93
  188.2 2.2 fusion.78
  190.4 2.0 fusion.17
  193.3 2.2 fusion.77
  195.5 2.2 fusion.14
  199.5 1.6 collective-permute-start.29
  201.1 12.2 %collective-permute-done.33 = bf16[128,2048]{1,0:T(8,128)(2,1)S(1)} collective-permute-done((bf16[128,2048]{1,0:T(8,128)(2,1)S(1)}, bf16[128,2048]{1,0:T(8,128)(2,1)S(1)}, u32[]{:S(2)}, u32[]{:S(2)}) %collective-permute-start.33) | collective-permute-done | bytes 524320 | tf_op jit(solution)/shard_map/ppermute | solution.py:93
  213.4 1.0 collective-permute-start.34
  214.9 1.0 collective-permute-start.25
  215.9 8.7 %collective-permute-done.29 = bf16[128,2048]{1,0:T(8,128)(2,1)S(1)} collective-permute-done((bf16[128,2048]{1,0:T(8,128)(2,1)S(1)}, bf16[128,2048]{1,0:T(8,128)(2,1)S(1)}, u32[]{:S(2)}, u32[]{:S(2)}) %collective-permute-start.29) | collective-permute-done | bytes 524320 | tf_op jit(solution)/shard_map/ppermute | solution.py:93
  224.5 3.8 %collective-permute-done.34 = bf16[128,2048]{1,0:T(8,128)(2,1)S(1)} collective-permute-done((bf16[128,2048]{1,0:T(8,128)(2,1)S(1)}, bf16[128,2048]{1,0:T(8,128)(2,1)S(1)}, u32[]{:S(2)}, u32[]{:S(2)}) %collective-permute-start.34) | collective-permute-done | bytes 524320 | tf_op jit(solution)/shard_map/ppermute | solution.py:93
  229.7 6.1 %collective-permute-done.25 = bf16[128,2048]{1,0:T(8,128)(2,1)S(1)} collective-permute-done((bf16[128,2048]{1,0:T(8,128)(2,1)S(1)}, bf16[128,2048]{1,0:T(8,128)(2,1)S(1)}, u32[]{:S(2)}, u32[]{:S(2)}) %collective-permute-start.25) | collective-permute-done | bytes 524320 | tf_op jit(solution)/shard_map/ppermute | solution.py:93
  235.8 6.8 %collective-permute-done.35 = bf16[128,2048]{1,0:T(8,128)(2,1)S(1)} collective-permute-done((bf16[128,2048]{1,0:T(8,128)(2,1)S(1)}, bf16[128,2048]{1,0:T(8,128)(2,1)S(1)}, u32[]{:S(2)}, u32[]{:S(2)}) %collective-permute-start.35) | collective-permute-done | bytes 524320 | tf_op jit(solution)/shard_map/ppermute | solution.py:93
  242.9 3.7 %collective-permute-done.18 = bf16[128,2048]{1,0:T(8,128)(2,1)S(1)} collective-permute-done((bf16[128,2048]{1,0:T(8,128)(2,1)S(1)}, bf16[128,2048]{1,0:T(8,128)(2,1)S(1)}, u32[]{:S(2)}, u32[]{:S(2)}) %collective-permute-start.18) | collective-permute-done | bytes 524320 | tf_op jit(solution)/shard_map/ppermute | solution.py:93
  246.6 9.4 %collective-permute-done.36 = bf16[128,2048]{1,0:T(8,128)(2,1)S(1)} collective-permute-done((bf16[128,2048]{1,0:T(8,128)(2,1)S(1)}, bf16[128,2048]{1,0:T(8,128)(2,1)S(1)}, u32[]{:S(2)}, u32[]{:S(2)}) %collective-permute-start.36) | collective-permute-done | bytes 524320 | tf_op jit(solution)/shard_map/ppermute | solution.py:93
  255.9 1.1 fusion.43
  (99 shorter events, 13.7 us)
Async XLA Ops:
  6.5 168.9 %copy-start = (bf16[1,768,2048]{2,1,0:T(8,128)(2,1)S(1)}, bf16[1,768,2048]{2,1,0:T(8,128)(2,1)}, u32[]{:S(2)}) copy-start(bf16[1,768,2048]{2,1,0:T(8,128)(2,1)} %param.25) | copy-start | bytes 9437188
  6.5 4.1 %copy-start.6 = (s32[128,8]{0,1:T(8,128)S(1)}, s32[128,8]{0,1:T(8,128)}, u32[]{:S(2)}) copy-start(s32[128,8]{0,1:T(8,128)} %param.15) | copy-start | bytes 12292
  6.5 4.1 %copy-start.5 = (f32[128,8]{0,1:T(8,128)S(1)}, f32[128,8]{0,1:T(8,128)}, u32[]{:S(2)}) copy-start(f32[128,8]{0,1:T(8,128)} %param.16) | copy-start | bytes 12292
  6.5 104.1 %all-gather.3.cloned.1.call-start = ((), (), s32[]{:S(2)}) async-start(), calls=%async_computation | async-start | bytes 18104320 | tf_op jit(solution)/shard_map/all_gather | solution.py:448
  8.3 37.9 %copy-start.4 = (f32[1280]{0:T(1024)S(1)}, f32[1280]{0:T(1024)}, u32[]{:S(2)}) copy-start(f32[1280]{0:T(1024)} %param.19) | copy-start | bytes 15364
  10.7 6.7 %collective-permute-start.8 = (f32[16,128]{1,0:T(8,128)S(1)}, f32[16,128]{1,0:T(8,128)S(1)}, u32[]{:S(2)}, u32[]{:S(2)}) collective-permute-start(f32[16,128]{1,0:T(8,128)S(1)} %select_reduce_fusion), channel_id=1, source_target_pairs={{0,4},{1,5},{2,6},{3,7},{4,8},{5,9},{6,10},{7,11},{8,12},{9,13},{1... | collective-permute-start | bytes 24584 | tf_op jit(solution)/shard_map/ppermute | solution.py:93
  17.4 5.6 %collective-permute-start.9 = (f32[16,128]{1,0:T(8,128)S(1)}, f32[16,128]{1,0:T(8,128)S(1)}, u32[]{:S(2)}, u32[]{:S(2)}) collective-permute-start(f32[16,128]{1,0:T(8,128)S(1)} %collective-permute-done.8), channel_id=1, source_target_pairs={{0,4},{1,5},{2,6},{3,7},{4,8},{5,9},{6,10},{7,11},{8,12},{9,13},{1... | collective-permute-start | bytes 24584 | tf_op jit(solution)/shard_map/ppermute | solution.py:93
  23.0 6.1 %collective-permute-start.10 = (f32[16,128]{1,0:T(8,128)S(1)}, f32[16,128]{1,0:T(8,128)S(1)}, u32[]{:S(2)}, u32[]{:S(2)}) collective-permute-start(f32[16,128]{1,0:T(8,128)S(1)} %collective-permute-done.9), channel_id=1, source_target_pairs={{0,4},{1,5},{2,6},{3,7},{4,8},{5,9},{6,10},{7,11},{8,12},{9,13},{1... | collective-permute-start | bytes 24584 | tf_op jit(solution)/shard_map/ppermute | solution.py:93
  23.0 17.3 %collective-permute-start.2 = (bf16[144,256]{1,0:T(8,128)(2,1)}, bf16[144,256]{1,0:T(8,128)(2,1)}, u32[]{:S(2)}, u32[]{:S(2)}) collective-permute-start(bf16[144,256]{1,0:T(8,128)(2,1)} %param.17), channel_id=1, source_target_pairs={{0,4},{1,5},{2,6},{3,7},{4,8},{5,9},{6,10},{7,11},{8,12},{9,13},{1... | collective-permute-start | bytes 221192 | tf_op jit(solution)/shard_map/ppermute | solution.py:179
  23.0 14.9 %collective-permute-start.1 = (bf16[144,256]{1,0:T(8,128)(2,1)}, bf16[144,256]{1,0:T(8,128)(2,1)}, u32[]{:S(2)}, u32[]{:S(2)}) collective-permute-start(bf16[144,256]{1,0:T(8,128)(2,1)} %param.17), channel_id=1, source_target_pairs={{0,2},{1,3},{2,0},{3,1},{4,6},{5,7},{6,4},{7,5},{8,10},{9,11},{10,... | collective-permute-start | bytes 221192 | tf_op jit(solution)/shard_map/ppermute | solution.py:179
  24.7 16.4 %collective-permute-start.3 = (bf16[144,256]{1,0:T(8,128)(2,1)}, bf16[144,256]{1,0:T(8,128)(2,1)}, u32[]{:S(2)}, u32[]{:S(2)}) collective-permute-start(bf16[144,256]{1,0:T(8,128)(2,1)} %param.17), channel_id=1, source_target_pairs={{0,8},{1,9},{2,10},{3,11},{4,12},{5,13},{6,14},{7,15},{8,0},{9,1},... | collective-permute-start | bytes 221192 | tf_op jit(solution)/shard_map/ppermute | solution.py:179
  29.1 12.9 %collective-permute-start.4 = (bf16[144,256]{1,0:T(8,128)(2,1)}, bf16[144,256]{1,0:T(8,128)(2,1)}, u32[]{:S(2)}, u32[]{:S(2)}) collective-permute-start(bf16[144,256]{1,0:T(8,128)(2,1)} %param.17), channel_id=1, source_target_pairs={{0,12},{1,13},{2,14},{3,15},{4,0},{5,1},{6,2},{7,3},{8,4},{9,5},{1... | collective-permute-start | bytes 221192 | tf_op jit(solution)/shard_map/ppermute | solution.py:179
  29.7 4.9 %collective-permute-start.11 = (f32[4,16,128]{2,1,0:T(8,128)}, f32[4,16,128]{2,1,0:T(8,128)}, u32[]{:S(2)}, u32[]{:S(2)}) collective-permute-start(f32[4,16,128]{2,1,0:T(8,128)} %get-tuple-element.34), channel_id=1, source_target_pairs={{0,2},{1,3},{2,0},{3,1},{4,6},{5,7},{6,4},{7,5},{8,10},{9,11},{10,... | collective-permute-start | bytes 98312 | tf_op jit(solution)/shard_map/ppermute | solution.py:93
  34.6 23.2 %collective-permute-start = (bf16[1,4096]{1,0:T(2,128)(2,1)}, bf16[1,4096]{1,0:T(2,128)(2,1)}, u32[]{:S(2)}, u32[]{:S(2)}) collective-permute-start(bf16[1,4096]{1,0:T(2,128)(2,1)} %slice.119), channel_id=1, source_target_pairs={{0,1},{1,2},{2,3},{3,4},{4,5},{5,6},{6,7},{7,8},{8,9},{9,10},{10,1... | collective-permute-start | bytes 24584 | tf_op jit(solution)/shard_map/ppermute | solution.py:18
  37.9 9.2 %collective-permute-start.12 = (f32[2,4,16,128]{3,2,1,0:T(8,128)}, f32[2,4,16,128]{3,2,1,0:T(8,128)}, u32[]{:S(2)}, u32[]{:S(2)}) collective-permute-start(f32[2,4,16,128]{3,2,1,0:T(8,128)} %get-tuple-element.31), channel_id=1, source_target_pairs={{0,1},{1,0},{2,3},{3,2},{4,5},{5,4},{6,7},{7,6},{8,9},{9,8},{10,11... | collective-permute-start | bytes 196616 | tf_op jit(solution)/shard_map/ppermute | solution.py:93
  42.9 14.9 %collective-permute-start.6 = (bf16[5,144,256]{2,1,0:T(8,128)(2,1)S(1)}, bf16[5,144,256]{2,1,0:T(8,128)(2,1)}, u32[]{:S(2)}, u32[]{:S(2)}) collective-permute-start(bf16[5,144,256]{2,1,0:T(8,128)(2,1)S(1)} %constant_dynamic-update-slice_fusion.refs_0_), channel_id=1, source_target_pairs={{0,1},{1,0},{2,3},{3,2},{4,5},{5,4},{6,7},{7,6},{8,9},{9,8},{10,11... | collective-permute-start | bytes 1105928 | tf_op jit(solution)/shard_map/ppermute | solution.py:179
  44.6 13.2 %collective-permute-start.5 = (bf16[3,144,256]{2,1,0:T(8,128)(2,1)}, bf16[3,144,256]{2,1,0:T(8,128)(2,1)}, u32[]{:S(2)}, u32[]{:S(2)}) collective-permute-start(bf16[3,144,256]{2,1,0:T(8,128)(2,1)} %pad_maximum_fusion.9), channel_id=1, source_target_pairs={{0,2},{1,3},{2,0},{3,1},{4,6},{5,7},{6,4},{7,5},{8,10},{9,11},{10,... | collective-permute-start | bytes 663560 | tf_op jit(solution)/shard_map/ppermute | solution.py:179
  57.8 1.7 collective-permute-start.7
  59.5 1.6 copy-start.3
  66.0 0.8 copy-start.1
  110.6 1.0 copy-start.2
  118.7 9.0 %collective-permute-start.13 = (bf16[128,1280]{1,0:T(8,128)(2,1)S(1)}, bf16[128,1280]{1,0:T(8,128)(2,1)S(1)}, u32[]{:S(2)}, u32[]{:S(2)}) collective-permute-start(bf16[128,1280]{1,0:T(8,128)(2,1)S(1)} %get-tuple-element.12.own), channel_id=1, source_target_pairs={{0,1},{1,2},{2,3},{3,4},{4,5},{5,6},{6,7},{7,8},{8,9},{9,10},{10,1... | collective-permute-start | bytes 983048 | tf_op jit(solution)/shard_map/ppermute | solution.py:18
  120.9 6.8 %collective-permute-start.14 = (bf16[128,1280]{1,0:T(8,128)(2,1)S(1)}, bf16[128,1280]{1,0:T(8,128)(2,1)S(1)}, u32[]{:S(2)}, u32[]{:S(2)}) collective-permute-start(bf16[128,1280]{1,0:T(8,128)(2,1)S(1)} %get-tuple-element.12.own), channel_id=1, source_target_pairs={{1,0},{2,1},{3,2},{4,3},{5,4},{6,5},{7,6},{8,7},{9,8},{10,9},{11,1... | collective-permute-start | bytes 983048 | tf_op jit(solution)/shard_map/ppermute | solution.py:18
  127.6 11.2 %slice-start = ((s8[6291456]{0:T(1024)(128)(4,1)}), s8[2097152]{0:T(1024)(128)(4,1)S(1)}, s32[]{:S(2)}) async-start(s8[6291456]{0:T(1024)(128)(4,1)} %bitcast.201), calls=%async_computation.1 | async-start | bytes 4194304
  127.8 11.1 %slice-start.1 = ((s8[6291456]{0:T(1024)(128)(4,1)}), s8[4194304]{0:T(1024)(128)(4,1)S(1)}, s32[]{:S(2)}) async-start(s8[6291456]{0:T(1024)(128)(4,1)} %bitcast.201), calls=%async_computation.2 | async-start | bytes 8388608
  133.3 5.5 %copy-start.7 = (f32[2048]{0:T(1024)S(1)}, f32[2048]{0:T(1024)}, u32[]{:S(2)}) copy-start(f32[2048]{0:T(1024)} %param.23) | copy-start | bytes 24580
  134.5 15.4 %collective-permute-start.19 = (bf16[128,1280]{1,0:T(8,128)(2,1)S(1)}, bf16[128,1280]{1,0:T(8,128)(2,1)S(1)}, u32[]{:S(2)}, u32[]{:S(2)}) collective-permute-start(bf16[128,1280]{1,0:T(8,128)(2,1)S(1)} %multiply_convert_fusion.1), channel_id=1, source_target_pairs={{0,4},{1,5},{2,6},{3,7},{4,8},{5,9},{6,10},{7,11},{8,12},{9,13},{1... | collective-permute-start | bytes 983048 | tf_op jit(solution)/shard_map/ppermute | solution.py:93
  148.9 10.6 %collective-permute-start.15 = (bf16[128,1280]{1,0:T(8,128)(2,1)S(1)}, bf16[128,1280]{1,0:T(8,128)(2,1)S(1)}, u32[]{:S(2)}, u32[]{:S(2)}) collective-permute-start(bf16[128,1280]{1,0:T(8,128)(2,1)S(1)} %multiply_convert_fusion.1), channel_id=1, source_target_pairs={{0,2},{1,3},{2,0},{3,1},{4,6},{5,7},{6,4},{7,5},{8,10},{9,11},{10,... | collective-permute-start | bytes 983048 | tf_op jit(solution)/shard_map/ppermute | solution.py:93
  149.9 11.5 %collective-permute-start.20 = (bf16[128,1280]{1,0:T(8,128)(2,1)S(1)}, bf16[128,1280]{1,0:T(8,128)(2,1)S(1)}, u32[]{:S(2)}, u32[]{:S(2)}) collective-permute-start(bf16[128,1280]{1,0:T(8,128)(2,1)S(1)} %add_convert_fusion), channel_id=1, source_target_pairs={{0,4},{1,5},{2,6},{3,7},{4,8},{5,9},{6,10},{7,11},{8,12},{9,13},{1... | collective-permute-start | bytes 983048 | tf_op jit(solution)/shard_map/ppermute | solution.py:93
  150.4 16.1 %collective-permute-start.30 = (bf16[128,1280]{1,0:T(8,128)(2,1)S(1)}, bf16[128,1280]{1,0:T(8,128)(2,1)S(1)}, u32[]{:S(2)}, u32[]{:S(2)}) collective-permute-start(bf16[128,1280]{1,0:T(8,128)(2,1)S(1)} %collective-permute-done.19), channel_id=1, source_target_pairs={{0,2},{1,3},{2,0},{3,1},{4,6},{5,7},{6,4},{7,5},{8,10},{9,11},{10,... | collective-permute-start | bytes 983048 | tf_op jit(solution)/shard_map/ppermute | solution.py:93
  159.6 13.5 %collective-permute-start.16 = (bf16[2,128,1280]{2,1,0:T(8,128)(2,1)S(1)}, bf16[2,128,1280]{2,1,0:T(8,128)(2,1)S(1)}, u32[]{:S(2)}, u32[]{:S(2)}) collective-permute-start(bf16[2,128,1280]{2,1,0:T(8,128)(2,1)S(1)} %get-tuple-element.30), channel_id=1, source_target_pairs={{0,1},{1,0},{2,3},{3,2},{4,5},{5,4},{6,7},{7,6},{8,9},{9,8},{10,11... | collective-permute-start | bytes 1966088 | tf_op jit(solution)/shard_map/ppermute | solution.py:93
  161.3 11.6 %collective-permute-start.26 = (bf16[128,1280]{1,0:T(8,128)(2,1)S(1)}, bf16[128,1280]{1,0:T(8,128)(2,1)S(1)}, u32[]{:S(2)}, u32[]{:S(2)}) collective-permute-start(bf16[128,1280]{1,0:T(8,128)(2,1)S(1)} %collective-permute-done.20), channel_id=1, source_target_pairs={{0,2},{1,3},{2,0},{3,1},{4,6},{5,7},{6,4},{7,5},{8,10},{9,11},{10,... | collective-permute-start | bytes 983048 | tf_op jit(solution)/shard_map/ppermute | solution.py:93
  166.6 12.5 %collective-permute-start.31 = (bf16[2,128,1280]{2,1,0:T(8,128)(2,1)S(1)}, bf16[2,128,1280]{2,1,0:T(8,128)(2,1)S(1)}, u32[]{:S(2)}, u32[]{:S(2)}) collective-permute-start(bf16[2,128,1280]{2,1,0:T(8,128)(2,1)S(1)} %get-tuple-element.24), channel_id=1, source_target_pairs={{0,1},{1,0},{2,3},{3,2},{4,5},{5,4},{6,7},{7,6},{8,9},{9,8},{10,11... | collective-permute-start | bytes 1966088 | tf_op jit(solution)/shard_map/ppermute | solution.py:93
  166.7 11.9 %collective-permute-start.21 = (bf16[128,1280]{1,0:T(8,128)(2,1)S(1)}, bf16[128,1280]{1,0:T(8,128)(2,1)S(1)}, u32[]{:S(2)}, u32[]{:S(2)}) collective-permute-start(bf16[128,1280]{1,0:T(8,128)(2,1)S(1)} %collective-permute-done.20), channel_id=1, source_target_pairs={{0,4},{1,5},{2,6},{3,7},{4,8},{5,9},{6,10},{7,11},{8,12},{9,13},{1... | collective-permute-start | bytes 983048 | tf_op jit(solution)/shard_map/ppermute | solution.py:93
  173.0 15.1 %collective-permute-start.27 = (bf16[2,128,1280]{2,1,0:T(8,128)(2,1)S(1)}, bf16[2,128,1280]{2,1,0:T(8,128)(2,1)S(1)}, u32[]{:S(2)}, u32[]{:S(2)}) collective-permute-start(bf16[2,128,1280]{2,1,0:T(8,128)(2,1)S(1)} %get-tuple-element.26), channel_id=1, source_target_pairs={{0,1},{1,0},{2,3},{3,2},{4,5},{5,4},{6,7},{7,6},{8,9},{9,8},{10,11... | collective-permute-start | bytes 1966088 | tf_op jit(solution)/shard_map/ppermute | solution.py:93
  177.6 51.0 %collective-permute-start.17 = (bf16[2,128,2048]{2,1,0:T(8,128)(2,1)S(1)}, bf16[2,128,2048]{2,1,0:T(8,128)(2,1)S(1)}, u32[]{:S(2)}, u32[]{:S(2)}) collective-permute-start(bf16[2,128,2048]{2,1,0:T(8,128)(2,1)S(1)} %bitcast.182), channel_id=1, source_target_pairs={{0,1},{1,0},{2,3},{3,2},{4,5},{5,4},{6,7},{7,6},{8,9},{9,8},{10,11... | collective-permute-start | bytes 3145736 | tf_op jit(solution)/shard_map/ppermute | solution.py:93
  178.6 9.3 %collective-permute-start.22 = (bf16[128,1280]{1,0:T(8,128)(2,1)S(1)}, bf16[128,1280]{1,0:T(8,128)(2,1)S(1)}, u32[]{:S(2)}, u32[]{:S(2)}) collective-permute-start(bf16[128,1280]{1,0:T(8,128)(2,1)S(1)} %collective-permute-done.21), channel_id=1, source_target_pairs={{0,2},{1,3},{2,0},{3,1},{4,6},{5,7},{6,4},{7,5},{8,10},{9,11},{10,... | collective-permute-start | bytes 983048 | tf_op jit(solution)/shard_map/ppermute | solution.py:93
  183.6 14.5 %collective-permute-start.32 = (bf16[2,128,2048]{2,1,0:T(8,128)(2,1)S(1)}, bf16[2,128,2048]{2,1,0:T(8,128)(2,1)S(1)}, u32[]{:S(2)}, u32[]{:S(2)}) collective-permute-start(bf16[2,128,2048]{2,1,0:T(8,128)(2,1)S(1)} %bitcast.183), channel_id=1, source_target_pairs={{0,1},{1,0},{2,3},{3,2},{4,5},{5,4},{6,7},{7,6},{8,9},{9,8},{10,11... | collective-permute-start | bytes 3145736 | tf_op jit(solution)/shard_map/ppermute | solution.py:93
  188.0 5.2 %collective-permute-start.23 = (bf16[2,128,1280]{2,1,0:T(8,128)(2,1)S(1)}, bf16[2,128,1280]{2,1,0:T(8,128)(2,1)S(1)}, u32[]{:S(2)}, u32[]{:S(2)}) collective-permute-start(bf16[2,128,1280]{2,1,0:T(8,128)(2,1)S(1)} %get-tuple-element.28), channel_id=1, source_target_pairs={{0,1},{1,0},{2,3},{3,2},{4,5},{5,4},{6,7},{7,6},{8,9},{9,8},{10,11... | collective-permute-start | bytes 1966088 | tf_op jit(solution)/shard_map/ppermute | solution.py:93
  192.6 6.4 %collective-permute-start.28 = (bf16[2,128,2048]{2,1,0:T(8,128)(2,1)S(1)}, bf16[2,128,2048]{2,1,0:T(8,128)(2,1)S(1)}, u32[]{:S(2)}, u32[]{:S(2)}) collective-permute-start(bf16[2,128,2048]{2,1,0:T(8,128)(2,1)S(1)} %bitcast.185), channel_id=1, source_target_pairs={{0,1},{1,0},{2,3},{3,2},{4,5},{5,4},{6,7},{7,6},{8,9},{9,8},{10,11... | collective-permute-start | bytes 3145736 | tf_op jit(solution)/shard_map/ppermute | solution.py:93
  198.0 16.5 %collective-permute-start.24 = (bf16[2,128,2048]{2,1,0:T(8,128)(2,1)S(1)}, bf16[2,128,2048]{2,1,0:T(8,128)(2,1)S(1)}, u32[]{:S(2)}, u32[]{:S(2)}) collective-permute-start(bf16[2,128,2048]{2,1,0:T(8,128)(2,1)S(1)} %bitcast.184), channel_id=1, source_target_pairs={{0,1},{1,0},{2,3},{3,2},{4,5},{5,4},{6,7},{7,6},{8,9},{9,8},{10,11... | collective-permute-start | bytes 3145736 | tf_op jit(solution)/shard_map/ppermute | solution.py:93
  198.5 14.8 %collective-permute-start.33 = (bf16[128,2048]{1,0:T(8,128)(2,1)S(1)}, bf16[128,2048]{1,0:T(8,128)(2,1)S(1)}, u32[]{:S(2)}, u32[]{:S(2)}) collective-permute-start(bf16[128,2048]{1,0:T(8,128)(2,1)S(1)} %fusion.59), channel_id=1, source_target_pairs={{0,2},{1,3},{2,0},{3,1},{4,6},{5,7},{6,4},{7,5},{8,10},{9,11},{10,... | collective-permute-start | bytes 1572872 | tf_op jit(solution)/shard_map/ppermute | solution.py:93
  199.5 25.1 %collective-permute-start.29 = (bf16[128,2048]{1,0:T(8,128)(2,1)S(1)}, bf16[128,2048]{1,0:T(8,128)(2,1)S(1)}, u32[]{:S(2)}, u32[]{:S(2)}) collective-permute-start(bf16[128,2048]{1,0:T(8,128)(2,1)S(1)} %fusion.58), channel_id=1, source_target_pairs={{0,2},{1,3},{2,0},{3,1},{4,6},{5,7},{6,4},{7,5},{8,10},{9,11},{10,... | collective-permute-start | bytes 1572872 | tf_op jit(solution)/shard_map/ppermute | solution.py:93
  213.4 15.0 %collective-permute-start.34 = (bf16[128,2048]{1,0:T(8,128)(2,1)S(1)}, bf16[128,2048]{1,0:T(8,128)(2,1)S(1)}, u32[]{:S(2)}, u32[]{:S(2)}) collective-permute-start(bf16[128,2048]{1,0:T(8,128)(2,1)S(1)} %fusion.33), channel_id=1, source_target_pairs={{0,4},{1,5},{2,6},{3,7},{4,8},{5,9},{6,10},{7,11},{8,12},{9,13},{1... | collective-permute-start | bytes 1572872 | tf_op jit(solution)/shard_map/ppermute | solution.py:93
  214.9 20.9 %collective-permute-start.25 = (bf16[128,2048]{1,0:T(8,128)(2,1)S(1)}, bf16[128,2048]{1,0:T(8,128)(2,1)S(1)}, u32[]{:S(2)}, u32[]{:S(2)}) collective-permute-start(bf16[128,2048]{1,0:T(8,128)(2,1)S(1)} %fusion.57), channel_id=1, source_target_pairs={{0,2},{1,3},{2,0},{3,1},{4,6},{5,7},{6,4},{7,5},{8,10},{9,11},{10,... | collective-permute-start | bytes 1572872 | tf_op jit(solution)/shard_map/ppermute | solution.py:93
  228.6 14.0 %collective-permute-start.35 = (bf16[128,2048]{1,0:T(8,128)(2,1)S(1)}, bf16[128,2048]{1,0:T(8,128)(2,1)S(1)}, u32[]{:S(2)}, u32[]{:S(2)}) collective-permute-start(bf16[128,2048]{1,0:T(8,128)(2,1)S(1)} %fusion.36), channel_id=1, source_target_pairs={{0,4},{1,5},{2,6},{3,7},{4,8},{5,9},{6,10},{7,11},{8,12},{9,13},{1... | collective-permute-start | bytes 1572872 | tf_op jit(solution)/shard_map/ppermute | solution.py:93
  229.1 17.5 %collective-permute-start.18 = (bf16[128,2048]{1,0:T(8,128)(2,1)S(1)}, bf16[128,2048]{1,0:T(8,128)(2,1)S(1)}, u32[]{:S(2)}, u32[]{:S(2)}) collective-permute-start(bf16[128,2048]{1,0:T(8,128)(2,1)S(1)} %fusion.56), channel_id=1, source_target_pairs={{0,2},{1,3},{2,0},{3,1},{4,6},{5,7},{6,4},{7,5},{8,10},{9,11},{10,... | collective-permute-start | bytes 1572872 | tf_op jit(solution)/shard_map/ppermute | solution.py:93
  242.8 13.1 %collective-permute-start.36 = (bf16[128,2048]{1,0:T(8,128)(2,1)S(1)}, bf16[128,2048]{1,0:T(8,128)(2,1)S(1)}, u32[]{:S(2)}, u32[]{:S(2)}) collective-permute-start(bf16[128,2048]{1,0:T(8,128)(2,1)S(1)} %fusion.39), channel_id=1, source_target_pairs={{0,4},{1,5},{2,6},{3,7},{4,8},{5,9},{6,10},{7,11},{8,12},{9,13},{1... | collective-permute-start | bytes 1572872 | tf_op jit(solution)/shard_map/ppermute | solution.py:93
Sparse Core Ops, SparseCore 0:
  10.7 99.8 all-gather.2

commit v2 on v1

--- a/solution.py
+++ b/solution.py
@@ -133,16 +133,18 @@
     inner = down.shape[0]
     width = down.shape[1]
     blocks = [scaled]
+    early = ring_step(scaled, cores, ys)
     for k in range(1, zs):
-        sent = once(blocks[-1], fused) if k == 2 else blocks[-1]
+        sent = once(once(blocks[-1], fused), early) if k == 2 else blocks[-1]
         blocks.append(ring_step(sent, ys * cores, zs))
     totals, columns, carry = {}, {}, None
 
     def send(k):
         block = blocks[k]
         line = [block]
-        for _ in range(ys - 1):
-            line.append(ring_step(line[-1], cores, ys))
+        for dy in range(1, ys):
+            known = k == 0 and dy == 1
+            line.append(early if known else ring_step(line[-1], cores, ys))
         pair = jnp.stack(line)
         return jnp.stack([pair, ring_step(pair, 1, cores)])
 
@@ -290,29 +292,33 @@
     ]
     for copy in copies:
         copy.start()
-    for copy in copies:
+    return copies
+
+
+def embed_kernel(
+    rows, act, gain, gathered, embed, query, key_rows, weight, attn, weight_sems, attn_sems
+):
+    weight_copies = fetch(gathered, rows, 0, weight, weight_sems)
+    attn_copies = fetch(
+        gathered, attn.shape[0] // gathered.shape[0], weight.shape[1], attn, attn_sems
+    )
+    for copy in weight_copies:
         copy.wait()
-
-
-def embed_kernel(rows, act, gain, gathered, embed, normed, weight, sems):
-    fetch(gathered, rows, 0, weight, sems)
     step = 256
     for low in range(0, embed.shape[1], step):
         span = slice(low, low + step)
         sums = jnp.dot(act[...], weight[:, span], preferred_element_type=jnp.float32)
         embed[:, span] = sums.astype(jnp.bfloat16)
     kept = embed[...].astype(jnp.float32)
-    normed[...] = (norm_rows(kept) * gain[...]).astype(jnp.bfloat16)
-
-
-def qkv_kernel(first, normed, gathered, query, key_rows, weight, sems):
-    fetch(gathered, weight.shape[0] // gathered.shape[0], first, weight, sems)
+    normed = (norm_rows(kept) * gain[...]).astype(jnp.bfloat16)
+    for copy in attn_copies:
+        copy.wait()
     width = query.shape[1]
     query[...] = jnp.dot(
-        normed[...], weight[:, :width], preferred_element_type=jnp.float32
+        normed, attn[:, :width], preferred_element_type=jnp.float32
     ).astype(jnp.bfloat16)
     key_rows[...] = jnp.dot(
-        normed[...], weight[:, width:], preferred_element_type=jnp.float32
+        normed, attn[:, width:], preferred_element_type=jnp.float32
     ).astype(jnp.bfloat16)
 
 
@@ -463,34 +469,22 @@
         [pltpu.VMEM((3, (bins + 1) * tokens, 2 * channels), jnp.bfloat16)],
         gates,
     )
-    embed, normed = pl.pallas_call(
+    embed, query, key_rows = pl.pallas_call(
         functools.partial(embed_kernel, high),
-        out_shape=(rows_of(tokens, dim), rows_of(tokens, dim)),
+        out_shape=(rows_of(tokens, dim), rows_of(tokens, width), rows_of(tokens, 2 * width)),
         in_specs=[VMEM, VMEM, HBM],
-        out_specs=(VMEM, VMEM),
+        out_specs=(VMEM, VMEM, VMEM),
         scratch_shapes=[
             pltpu.VMEM((devices * high, dim), jnp.bfloat16),
+            pltpu.VMEM((devices * rows, wide), jnp.bfloat16),
+            pltpu.SemaphoreType.DMA((devices,)),
             pltpu.SemaphoreType.DMA((devices,)),
         ],
         compiler_params=room(46),
         cost_estimate=pl.CostEstimate(
-            flops=4 * 10**9, bytes_accessed=5 * 10**6, transcendentals=0
+            flops=8 * 10**9, bytes_accessed=10**7, transcendentals=0
         ),
     )(conv_act, ln_gain[None], late_full)
-    query, key_rows = pl.pallas_call(
-        functools.partial(qkv_kernel, dim),
-        out_shape=(rows_of(tokens, width), rows_of(tokens, 2 * width)),
-        in_specs=[VMEM, HBM],
-        out_specs=(VMEM, VMEM),
-        scratch_shapes=[
-            pltpu.VMEM((devices * rows, wide), jnp.bfloat16),
-            pltpu.SemaphoreType.DMA((devices,)),
-        ],
-        compiler_params=room(46),
-        cost_estimate=pl.CostEstimate(
-            flops=4 * 10**9, bytes_accessed=5 * 10**6, transcendentals=0
-        ),
-    )(normed, late_full)
     left = shifted(key_rows[-WIN:], "seq", 1)
     right = shifted(key_rows[:WIN], "seq", -1)
     ends = jnp.cumsum(recording_lengths).astype(jnp.int32)

time: 265 us -> 262 us (0.989)
  waiting for transfers between devices: 140 us -> 134 us
    ppermute x27, waiting for transfers between devices: 84.5 us -> 78.9 us  [ring_step(): return lax.ppermute(block, 'seq', route)]
    pallas_call x1 -> x0, Pallas kernels: 3.36 us -> none  [dense_device(): pl.pallas_call(functools.partial(qkv_kernel, dim), out_shape=(rows_of(tok...]
    pallas_call x1, Pallas kernels: 3.71 us -> 6.42 us  [dense_device(): pl.pallas_call(functools.partial(embed_kernel, high), out_shape=(rows_of(...]
  transfers between devices with their start and end apart: 38 -> 38, of which waited for: 20 -> 16; matrix products, arithmetic and copies ran while one was open for 18% -> 18% of each run, Pallas kernels for 2% -> 2%
where the time goes in v2:
time: 262 us; the launch traced here: 261 us
  waiting for transfers between devices  134 us (51%)
  starting transfers between devices  37.4 us (14%)
  matrix products  26.9 us (10%)
  local copies, waits for them, and re-layouts  18.5 us (7%)
  Pallas kernels  16.9 us (6%)
  between operations  15.2 us (6%)
  other arithmetic  12 us (5%)
    ppermute x27, waiting for transfers between devices, ring_step(): return lax.ppermute(block, 'seq', route)  78.9 us
    all_gather x1, waiting for transfers between devices, dense_device(): late_full = lax.all_gather(packed, 'seq', axis=0)  43.8 us
    ppermute x27, starting transfers between devices, ring_step(): return lax.ppermute(block, 'seq', route)  24.4 us
    ppermute x7, waiting for transfers between devices, hop(): return lax.ppermute(block, 'seq', route)  11.6 us
    dot_general x1, matrix products, dense_device(): fused = jnp.dot(audio_full, weighted, preferred_element_type=jnp.float32)  8.87 us
    dot_general x4, matrix products, dense_experts(): both = jnp.dot(rows, fused, preferred_element_type=jnp.float32)  8.77 us
    dot_general x4, matrix products, dense_experts(): jnp.dot(hidden, down, preferred_element_type=jnp.float32)  8.31 us
    ppermute x7, starting transfers between devices, hop(): return lax.ppermute(block, 'seq', route)  7.68 us
  transfers between devices with their start and end apart: 38, of which 16 were waited for; matrix products, arithmetic and copies ran while one was open for 18% of the time, Pallas kernels for 2%

profile of v2, /device:TPU:0, one launch (start us, length us, event | category | flops | bytes accessed | tf_op | source)
XLA Modules:
  0.0 261.2 jit_solution(15311847794139223090)
XLA Ops:
  6.5 1.0 slice.127
  8.3 2.3 maximum_maximum_fusion
  10.7 3.1 %collective-permute-start.8 = (f32[16,128]{1,0:T(8,128)S(1)}, f32[16,128]{1,0:T(8,128)S(1)}, u32[]{:S(2)}, u32[]{:S(2)}) collective-permute-start(f32[16,128]{1,0:T(8,128)S(1)} %select_reduce_fusion), channel_id=1, source_target_pairs={{0,4},{1,5},{2,6},{3,7},{4,8},{5,9},{6,10},{7,11},{8,12},{9,13},{1... | collective-permute-start | bytes 24584 | tf_op jit(solution)/shard_map/ppermute | solution.py:93
  13.7 3.7 %collective-permute-done.8 = f32[16,128]{1,0:T(8,128)S(1)} collective-permute-done((f32[16,128]{1,0:T(8,128)S(1)}, f32[16,128]{1,0:T(8,128)S(1)}, u32[]{:S(2)}, u32[]{:S(2)}) %collective-permute-start.8) | collective-permute-done | bytes 8224 | tf_op jit(solution)/shard_map/ppermute | solution.py:93
  17.4 5.6 %collective-permute-done.9 = f32[16,128]{1,0:T(8,128)S(1)} collective-permute-done((f32[16,128]{1,0:T(8,128)S(1)}, f32[16,128]{1,0:T(8,128)S(1)}, u32[]{:S(2)}, u32[]{:S(2)}) %collective-permute-start.9) | collective-permute-done | bytes 8224 | tf_op jit(solution)/shard_map/ppermute | solution.py:93
  23.0 1.7 collective-permute-start.1
  24.7 4.4 %collective-permute-start.3 = (bf16[144,256]{1,0:T(8,128)(2,1)}, bf16[144,256]{1,0:T(8,128)(2,1)}, u32[]{:S(2)}, u32[]{:S(2)}) collective-permute-start(bf16[144,256]{1,0:T(8,128)(2,1)} %param.17), channel_id=1, source_target_pairs={{0,8},{1,9},{2,10},{3,11},{4,12},{5,13},{6,14},{7,15},{8,0},{9,1},... | collective-permute-start | bytes 221192 | tf_op jit(solution)/shard_map/ppermute | solution.py:181
  29.7 1.3 collective-permute-start.11
  31.0 0.9 bitcast_dynamic-update-slice_fusion.1
  31.9 1.5 slice.122
  33.3 1.3 collective-permute-done.11
  34.6 1.9 collective-permute-start
  36.5 1.4 pad_maximum_fusion.10
  37.9 1.4 collective-permute-start.12
  39.3 0.9 bitcast_dynamic-update-slice_fusion
  40.2 0.9 constant_dynamic-update-slice_fusion.2
  41.1 0.9 constant_dynamic-update-slice_fusion.1
  42.0 0.9 constant_dynamic-update-slice_fusion.refs_0_
  42.9 1.7 pad_maximum_fusion.9
  44.6 1.5 collective-permute-start.5
  46.2 0.8 reduce-window.9
  47.1 0.8 fusion.60
  47.9 9.9 %collective-permute-done.5.refs_1_ = bf16[3,144,256]{2,1,0:T(8,128)(2,1)} collective-permute-done((bf16[3,144,256]{2,1,0:T(8,128)(2,1)}, bf16[3,144,256]{2,1,0:T(8,128)(2,1)}, u32[]{:S(2)}, u32[]{:S(2)}) %collective-permute-start.5) | collective-permute-done | bytes 221216 | tf_op jit(solution)/shard_map/ppermute | solution.py:181
  57.8 1.7 collective-permute-done.7.refs_3_
  59.5 1.6 copy-done.1
  61.1 4.9 %shard_map.127.act = bf16[128,2048]{1,0:T(8,128)(2,1)S(1)} custom-call(s32[4]{0:T(128)S(1)} %pad_add_fusion.place, bf16[256,4096]{1,0:T(8,128)(2,1)S(1)} %copy-done.1, bf16[1,4096]{1,0:T(2,128)(2,1)} %collective-permute-done.rim, bf16[5,144,256]{2,1,0:T(8,128)(2,1)S(1)} %constant_dynamic-update-slice_fusion.refs_0_, ...), custom_call_target="tpu_custom_call" | custom-call | flops 1207959552 | bytes 2359296 | tf_op jit(solution)/shard_map/pallas_call | solution.py:398
  66.8 43.8 %all-gather.3.cloned.1.call-done = bf16[2560,3328]{1,0:T(8,128)(2,1)} async-done(((bf16[160,3328]{1,0:T(8,128)(2,1)}), bf16[2560,3328]{1,0:T(8,128)(2,1)}) %all-gather.3.cloned.1.call-update) | async-done | bytes 17039376 | tf_op jit(solution)/shard_map/all_gather | solution.py:454
  110.6 1.0 copy-done.3
  111.7 6.4 %shard_map.128 = (bf16[128,1280]{1,0:T(8,128)(2,1)S(1)}, bf16[128,640]{1,0:T(8,128)(2,1)S(1)}, bf16[128,1280]{1,0:T(8,128)(2,1)S(1)}) custom-call(bf16[128,2048]{1,0:T(8,128)(2,1)S(1)} %copy-done.3, f32[1,1280]{1,0:T(1,128)S(1)} %broadcast_in_dim.26.gain, bf16[16,160,3328]{2,1,0:T(8,128)(2,1)} %bitcast.173), custom_call_target="tpu_custom_call" | custom-call | flops 8000000000 | bytes 10000000 | tf_op jit(solution)/shard_map/pallas_call | solution.py:472
  118.1 2.2 collective-permute-start.13
  120.3 1.3 collective-permute-start.14
  121.6 1.0 slice_bitcast_fusion.4
  122.6 1.4 slice.162
  124.0 3.0 %slice.164 = bf16[16,80,2048]{2,1,0:T(8,128)(2,1)S(1)} slice(bf16[16,160,3328]{2,1,0:T(8,128)(2,1)} %bitcast.176), slice={[0:16], [80:160], [1280:3328]} | slice | bytes 10485760 | tf_op jit(solution)/shard_map/slice | solution.py:455
  127.1 5.5 %shard_map.129 = (bf16[128,1280]{1,0:T(8,128)(2,1)}, bf16[128,1280]{1,0:T(8,128)(2,1)S(1)}) custom-call(s32[4]{0:T(128)S(1)} %bitcast.166, s32[1]{0:T(128)} %bitcast.2.first, bf16[128,640]{1,0:T(8,128)(2,1)S(1)} %get-tuple-element.9.query, bf16[128,1280]{1,0:T(8,128)(2,1)S(1)} %collective-permute-done.13.left, bf16[128,1280]{1,0:T(8,128)(2,1)S(1)} %get-tuple-element.10.own, ...), custom_call_target="tpu_custom_call" | custom-call | flops 4000000000 | bytes 4000000 | tf_op jit(solution)/shard_map/pallas_call | solution.py:494
  132.7 1.0 multiply_reduce_fusion
  133.8 4.4 %collective-permute-start.19 = (bf16[128,1280]{1,0:T(8,128)(2,1)S(1)}, bf16[128,1280]{1,0:T(8,128)(2,1)S(1)}, u32[]{:S(2)}, u32[]{:S(2)}) collective-permute-start(bf16[128,1280]{1,0:T(8,128)(2,1)S(1)} %multiply_convert_fusion.1), channel_id=1, source_target_pairs={{0,4},{1,5},{2,6},{3,7},{4,8},{5,9},{6,10},{7,11},{8,12},{9,13},{1... | collective-permute-start | bytes 983048 | tf_op jit(solution)/shard_map/ppermute | solution.py:93
  138.7 8.9 %convolution_convert_fusion = bf16[1280,1536]{1,0:T(8,128)(2,1)S(1)} fusion(bf16[1280,2048]{1,0:T(8,128)(2,1)S(1)} %bitcast.168, bf16[1,2048,1536]{2,1,0:T(8,128)(2,1)S(1)} %bitcast.202, f32[2048]{0:T(1024)S(1)} %copy-done.7), kind=kOutput, calls=%fused_computation.1 | convolution fusion | flops 8064466944 | bytes 15474688 | tf_op jit(solution)/shard_map/dot_general | solution.py:492
  150.9 1.2 collective-permute-start.30
  152.2 1.3 collective-permute-start.16
  153.5 8.0 %collective-permute-done.20 = bf16[128,1280]{1,0:T(8,128)(2,1)S(1)} collective-permute-done((bf16[128,1280]{1,0:T(8,128)(2,1)S(1)}, bf16[128,1280]{1,0:T(8,128)(2,1)S(1)}, u32[]{:S(2)}, u32[]{:S(2)}) %collective-permute-start.20) | collective-permute-done | bytes 327712 | tf_op jit(solution)/shard_map/ppermute | solution.py:93
  161.5 1.5 collective-permute-start.26
  163.5 6.8 %collective-permute-done.26 = bf16[128,1280]{1,0:T(8,128)(2,1)S(1)} collective-permute-done((bf16[128,1280]{1,0:T(8,128)(2,1)S(1)}, bf16[128,1280]{1,0:T(8,128)(2,1)S(1)}, u32[]{:S(2)}, u32[]{:S(2)}) %collective-permute-start.26) | collective-permute-done | bytes 327712 | tf_op jit(solution)/shard_map/ppermute | solution.py:93
  170.7 2.2 fusion.76
  172.9 2.1 fusion.11
  175.6 1.4 collective-permute-start.22
  177.2 2.2 fusion.79
  179.4 2.0 fusion.20
  181.7 3.7 %collective-permute-done.22 = bf16[128,1280]{1,0:T(8,128)(2,1)S(1)} collective-permute-done((bf16[128,1280]{1,0:T(8,128)(2,1)S(1)}, bf16[128,1280]{1,0:T(8,128)(2,1)S(1)}, u32[]{:S(2)}, u32[]{:S(2)}) %collective-permute-start.22) | collective-permute-done | bytes 327712 | tf_op jit(solution)/shard_map/ppermute | solution.py:93
  185.7 2.2 fusion.78
  187.9 2.0 fusion.17
  190.8 2.2 fusion.77
  192.9 2.2 fusion.14
  195.9 1.5 collective-permute-start.33
  198.5 12.2 %collective-permute-done.33 = bf16[128,2048]{1,0:T(8,128)(2,1)S(1)} collective-permute-done((bf16[128,2048]{1,0:T(8,128)(2,1)S(1)}, bf16[128,2048]{1,0:T(8,128)(2,1)S(1)}, u32[]{:S(2)}, u32[]{:S(2)}) %collective-permute-start.33) | collective-permute-done | bytes 524320 | tf_op jit(solution)/shard_map/ppermute | solution.py:93
  212.0 1.2 collective-permute-start.25
  213.2 8.7 %collective-permute-done.29 = bf16[128,2048]{1,0:T(8,128)(2,1)S(1)} collective-permute-done((bf16[128,2048]{1,0:T(8,128)(2,1)S(1)}, bf16[128,2048]{1,0:T(8,128)(2,1)S(1)}, u32[]{:S(2)}, u32[]{:S(2)}) %collective-permute-start.29) | collective-permute-done | bytes 524320 | tf_op jit(solution)/shard_map/ppermute | solution.py:93
  221.9 3.8 %collective-permute-done.34 = bf16[128,2048]{1,0:T(8,128)(2,1)S(1)} collective-permute-done((bf16[128,2048]{1,0:T(8,128)(2,1)S(1)}, bf16[128,2048]{1,0:T(8,128)(2,1)S(1)}, u32[]{:S(2)}, u32[]{:S(2)}) %collective-permute-start.34) | collective-permute-done | bytes 524320 | tf_op jit(solution)/shard_map/ppermute | solution.py:93
  226.5 1.5 collective-permute-start.18
  228.0 5.2 %collective-permute-done.25 = bf16[128,2048]{1,0:T(8,128)(2,1)S(1)} collective-permute-done((bf16[128,2048]{1,0:T(8,128)(2,1)S(1)}, bf16[128,2048]{1,0:T(8,128)(2,1)S(1)}, u32[]{:S(2)}, u32[]{:S(2)}) %collective-permute-start.25) | collective-permute-done | bytes 524320 | tf_op jit(solution)/shard_map/ppermute | solution.py:93
  233.2 6.8 %collective-permute-done.35 = bf16[128,2048]{1,0:T(8,128)(2,1)S(1)} collective-permute-done((bf16[128,2048]{1,0:T(8,128)(2,1)S(1)}, bf16[128,2048]{1,0:T(8,128)(2,1)S(1)}, u32[]{:S(2)}, u32[]{:S(2)}) %collective-permute-start.35) | collective-permute-done | bytes 524320 | tf_op jit(solution)/shard_map/ppermute | solution.py:93
  240.3 3.7 %collective-permute-done.18 = bf16[128,2048]{1,0:T(8,128)(2,1)S(1)} collective-permute-done((bf16[128,2048]{1,0:T(8,128)(2,1)S(1)}, bf16[128,2048]{1,0:T(8,128)(2,1)S(1)}, u32[]{:S(2)}, u32[]{:S(2)}) %collective-permute-start.18) | collective-permute-done | bytes 524320 | tf_op jit(solution)/shard_map/ppermute | solution.py:93
  244.0 9.3 %collective-permute-done.36 = bf16[128,2048]{1,0:T(8,128)(2,1)S(1)} collective-permute-done((bf16[128,2048]{1,0:T(8,128)(2,1)S(1)}, bf16[128,2048]{1,0:T(8,128)(2,1)S(1)}, u32[]{:S(2)}, u32[]{:S(2)}) %collective-permute-start.36) | collective-permute-done | bytes 524320 | tf_op jit(solution)/shard_map/ppermute | solution.py:93
  253.3 1.1 fusion.43
  (99 shorter events, 12.1 us)
Async XLA Ops:
  6.5 166.3 %copy-start = (bf16[1,768,2048]{2,1,0:T(8,128)(2,1)S(1)}, bf16[1,768,2048]{2,1,0:T(8,128)(2,1)}, u32[]{:S(2)}) copy-start(bf16[1,768,2048]{2,1,0:T(8,128)(2,1)} %param.25) | copy-start | bytes 9437188
  6.5 4.1 %copy-start.6 = (s32[128,8]{0,1:T(8,128)S(1)}, s32[128,8]{0,1:T(8,128)}, u32[]{:S(2)}) copy-start(s32[128,8]{0,1:T(8,128)} %param.15) | copy-start | bytes 12292
  6.5 4.1 %copy-start.5 = (f32[128,8]{0,1:T(8,128)S(1)}, f32[128,8]{0,1:T(8,128)}, u32[]{:S(2)}) copy-start(f32[128,8]{0,1:T(8,128)} %param.16) | copy-start | bytes 12292
  6.5 104.1 %all-gather.3.cloned.1.call-start = ((), (), s32[]{:S(2)}) async-start(), calls=%async_computation | async-start | bytes 18104320 | tf_op jit(solution)/shard_map/all_gather | solution.py:454
  8.3 37.9 %copy-start.4 = (f32[1280]{0:T(1024)S(1)}, f32[1280]{0:T(1024)}, u32[]{:S(2)}) copy-start(f32[1280]{0:T(1024)} %param.19) | copy-start | bytes 15364
  10.7 6.7 %collective-permute-start.8 = (f32[16,128]{1,0:T(8,128)S(1)}, f32[16,128]{1,0:T(8,128)S(1)}, u32[]{:S(2)}, u32[]{:S(2)}) collective-permute-start(f32[16,128]{1,0:T(8,128)S(1)} %select_reduce_fusion), channel_id=1, source_target_pairs={{0,4},{1,5},{2,6},{3,7},{4,8},{5,9},{6,10},{7,11},{8,12},{9,13},{1... | collective-permute-start | bytes 24584 | tf_op jit(solution)/shard_map/ppermute | solution.py:93
  17.4 5.6 %collective-permute-start.9 = (f32[16,128]{1,0:T(8,128)S(1)}, f32[16,128]{1,0:T(8,128)S(1)}, u32[]{:S(2)}, u32[]{:S(2)}) collective-permute-start(f32[16,128]{1,0:T(8,128)S(1)} %collective-permute-done.8), channel_id=1, source_target_pairs={{0,4},{1,5},{2,6},{3,7},{4,8},{5,9},{6,10},{7,11},{8,12},{9,13},{1... | collective-permute-start | bytes 24584 | tf_op jit(solution)/shard_map/ppermute | solution.py:93
  23.0 6.1 %collective-permute-start.10 = (f32[16,128]{1,0:T(8,128)S(1)}, f32[16,128]{1,0:T(8,128)S(1)}, u32[]{:S(2)}, u32[]{:S(2)}) collective-permute-start(f32[16,128]{1,0:T(8,128)S(1)} %collective-permute-done.9), channel_id=1, source_target_pairs={{0,4},{1,5},{2,6},{3,7},{4,8},{5,9},{6,10},{7,11},{8,12},{9,13},{1... | collective-permute-start | bytes 24584 | tf_op jit(solution)/shard_map/ppermute | solution.py:93
  23.0 17.3 %collective-permute-start.2 = (bf16[144,256]{1,0:T(8,128)(2,1)}, bf16[144,256]{1,0:T(8,128)(2,1)}, u32[]{:S(2)}, u32[]{:S(2)}) collective-permute-start(bf16[144,256]{1,0:T(8,128)(2,1)} %param.17), channel_id=1, source_target_pairs={{0,4},{1,5},{2,6},{3,7},{4,8},{5,9},{6,10},{7,11},{8,12},{9,13},{1... | collective-permute-start | bytes 221192 | tf_op jit(solution)/shard_map/ppermute | solution.py:181
  23.0 14.9 %collective-permute-start.1 = (bf16[144,256]{1,0:T(8,128)(2,1)}, bf16[144,256]{1,0:T(8,128)(2,1)}, u32[]{:S(2)}, u32[]{:S(2)}) collective-permute-start(bf16[144,256]{1,0:T(8,128)(2,1)} %param.17), channel_id=1, source_target_pairs={{0,2},{1,3},{2,0},{3,1},{4,6},{5,7},{6,4},{7,5},{8,10},{9,11},{10,... | collective-permute-start | bytes 221192 | tf_op jit(solution)/shard_map/ppermute | solution.py:181
  24.7 16.4 %collective-permute-start.3 = (bf16[144,256]{1,0:T(8,128)(2,1)}, bf16[144,256]{1,0:T(8,128)(2,1)}, u32[]{:S(2)}, u32[]{:S(2)}) collective-permute-start(bf16[144,256]{1,0:T(8,128)(2,1)} %param.17), channel_id=1, source_target_pairs={{0,8},{1,9},{2,10},{3,11},{4,12},{5,13},{6,14},{7,15},{8,0},{9,1},... | collective-permute-start | bytes 221192 | tf_op jit(solution)/shard_map/ppermute | solution.py:181
  29.1 12.9 %collective-permute-start.4 = (bf16[144,256]{1,0:T(8,128)(2,1)}, bf16[144,256]{1,0:T(8,128)(2,1)}, u32[]{:S(2)}, u32[]{:S(2)}) collective-permute-start(bf16[144,256]{1,0:T(8,128)(2,1)} %param.17), channel_id=1, source_target_pairs={{0,12},{1,13},{2,14},{3,15},{4,0},{5,1},{6,2},{7,3},{8,4},{9,5},{1... | collective-permute-start | bytes 221192 | tf_op jit(solution)/shard_map/ppermute | solution.py:181
  29.7 4.9 %collective-permute-start.11 = (f32[4,16,128]{2,1,0:T(8,128)}, f32[4,16,128]{2,1,0:T(8,128)}, u32[]{:S(2)}, u32[]{:S(2)}) collective-permute-start(f32[4,16,128]{2,1,0:T(8,128)} %get-tuple-element.32), channel_id=1, source_target_pairs={{0,2},{1,3},{2,0},{3,1},{4,6},{5,7},{6,4},{7,5},{8,10},{9,11},{10,... | collective-permute-start | bytes 98312 | tf_op jit(solution)/shard_map/ppermute | solution.py:93
  34.6 23.2 %collective-permute-start = (bf16[1,4096]{1,0:T(2,128)(2,1)}, bf16[1,4096]{1,0:T(2,128)(2,1)}, u32[]{:S(2)}, u32[]{:S(2)}) collective-permute-start(bf16[1,4096]{1,0:T(2,128)(2,1)} %slice.122), channel_id=1, source_target_pairs={{0,1},{1,2},{2,3},{3,4},{4,5},{5,6},{6,7},{7,8},{8,9},{9,10},{10,1... | collective-permute-start | bytes 24584 | tf_op jit(solution)/shard_map/ppermute | solution.py:18
  37.9 9.2 %collective-permute-start.12 = (f32[2,4,16,128]{3,2,1,0:T(8,128)}, f32[2,4,16,128]{3,2,1,0:T(8,128)}, u32[]{:S(2)}, u32[]{:S(2)}) collective-permute-start(f32[2,4,16,128]{3,2,1,0:T(8,128)} %get-tuple-element.29), channel_id=1, source_target_pairs={{0,1},{1,0},{2,3},{3,2},{4,5},{5,4},{6,7},{7,6},{8,9},{9,8},{10,11... | collective-permute-start | bytes 196616 | tf_op jit(solution)/shard_map/ppermute | solution.py:93
  42.9 14.9 %collective-permute-start.6 = (bf16[5,144,256]{2,1,0:T(8,128)(2,1)S(1)}, bf16[5,144,256]{2,1,0:T(8,128)(2,1)}, u32[]{:S(2)}, u32[]{:S(2)}) collective-permute-start(bf16[5,144,256]{2,1,0:T(8,128)(2,1)S(1)} %constant_dynamic-update-slice_fusion.refs_0_), channel_id=1, source_target_pairs={{0,1},{1,0},{2,3},{3,2},{4,5},{5,4},{6,7},{7,6},{8,9},{9,8},{10,11... | collective-permute-start | bytes 1105928 | tf_op jit(solution)/shard_map/ppermute | solution.py:181
  44.6 13.2 %collective-permute-start.5 = (bf16[3,144,256]{2,1,0:T(8,128)(2,1)}, bf16[3,144,256]{2,1,0:T(8,128)(2,1)}, u32[]{:S(2)}, u32[]{:S(2)}) collective-permute-start(bf16[3,144,256]{2,1,0:T(8,128)(2,1)} %pad_maximum_fusion.9), channel_id=1, source_target_pairs={{0,2},{1,3},{2,0},{3,1},{4,6},{5,7},{6,4},{7,5},{8,10},{9,11},{10,... | collective-permute-start | bytes 663560 | tf_op jit(solution)/shard_map/ppermute | solution.py:181
  57.8 1.7 collective-permute-start.7
  59.5 1.6 copy-start.1
  66.0 0.8 copy-start.2
  110.6 1.0 copy-start.3
  118.1 9.0 %collective-permute-start.13 = (bf16[128,1280]{1,0:T(8,128)(2,1)S(1)}, bf16[128,1280]{1,0:T(8,128)(2,1)S(1)}, u32[]{:S(2)}, u32[]{:S(2)}) collective-permute-start(bf16[128,1280]{1,0:T(8,128)(2,1)S(1)} %get-tuple-element.10.own), channel_id=1, source_target_pairs={{0,1},{1,2},{2,3},{3,4},{4,5},{5,6},{6,7},{7,8},{8,9},{9,10},{10,1... | collective-permute-start | bytes 983048 | tf_op jit(solution)/shard_map/ppermute | solution.py:18
  120.3 6.8 %collective-permute-start.14 = (bf16[128,1280]{1,0:T(8,128)(2,1)S(1)}, bf16[128,1280]{1,0:T(8,128)(2,1)S(1)}, u32[]{:S(2)}, u32[]{:S(2)}) collective-permute-start(bf16[128,1280]{1,0:T(8,128)(2,1)S(1)} %get-tuple-element.10.own), channel_id=1, source_target_pairs={{1,0},{2,1},{3,2},{4,3},{5,4},{6,5},{7,6},{8,7},{9,8},{10,9},{11,1... | collective-permute-start | bytes 983048 | tf_op jit(solution)/shard_map/ppermute | solution.py:18
  127.0 11.7 %slice-start = ((s8[6291456]{0:T(1024)(128)(4,1)}), s8[2097152]{0:T(1024)(128)(4,1)S(1)}, s32[]{:S(2)}) async-start(s8[6291456]{0:T(1024)(128)(4,1)} %bitcast.201), calls=%async_computation.1 | async-start | bytes 4194304
  127.1 11.6 %slice-start.1 = ((s8[6291456]{0:T(1024)(128)(4,1)}), s8[4194304]{0:T(1024)(128)(4,1)S(1)}, s32[]{:S(2)}) async-start(s8[6291456]{0:T(1024)(128)(4,1)} %bitcast.201), calls=%async_computation.2 | async-start | bytes 8388608
  132.7 6.0 %copy-start.7 = (f32[2048]{0:T(1024)S(1)}, f32[2048]{0:T(1024)}, u32[]{:S(2)}) copy-start(f32[2048]{0:T(1024)} %param.23) | copy-start | bytes 24580
  133.8 16.1 %collective-permute-start.19 = (bf16[128,1280]{1,0:T(8,128)(2,1)S(1)}, bf16[128,1280]{1,0:T(8,128)(2,1)S(1)}, u32[]{:S(2)}, u32[]{:S(2)}) collective-permute-start(bf16[128,1280]{1,0:T(8,128)(2,1)S(1)} %multiply_convert_fusion.1), channel_id=1, source_target_pairs={{0,4},{1,5},{2,6},{3,7},{4,8},{5,9},{6,10},{7,11},{8,12},{9,13},{1... | collective-permute-start | bytes 983048 | tf_op jit(solution)/shard_map/ppermute | solution.py:93
  138.2 10.6 %collective-permute-start.15 = (bf16[128,1280]{1,0:T(8,128)(2,1)S(1)}, bf16[128,1280]{1,0:T(8,128)(2,1)S(1)}, u32[]{:S(2)}, u32[]{:S(2)}) collective-permute-start(bf16[128,1280]{1,0:T(8,128)(2,1)S(1)} %multiply_convert_fusion.1), channel_id=1, source_target_pairs={{0,2},{1,3},{2,0},{3,1},{4,6},{5,7},{6,4},{7,5},{8,10},{9,11},{10,... | collective-permute-start | bytes 983048 | tf_op jit(solution)/shard_map/ppermute | solution.py:93
  150.0 11.5 %collective-permute-start.20 = (bf16[128,1280]{1,0:T(8,128)(2,1)S(1)}, bf16[128,1280]{1,0:T(8,128)(2,1)S(1)}, u32[]{:S(2)}, u32[]{:S(2)}) collective-permute-start(bf16[128,1280]{1,0:T(8,128)(2,1)S(1)} %add_convert_fusion), channel_id=1, source_target_pairs={{0,4},{1,5},{2,6},{3,7},{4,8},{5,9},{6,10},{7,11},{8,12},{9,13},{1... | collective-permute-start | bytes 983048 | tf_op jit(solution)/shard_map/ppermute | solution.py:93
  150.9 12.1 %collective-permute-start.30 = (bf16[128,1280]{1,0:T(8,128)(2,1)S(1)}, bf16[128,1280]{1,0:T(8,128)(2,1)S(1)}, u32[]{:S(2)}, u32[]{:S(2)}) collective-permute-start(bf16[128,1280]{1,0:T(8,128)(2,1)S(1)} %collective-permute-done.19), channel_id=1, source_target_pairs={{0,2},{1,3},{2,0},{3,1},{4,6},{5,7},{6,4},{7,5},{8,10},{9,11},{10,... | collective-permute-start | bytes 983048 | tf_op jit(solution)/shard_map/ppermute | solution.py:93
  152.2 18.4 %collective-permute-start.16 = (bf16[2,128,1280]{2,1,0:T(8,128)(2,1)S(1)}, bf16[2,128,1280]{2,1,0:T(8,128)(2,1)S(1)}, u32[]{:S(2)}, u32[]{:S(2)}) collective-permute-start(bf16[2,128,1280]{2,1,0:T(8,128)(2,1)S(1)} %get-tuple-element.28), channel_id=1, source_target_pairs={{0,1},{1,0},{2,3},{3,2},{4,5},{5,4},{6,7},{7,6},{8,9},{9,8},{10,11... | collective-permute-start | bytes 1966088 | tf_op jit(solution)/shard_map/ppermute | solution.py:93
  161.5 8.8 %collective-permute-start.26 = (bf16[128,1280]{1,0:T(8,128)(2,1)S(1)}, bf16[128,1280]{1,0:T(8,128)(2,1)S(1)}, u32[]{:S(2)}, u32[]{:S(2)}) collective-permute-start(bf16[128,1280]{1,0:T(8,128)(2,1)S(1)} %collective-permute-done.20), channel_id=1, source_target_pairs={{0,2},{1,3},{2,0},{3,1},{4,6},{5,7},{6,4},{7,5},{8,10},{9,11},{10,... | collective-permute-start | bytes 983048 | tf_op jit(solution)/shard_map/ppermute | solution.py:93
  163.1 14.0 %collective-permute-start.31 = (bf16[2,128,1280]{2,1,0:T(8,128)(2,1)S(1)}, bf16[2,128,1280]{2,1,0:T(8,128)(2,1)S(1)}, u32[]{:S(2)}, u32[]{:S(2)}) collective-permute-start(bf16[2,128,1280]{2,1,0:T(8,128)(2,1)S(1)} %get-tuple-element.22), channel_id=1, source_target_pairs={{0,1},{1,0},{2,3},{3,2},{4,5},{5,4},{6,7},{7,6},{8,9},{9,8},{10,11... | collective-permute-start | bytes 1966088 | tf_op jit(solution)/shard_map/ppermute | solution.py:93
  163.2 12.4 %collective-permute-start.21 = (bf16[128,1280]{1,0:T(8,128)(2,1)S(1)}, bf16[128,1280]{1,0:T(8,128)(2,1)S(1)}, u32[]{:S(2)}, u32[]{:S(2)}) collective-permute-start(bf16[128,1280]{1,0:T(8,128)(2,1)S(1)} %collective-permute-done.20), channel_id=1, source_target_pairs={{0,4},{1,5},{2,6},{3,7},{4,8},{5,9},{6,10},{7,11},{8,12},{9,13},{1... | collective-permute-start | bytes 983048 | tf_op jit(solution)/shard_map/ppermute | solution.py:93
  170.5 15.1 %collective-permute-start.27 = (bf16[2,128,1280]{2,1,0:T(8,128)(2,1)S(1)}, bf16[2,128,1280]{2,1,0:T(8,128)(2,1)S(1)}, u32[]{:S(2)}, u32[]{:S(2)}) collective-permute-start(bf16[2,128,1280]{2,1,0:T(8,128)(2,1)S(1)} %get-tuple-element.24), channel_id=1, source_target_pairs={{0,1},{1,0},{2,3},{3,2},{4,5},{5,4},{6,7},{7,6},{8,9},{9,8},{10,11... | collective-permute-start | bytes 1966088 | tf_op jit(solution)/shard_map/ppermute | solution.py:93
  175.1 51.0 %collective-permute-start.17 = (bf16[2,128,2048]{2,1,0:T(8,128)(2,1)S(1)}, bf16[2,128,2048]{2,1,0:T(8,128)(2,1)S(1)}, u32[]{:S(2)}, u32[]{:S(2)}) collective-permute-start(bf16[2,128,2048]{2,1,0:T(8,128)(2,1)S(1)} %bitcast.182), channel_id=1, source_target_pairs={{0,1},{1,0},{2,3},{3,2},{4,5},{5,4},{6,7},{7,6},{8,9},{9,8},{10,11... | collective-permute-start | bytes 3145736 | tf_op jit(solution)/shard_map/ppermute | solution.py:93
  175.6 9.7 %collective-permute-start.22 = (bf16[128,1280]{1,0:T(8,128)(2,1)S(1)}, bf16[128,1280]{1,0:T(8,128)(2,1)S(1)}, u32[]{:S(2)}, u32[]{:S(2)}) collective-permute-start(bf16[128,1280]{1,0:T(8,128)(2,1)S(1)} %collective-permute-done.21), channel_id=1, source_target_pairs={{0,2},{1,3},{2,0},{3,1},{4,6},{5,7},{6,4},{7,5},{8,10},{9,11},{10,... | collective-permute-start | bytes 983048 | tf_op jit(solution)/shard_map/ppermute | solution.py:93
  181.6 13.9 %collective-permute-start.32 = (bf16[2,128,2048]{2,1,0:T(8,128)(2,1)S(1)}, bf16[2,128,2048]{2,1,0:T(8,128)(2,1)S(1)}, u32[]{:S(2)}, u32[]{:S(2)}) collective-permute-start(bf16[2,128,2048]{2,1,0:T(8,128)(2,1)S(1)} %bitcast.183), channel_id=1, source_target_pairs={{0,1},{1,0},{2,3},{3,2},{4,5},{5,4},{6,7},{7,6},{8,9},{9,8},{10,11... | collective-permute-start | bytes 3145736 | tf_op jit(solution)/shard_map/ppermute | solution.py:93
  185.4 5.2 %collective-permute-start.23 = (bf16[2,128,1280]{2,1,0:T(8,128)(2,1)S(1)}, bf16[2,128,1280]{2,1,0:T(8,128)(2,1)S(1)}, u32[]{:S(2)}, u32[]{:S(2)}) collective-permute-start(bf16[2,128,1280]{2,1,0:T(8,128)(2,1)S(1)} %get-tuple-element.26), channel_id=1, source_target_pairs={{0,1},{1,0},{2,3},{3,2},{4,5},{5,4},{6,7},{7,6},{8,9},{9,8},{10,11... | collective-permute-start | bytes 1966088 | tf_op jit(solution)/shard_map/ppermute | solution.py:93
  190.1 7.3 %collective-permute-start.28 = (bf16[2,128,2048]{2,1,0:T(8,128)(2,1)S(1)}, bf16[2,128,2048]{2,1,0:T(8,128)(2,1)S(1)}, u32[]{:S(2)}, u32[]{:S(2)}) collective-permute-start(bf16[2,128,2048]{2,1,0:T(8,128)(2,1)S(1)} %bitcast.185), channel_id=1, source_target_pairs={{0,1},{1,0},{2,3},{3,2},{4,5},{5,4},{6,7},{7,6},{8,9},{9,8},{10,11... | collective-permute-start | bytes 3145736 | tf_op jit(solution)/shard_map/ppermute | solution.py:93
  195.4 16.2 %collective-permute-start.24 = (bf16[2,128,2048]{2,1,0:T(8,128)(2,1)S(1)}, bf16[2,128,2048]{2,1,0:T(8,128)(2,1)S(1)}, u32[]{:S(2)}, u32[]{:S(2)}) collective-permute-start(bf16[2,128,2048]{2,1,0:T(8,128)(2,1)S(1)} %bitcast.184), channel_id=1, source_target_pairs={{0,1},{1,0},{2,3},{3,2},{4,5},{5,4},{6,7},{7,6},{8,9},{9,8},{10,11... | collective-permute-start | bytes 3145736 | tf_op jit(solution)/shard_map/ppermute | solution.py:93
  195.9 14.8 %collective-permute-start.33 = (bf16[128,2048]{1,0:T(8,128)(2,1)S(1)}, bf16[128,2048]{1,0:T(8,128)(2,1)S(1)}, u32[]{:S(2)}, u32[]{:S(2)}) collective-permute-start(bf16[128,2048]{1,0:T(8,128)(2,1)S(1)} %fusion.59), channel_id=1, source_target_pairs={{0,2},{1,3},{2,0},{3,1},{4,6},{5,7},{6,4},{7,5},{8,10},{9,11},{10,... | collective-permute-start | bytes 1572872 | tf_op jit(solution)/shard_map/ppermute | solution.py:93
  197.8 24.1 %collective-permute-start.29 = (bf16[128,2048]{1,0:T(8,128)(2,1)S(1)}, bf16[128,2048]{1,0:T(8,128)(2,1)S(1)}, u32[]{:S(2)}, u32[]{:S(2)}) collective-permute-start(bf16[128,2048]{1,0:T(8,128)(2,1)S(1)} %fusion.58), channel_id=1, source_target_pairs={{0,2},{1,3},{2,0},{3,1},{4,6},{5,7},{6,4},{7,5},{8,10},{9,11},{10,... | collective-permute-start | bytes 1572872 | tf_op jit(solution)/shard_map/ppermute | solution.py:93
  210.8 15.0 %collective-permute-start.34 = (bf16[128,2048]{1,0:T(8,128)(2,1)S(1)}, bf16[128,2048]{1,0:T(8,128)(2,1)S(1)}, u32[]{:S(2)}, u32[]{:S(2)}) collective-permute-start(bf16[128,2048]{1,0:T(8,128)(2,1)S(1)} %fusion.33), channel_id=1, source_target_pairs={{0,4},{1,5},{2,6},{3,7},{4,8},{5,9},{6,10},{7,11},{8,12},{9,13},{1... | collective-permute-start | bytes 1572872 | tf_op jit(solution)/shard_map/ppermute | solution.py:93
  212.0 21.1 %collective-permute-start.25 = (bf16[128,2048]{1,0:T(8,128)(2,1)S(1)}, bf16[128,2048]{1,0:T(8,128)(2,1)S(1)}, u32[]{:S(2)}, u32[]{:S(2)}) collective-permute-start(bf16[128,2048]{1,0:T(8,128)(2,1)S(1)} %fusion.57), channel_id=1, source_target_pairs={{0,2},{1,3},{2,0},{3,1},{4,6},{5,7},{6,4},{7,5},{8,10},{9,11},{10,... | collective-permute-start | bytes 1572872 | tf_op jit(solution)/shard_map/ppermute | solution.py:93
  226.0 14.0 %collective-permute-start.35 = (bf16[128,2048]{1,0:T(8,128)(2,1)S(1)}, bf16[128,2048]{1,0:T(8,128)(2,1)S(1)}, u32[]{:S(2)}, u32[]{:S(2)}) collective-permute-start(bf16[128,2048]{1,0:T(8,128)(2,1)S(1)} %fusion.36), channel_id=1, source_target_pairs={{0,4},{1,5},{2,6},{3,7},{4,8},{5,9},{6,10},{7,11},{8,12},{9,13},{1... | collective-permute-start | bytes 1572872 | tf_op jit(solution)/shard_map/ppermute | solution.py:93
  226.5 17.5 %collective-permute-start.18 = (bf16[128,2048]{1,0:T(8,128)(2,1)S(1)}, bf16[128,2048]{1,0:T(8,128)(2,1)S(1)}, u32[]{:S(2)}, u32[]{:S(2)}) collective-permute-start(bf16[128,2048]{1,0:T(8,128)(2,1)S(1)} %fusion.56), channel_id=1, source_target_pairs={{0,2},{1,3},{2,0},{3,1},{4,6},{5,7},{6,4},{7,5},{8,10},{9,11},{10,... | collective-permute-start | bytes 1572872 | tf_op jit(solution)/shard_map/ppermute | solution.py:93
  240.2 13.1 %collective-permute-start.36 = (bf16[128,2048]{1,0:T(8,128)(2,1)S(1)}, bf16[128,2048]{1,0:T(8,128)(2,1)S(1)}, u32[]{:S(2)}, u32[]{:S(2)}) collective-permute-start(bf16[128,2048]{1,0:T(8,128)(2,1)S(1)} %fusion.39), channel_id=1, source_target_pairs={{0,4},{1,5},{2,6},{3,7},{4,8},{5,9},{6,10},{7,11},{8,12},{9,13},{1... | collective-permute-start | bytes 1572872 | tf_op jit(solution)/shard_map/ppermute | solution.py:93
Sparse Core Ops, SparseCore 0:
  10.7 99.8 all-gather.2

commit v3 on v2

--- a/solution.py
+++ b/solution.py
@@ -149,7 +149,7 @@
         return jnp.stack([pair, ring_step(pair, 1, cores)])
 
     theirs = None
-    for k in [*range(1, zs), 0]:
+    for k in range(zs):
         rows = send(k).reshape(-1, scaled.shape[1])
         weight = gates[k][:, None]
         both = jnp.dot(rows, fused, preferred_element_type=jnp.float32)

time: 262 us -> 262 us (level)
  no operation moved by 1% of the time
where the time goes in v3:
time: 262 us; the launch traced here: 261 us
  waiting for transfers between devices  134 us (51%)
  starting transfers between devices  37.4 us (14%)
  matrix products  26.9 us (10%)
  local copies, waits for them, and re-layouts  18.5 us (7%)
  Pallas kernels  16.9 us (6%)
  between operations  15.2 us (6%)
  other arithmetic  12 us (5%)
    ppermute x27, waiting for transfers between devices, ring_step(): return lax.ppermute(block, 'seq', route)  78.9 us
    all_gather x1, waiting for transfers between devices, dense_device(): late_full = lax.all_gather(packed, 'seq', axis=0)  43.8 us
    ppermute x27, starting transfers between devices, ring_step(): return lax.ppermute(block, 'seq', route)  24.4 us
    ppermute x7, waiting for transfers between devices, hop(): return lax.ppermute(block, 'seq', route)  11.6 us
    dot_general x1, matrix products, dense_device(): fused = jnp.dot(audio_full, weighted, preferred_element_type=jnp.float32)  8.87 us
    dot_general x4, matrix products, dense_experts(): both = jnp.dot(rows, fused, preferred_element_type=jnp.float32)  8.77 us
    dot_general x4, matrix products, dense_experts(): jnp.dot(hidden, down, preferred_element_type=jnp.float32)  8.31 us
    ppermute x7, starting transfers between devices, hop(): return lax.ppermute(block, 'seq', route)  7.68 us
  transfers between devices with their start and end apart: 38, of which 16 were waited for; matrix products, arithmetic and copies ran while one was open for 18% of the time, Pallas kernels for 2%

profile of v3, /device:TPU:0, one launch (start us, length us, event | category | flops | bytes accessed | tf_op | source)
XLA Modules:
  0.0 261.2 jit_solution(15311847794139223090)
XLA Ops:
  6.5 1.0 slice.127
  8.3 2.3 maximum_maximum_fusion
  10.7 3.1 %collective-permute-start.8 = (f32[16,128]{1,0:T(8,128)S(1)}, f32[16,128]{1,0:T(8,128)S(1)}, u32[]{:S(2)}, u32[]{:S(2)}) collective-permute-start(f32[16,128]{1,0:T(8,128)S(1)} %select_reduce_fusion), channel_id=1, source_target_pairs={{0,4},{1,5},{2,6},{3,7},{4,8},{5,9},{6,10},{7,11},{8,12},{9,13},{1... | collective-permute-start | bytes 24584 | tf_op jit(solution)/shard_map/ppermute | solution.py:93
  13.7 3.7 %collective-permute-done.8 = f32[16,128]{1,0:T(8,128)S(1)} collective-permute-done((f32[16,128]{1,0:T(8,128)S(1)}, f32[16,128]{1,0:T(8,128)S(1)}, u32[]{:S(2)}, u32[]{:S(2)}) %collective-permute-start.8) | collective-permute-done | bytes 8224 | tf_op jit(solution)/shard_map/ppermute | solution.py:93
  17.4 5.6 %collective-permute-done.9 = f32[16,128]{1,0:T(8,128)S(1)} collective-permute-done((f32[16,128]{1,0:T(8,128)S(1)}, f32[16,128]{1,0:T(8,128)S(1)}, u32[]{:S(2)}, u32[]{:S(2)}) %collective-permute-start.9) | collective-permute-done | bytes 8224 | tf_op jit(solution)/shard_map/ppermute | solution.py:93
  23.0 1.7 collective-permute-start.1
  24.7 4.4 %collective-permute-start.3 = (bf16[144,256]{1,0:T(8,128)(2,1)}, bf16[144,256]{1,0:T(8,128)(2,1)}, u32[]{:S(2)}, u32[]{:S(2)}) collective-permute-start(bf16[144,256]{1,0:T(8,128)(2,1)} %param.17), channel_id=1, source_target_pairs={{0,8},{1,9},{2,10},{3,11},{4,12},{5,13},{6,14},{7,15},{8,0},{9,1},... | collective-permute-start | bytes 221192 | tf_op jit(solution)/shard_map/ppermute | solution.py:181
  29.7 1.3 collective-permute-start.11
  31.0 0.9 bitcast_dynamic-update-slice_fusion.1
  31.9 1.5 slice.122
  33.3 1.3 collective-permute-done.11
  34.6 1.9 collective-permute-start
  36.5 1.4 pad_maximum_fusion.10
  37.9 1.4 collective-permute-start.12
  39.3 0.9 bitcast_dynamic-update-slice_fusion
  40.2 0.9 constant_dynamic-update-slice_fusion.2
  41.1 0.9 constant_dynamic-update-slice_fusion.1
  42.0 0.9 constant_dynamic-update-slice_fusion.refs_0_
  42.9 1.7 pad_maximum_fusion.9
  44.6 1.5 collective-permute-start.5
  46.2 0.8 reduce-window.9
  47.1 0.8 fusion.60
  47.9 9.9 %collective-permute-done.5.refs_1_ = bf16[3,144,256]{2,1,0:T(8,128)(2,1)} collective-permute-done((bf16[3,144,256]{2,1,0:T(8,128)(2,1)}, bf16[3,144,256]{2,1,0:T(8,128)(2,1)}, u32[]{:S(2)}, u32[]{:S(2)}) %collective-permute-start.5) | collective-permute-done | bytes 221216 | tf_op jit(solution)/shard_map/ppermute | solution.py:181
  57.8 1.7 collective-permute-done.7.refs_3_
  59.5 1.6 copy-done.1
  61.1 4.9 %shard_map.127.act = bf16[128,2048]{1,0:T(8,128)(2,1)S(1)} custom-call(s32[4]{0:T(128)S(1)} %pad_add_fusion.place, bf16[256,4096]{1,0:T(8,128)(2,1)S(1)} %copy-done.1, bf16[1,4096]{1,0:T(2,128)(2,1)} %collective-permute-done.rim, bf16[5,144,256]{2,1,0:T(8,128)(2,1)S(1)} %constant_dynamic-update-slice_fusion.refs_0_, ...), custom_call_target="tpu_custom_call" | custom-call | flops 1207959552 | bytes 2359296 | tf_op jit(solution)/shard_map/pallas_call | solution.py:398
  66.8 43.8 %all-gather.3.cloned.1.call-done = bf16[2560,3328]{1,0:T(8,128)(2,1)} async-done(((bf16[160,3328]{1,0:T(8,128)(2,1)}), bf16[2560,3328]{1,0:T(8,128)(2,1)}) %all-gather.3.cloned.1.call-update) | async-done | bytes 17039376 | tf_op jit(solution)/shard_map/all_gather | solution.py:454
  110.6 1.0 copy-done.3
  111.7 6.4 %shard_map.128 = (bf16[128,1280]{1,0:T(8,128)(2,1)S(1)}, bf16[128,640]{1,0:T(8,128)(2,1)S(1)}, bf16[128,1280]{1,0:T(8,128)(2,1)S(1)}) custom-call(bf16[128,2048]{1,0:T(8,128)(2,1)S(1)} %copy-done.3, f32[1,1280]{1,0:T(1,128)S(1)} %broadcast_in_dim.26.gain, bf16[16,160,3328]{2,1,0:T(8,128)(2,1)} %bitcast.173), custom_call_target="tpu_custom_call" | custom-call | flops 8000000000 | bytes 10000000 | tf_op jit(solution)/shard_map/pallas_call | solution.py:472
  118.1 2.2 collective-permute-start.13
  120.3 1.3 collective-permute-start.14
  121.6 1.0 slice_bitcast_fusion.4
  122.6 1.4 slice.162
  124.0 3.0 %slice.164 = bf16[16,80,2048]{2,1,0:T(8,128)(2,1)S(1)} slice(bf16[16,160,3328]{2,1,0:T(8,128)(2,1)} %bitcast.176), slice={[0:16], [80:160], [1280:3328]} | slice | bytes 10485760 | tf_op jit(solution)/shard_map/slice | solution.py:455
  127.1 5.5 %shard_map.129 = (bf16[128,1280]{1,0:T(8,128)(2,1)}, bf16[128,1280]{1,0:T(8,128)(2,1)S(1)}) custom-call(s32[4]{0:T(128)S(1)} %bitcast.166, s32[1]{0:T(128)} %bitcast.2.first, bf16[128,640]{1,0:T(8,128)(2,1)S(1)} %get-tuple-element.9.query, bf16[128,1280]{1,0:T(8,128)(2,1)S(1)} %collective-permute-done.13.left, bf16[128,1280]{1,0:T(8,128)(2,1)S(1)} %get-tuple-element.10.own, ...), custom_call_target="tpu_custom_call" | custom-call | flops 4000000000 | bytes 4000000 | tf_op jit(solution)/shard_map/pallas_call | solution.py:494
  132.7 1.0 multiply_reduce_fusion
  133.8 4.4 %collective-permute-start.19 = (bf16[128,1280]{1,0:T(8,128)(2,1)S(1)}, bf16[128,1280]{1,0:T(8,128)(2,1)S(1)}, u32[]{:S(2)}, u32[]{:S(2)}) collective-permute-start(bf16[128,1280]{1,0:T(8,128)(2,1)S(1)} %multiply_convert_fusion.1), channel_id=1, source_target_pairs={{0,4},{1,5},{2,6},{3,7},{4,8},{5,9},{6,10},{7,11},{8,12},{9,13},{1... | collective-permute-start | bytes 983048 | tf_op jit(solution)/shard_map/ppermute | solution.py:93
  138.7 8.9 %convolution_convert_fusion = bf16[1280,1536]{1,0:T(8,128)(2,1)S(1)} fusion(bf16[1280,2048]{1,0:T(8,128)(2,1)S(1)} %bitcast.168, bf16[1,2048,1536]{2,1,0:T(8,128)(2,1)S(1)} %bitcast.202, f32[2048]{0:T(1024)S(1)} %copy-done.7), kind=kOutput, calls=%fused_computation.1 | convolution fusion | flops 8064466944 | bytes 15474688 | tf_op jit(solution)/shard_map/dot_general | solution.py:492
  150.9 1.2 collective-permute-start.30
  152.2 1.3 collective-permute-start.16
  153.5 8.0 %collective-permute-done.20 = bf16[128,1280]{1,0:T(8,128)(2,1)S(1)} collective-permute-done((bf16[128,1280]{1,0:T(8,128)(2,1)S(1)}, bf16[128,1280]{1,0:T(8,128)(2,1)S(1)}, u32[]{:S(2)}, u32[]{:S(2)}) %collective-permute-start.20) | collective-permute-done | bytes 327712 | tf_op jit(solution)/shard_map/ppermute | solution.py:93
  161.5 1.5 collective-permute-start.26
  163.5 6.8 %collective-permute-done.26 = bf16[128,1280]{1,0:T(8,128)(2,1)S(1)} collective-permute-done((bf16[128,1280]{1,0:T(8,128)(2,1)S(1)}, bf16[128,1280]{1,0:T(8,128)(2,1)S(1)}, u32[]{:S(2)}, u32[]{:S(2)}) %collective-permute-start.26) | collective-permute-done | bytes 327712 | tf_op jit(solution)/shard_map/ppermute | solution.py:93
  170.7 2.2 fusion.76
  172.9 2.1 fusion.11
  175.6 1.4 collective-permute-start.22
  177.2 2.2 fusion.79
  179.4 2.0 fusion.20
  181.7 3.7 %collective-permute-done.22 = bf16[128,1280]{1,0:T(8,128)(2,1)S(1)} collective-permute-done((bf16[128,1280]{1,0:T(8,128)(2,1)S(1)}, bf16[128,1280]{1,0:T(8,128)(2,1)S(1)}, u32[]{:S(2)}, u32[]{:S(2)}) %collective-permute-start.22) | collective-permute-done | bytes 327712 | tf_op jit(solution)/shard_map/ppermute | solution.py:93
  185.7 2.2 fusion.78
  187.9 2.0 fusion.17
  190.8 2.2 fusion.77
  192.9 2.2 fusion.14
  195.9 1.5 collective-permute-start.33
  198.5 12.2 %collective-permute-done.33 = bf16[128,2048]{1,0:T(8,128)(2,1)S(1)} collective-permute-done((bf16[128,2048]{1,0:T(8,128)(2,1)S(1)}, bf16[128,2048]{1,0:T(8,128)(2,1)S(1)}, u32[]{:S(2)}, u32[]{:S(2)}) %collective-permute-start.33) | collective-permute-done | bytes 524320 | tf_op jit(solution)/shard_map/ppermute | solution.py:93
  212.0 1.2 collective-permute-start.25
  213.2 8.7 %collective-permute-done.29 = bf16[128,2048]{1,0:T(8,128)(2,1)S(1)} collective-permute-done((bf16[128,2048]{1,0:T(8,128)(2,1)S(1)}, bf16[128,2048]{1,0:T(8,128)(2,1)S(1)}, u32[]{:S(2)}, u32[]{:S(2)}) %collective-permute-start.29) | collective-permute-done | bytes 524320 | tf_op jit(solution)/shard_map/ppermute | solution.py:93
  221.9 3.8 %collective-permute-done.34 = bf16[128,2048]{1,0:T(8,128)(2,1)S(1)} collective-permute-done((bf16[128,2048]{1,0:T(8,128)(2,1)S(1)}, bf16[128,2048]{1,0:T(8,128)(2,1)S(1)}, u32[]{:S(2)}, u32[]{:S(2)}) %collective-permute-start.34) | collective-permute-done | bytes 524320 | tf_op jit(solution)/shard_map/ppermute | solution.py:93
  226.5 1.5 collective-permute-start.18
  228.0 5.2 %collective-permute-done.25 = bf16[128,2048]{1,0:T(8,128)(2,1)S(1)} collective-permute-done((bf16[128,2048]{1,0:T(8,128)(2,1)S(1)}, bf16[128,2048]{1,0:T(8,128)(2,1)S(1)}, u32[]{:S(2)}, u32[]{:S(2)}) %collective-permute-start.25) | collective-permute-done | bytes 524320 | tf_op jit(solution)/shard_map/ppermute | solution.py:93
  233.2 6.8 %collective-permute-done.35 = bf16[128,2048]{1,0:T(8,128)(2,1)S(1)} collective-permute-done((bf16[128,2048]{1,0:T(8,128)(2,1)S(1)}, bf16[128,2048]{1,0:T(8,128)(2,1)S(1)}, u32[]{:S(2)}, u32[]{:S(2)}) %collective-permute-start.35) | collective-permute-done | bytes 524320 | tf_op jit(solution)/shard_map/ppermute | solution.py:93
  240.3 3.7 %collective-permute-done.18 = bf16[128,2048]{1,0:T(8,128)(2,1)S(1)} collective-permute-done((bf16[128,2048]{1,0:T(8,128)(2,1)S(1)}, bf16[128,2048]{1,0:T(8,128)(2,1)S(1)}, u32[]{:S(2)}, u32[]{:S(2)}) %collective-permute-start.18) | collective-permute-done | bytes 524320 | tf_op jit(solution)/shard_map/ppermute | solution.py:93
  244.0 9.3 %collective-permute-done.36 = bf16[128,2048]{1,0:T(8,128)(2,1)S(1)} collective-permute-done((bf16[128,2048]{1,0:T(8,128)(2,1)S(1)}, bf16[128,2048]{1,0:T(8,128)(2,1)S(1)}, u32[]{:S(2)}, u32[]{:S(2)}) %collective-permute-start.36) | collective-permute-done | bytes 524320 | tf_op jit(solution)/shard_map/ppermute | solution.py:93
  253.3 1.1 fusion.43
  (99 shorter events, 12.1 us)
Async XLA Ops:
  6.5 166.3 %copy-start = (bf16[1,768,2048]{2,1,0:T(8,128)(2,1)S(1)}, bf16[1,768,2048]{2,1,0:T(8,128)(2,1)}, u32[]{:S(2)}) copy-start(bf16[1,768,2048]{2,1,0:T(8,128)(2,1)} %param.25) | copy-start | bytes 9437188
  6.5 4.1 %copy-start.6 = (s32[128,8]{0,1:T(8,128)S(1)}, s32[128,8]{0,1:T(8,128)}, u32[]{:S(2)}) copy-start(s32[128,8]{0,1:T(8,128)} %param.15) | copy-start | bytes 12292
  6.5 4.1 %copy-start.5 = (f32[128,8]{0,1:T(8,128)S(1)}, f32[128,8]{0,1:T(8,128)}, u32[]{:S(2)}) copy-start(f32[128,8]{0,1:T(8,128)} %param.16) | copy-start | bytes 12292
  6.5 104.1 %all-gather.3.cloned.1.call-start = ((), (), s32[]{:S(2)}) async-start(), calls=%async_computation | async-start | bytes 18104320 | tf_op jit(solution)/shard_map/all_gather | solution.py:454
  8.3 37.9 %copy-start.4 = (f32[1280]{0:T(1024)S(1)}, f32[1280]{0:T(1024)}, u32[]{:S(2)}) copy-start(f32[1280]{0:T(1024)} %param.19) | copy-start | bytes 15364
  10.7 6.7 %collective-permute-start.8 = (f32[16,128]{1,0:T(8,128)S(1)}, f32[16,128]{1,0:T(8,128)S(1)}, u32[]{:S(2)}, u32[]{:S(2)}) collective-permute-start(f32[16,128]{1,0:T(8,128)S(1)} %select_reduce_fusion), channel_id=1, source_target_pairs={{0,4},{1,5},{2,6},{3,7},{4,8},{5,9},{6,10},{7,11},{8,12},{9,13},{1... | collective-permute-start | bytes 24584 | tf_op jit(solution)/shard_map/ppermute | solution.py:93
  17.4 5.6 %collective-permute-start.9 = (f32[16,128]{1,0:T(8,128)S(1)}, f32[16,128]{1,0:T(8,128)S(1)}, u32[]{:S(2)}, u32[]{:S(2)}) collective-permute-start(f32[16,128]{1,0:T(8,128)S(1)} %collective-permute-done.8), channel_id=1, source_target_pairs={{0,4},{1,5},{2,6},{3,7},{4,8},{5,9},{6,10},{7,11},{8,12},{9,13},{1... | collective-permute-start | bytes 24584 | tf_op jit(solution)/shard_map/ppermute | solution.py:93
  23.0 6.1 %collective-permute-start.10 = (f32[16,128]{1,0:T(8,128)S(1)}, f32[16,128]{1,0:T(8,128)S(1)}, u32[]{:S(2)}, u32[]{:S(2)}) collective-permute-start(f32[16,128]{1,0:T(8,128)S(1)} %collective-permute-done.9), channel_id=1, source_target_pairs={{0,4},{1,5},{2,6},{3,7},{4,8},{5,9},{6,10},{7,11},{8,12},{9,13},{1... | collective-permute-start | bytes 24584 | tf_op jit(solution)/shard_map/ppermute | solution.py:93
  23.0 17.3 %collective-permute-start.2 = (bf16[144,256]{1,0:T(8,128)(2,1)}, bf16[144,256]{1,0:T(8,128)(2,1)}, u32[]{:S(2)}, u32[]{:S(2)}) collective-permute-start(bf16[144,256]{1,0:T(8,128)(2,1)} %param.17), channel_id=1, source_target_pairs={{0,4},{1,5},{2,6},{3,7},{4,8},{5,9},{6,10},{7,11},{8,12},{9,13},{1... | collective-permute-start | bytes 221192 | tf_op jit(solution)/shard_map/ppermute | solution.py:181
  23.0 14.9 %collective-permute-start.1 = (bf16[144,256]{1,0:T(8,128)(2,1)}, bf16[144,256]{1,0:T(8,128)(2,1)}, u32[]{:S(2)}, u32[]{:S(2)}) collective-permute-start(bf16[144,256]{1,0:T(8,128)(2,1)} %param.17), channel_id=1, source_target_pairs={{0,2},{1,3},{2,0},{3,1},{4,6},{5,7},{6,4},{7,5},{8,10},{9,11},{10,... | collective-permute-start | bytes 221192 | tf_op jit(solution)/shard_map/ppermute | solution.py:181
  24.7 16.4 %collective-permute-start.3 = (bf16[144,256]{1,0:T(8,128)(2,1)}, bf16[144,256]{1,0:T(8,128)(2,1)}, u32[]{:S(2)}, u32[]{:S(2)}) collective-permute-start(bf16[144,256]{1,0:T(8,128)(2,1)} %param.17), channel_id=1, source_target_pairs={{0,8},{1,9},{2,10},{3,11},{4,12},{5,13},{6,14},{7,15},{8,0},{9,1},... | collective-permute-start | bytes 221192 | tf_op jit(solution)/shard_map/ppermute | solution.py:181
  29.1 12.9 %collective-permute-start.4 = (bf16[144,256]{1,0:T(8,128)(2,1)}, bf16[144,256]{1,0:T(8,128)(2,1)}, u32[]{:S(2)}, u32[]{:S(2)}) collective-permute-start(bf16[144,256]{1,0:T(8,128)(2,1)} %param.17), channel_id=1, source_target_pairs={{0,12},{1,13},{2,14},{3,15},{4,0},{5,1},{6,2},{7,3},{8,4},{9,5},{1... | collective-permute-start | bytes 221192 | tf_op jit(solution)/shard_map/ppermute | solution.py:181
  29.7 4.9 %collective-permute-start.11 = (f32[4,16,128]{2,1,0:T(8,128)}, f32[4,16,128]{2,1,0:T(8,128)}, u32[]{:S(2)}, u32[]{:S(2)}) collective-permute-start(f32[4,16,128]{2,1,0:T(8,128)} %get-tuple-element.32), channel_id=1, source_target_pairs={{0,2},{1,3},{2,0},{3,1},{4,6},{5,7},{6,4},{7,5},{8,10},{9,11},{10,... | collective-permute-start | bytes 98312 | tf_op jit(solution)/shard_map/ppermute | solution.py:93
  34.6 23.2 %collective-permute-start = (bf16[1,4096]{1,0:T(2,128)(2,1)}, bf16[1,4096]{1,0:T(2,128)(2,1)}, u32[]{:S(2)}, u32[]{:S(2)}) collective-permute-start(bf16[1,4096]{1,0:T(2,128)(2,1)} %slice.122), channel_id=1, source_target_pairs={{0,1},{1,2},{2,3},{3,4},{4,5},{5,6},{6,7},{7,8},{8,9},{9,10},{10,1... | collective-permute-start | bytes 24584 | tf_op jit(solution)/shard_map/ppermute | solution.py:18
  37.9 9.2 %collective-permute-start.12 = (f32[2,4,16,128]{3,2,1,0:T(8,128)}, f32[2,4,16,128]{3,2,1,0:T(8,128)}, u32[]{:S(2)}, u32[]{:S(2)}) collective-permute-start(f32[2,4,16,128]{3,2,1,0:T(8,128)} %get-tuple-element.29), channel_id=1, source_target_pairs={{0,1},{1,0},{2,3},{3,2},{4,5},{5,4},{6,7},{7,6},{8,9},{9,8},{10,11... | collective-permute-start | bytes 196616 | tf_op jit(solution)/shard_map/ppermute | solution.py:93
  42.9 14.9 %collective-permute-start.6 = (bf16[5,144,256]{2,1,0:T(8,128)(2,1)S(1)}, bf16[5,144,256]{2,1,0:T(8,128)(2,1)}, u32[]{:S(2)}, u32[]{:S(2)}) collective-permute-start(bf16[5,144,256]{2,1,0:T(8,128)(2,1)S(1)} %constant_dynamic-update-slice_fusion.refs_0_), channel_id=1, source_target_pairs={{0,1},{1,0},{2,3},{3,2},{4,5},{5,4},{6,7},{7,6},{8,9},{9,8},{10,11... | collective-permute-start | bytes 1105928 | tf_op jit(solution)/shard_map/ppermute | solution.py:181
  44.6 13.2 %collective-permute-start.5 = (bf16[3,144,256]{2,1,0:T(8,128)(2,1)}, bf16[3,144,256]{2,1,0:T(8,128)(2,1)}, u32[]{:S(2)}, u32[]{:S(2)}) collective-permute-start(bf16[3,144,256]{2,1,0:T(8,128)(2,1)} %pad_maximum_fusion.9), channel_id=1, source_target_pairs={{0,2},{1,3},{2,0},{3,1},{4,6},{5,7},{6,4},{7,5},{8,10},{9,11},{10,... | collective-permute-start | bytes 663560 | tf_op jit(solution)/shard_map/ppermute | solution.py:181
  57.8 1.7 collective-permute-start.7
  59.5 1.6 copy-start.1
  66.0 0.8 copy-start.2
  110.6 1.0 copy-start.3
  118.1 9.0 %collective-permute-start.13 = (bf16[128,1280]{1,0:T(8,128)(2,1)S(1)}, bf16[128,1280]{1,0:T(8,128)(2,1)S(1)}, u32[]{:S(2)}, u32[]{:S(2)}) collective-permute-start(bf16[128,1280]{1,0:T(8,128)(2,1)S(1)} %get-tuple-element.10.own), channel_id=1, source_target_pairs={{0,1},{1,2},{2,3},{3,4},{4,5},{5,6},{6,7},{7,8},{8,9},{9,10},{10,1... | collective-permute-start | bytes 983048 | tf_op jit(solution)/shard_map/ppermute | solution.py:18
  120.3 6.8 %collective-permute-start.14 = (bf16[128,1280]{1,0:T(8,128)(2,1)S(1)}, bf16[128,1280]{1,0:T(8,128)(2,1)S(1)}, u32[]{:S(2)}, u32[]{:S(2)}) collective-permute-start(bf16[128,1280]{1,0:T(8,128)(2,1)S(1)} %get-tuple-element.10.own), channel_id=1, source_target_pairs={{1,0},{2,1},{3,2},{4,3},{5,4},{6,5},{7,6},{8,7},{9,8},{10,9},{11,1... | collective-permute-start | bytes 983048 | tf_op jit(solution)/shard_map/ppermute | solution.py:18
  127.0 11.7 %slice-start = ((s8[6291456]{0:T(1024)(128)(4,1)}), s8[2097152]{0:T(1024)(128)(4,1)S(1)}, s32[]{:S(2)}) async-start(s8[6291456]{0:T(1024)(128)(4,1)} %bitcast.201), calls=%async_computation.1 | async-start | bytes 4194304
  127.1 11.6 %slice-start.1 = ((s8[6291456]{0:T(1024)(128)(4,1)}), s8[4194304]{0:T(1024)(128)(4,1)S(1)}, s32[]{:S(2)}) async-start(s8[6291456]{0:T(1024)(128)(4,1)} %bitcast.201), calls=%async_computation.2 | async-start | bytes 8388608
  132.7 6.0 %copy-start.7 = (f32[2048]{0:T(1024)S(1)}, f32[2048]{0:T(1024)}, u32[]{:S(2)}) copy-start(f32[2048]{0:T(1024)} %param.23) | copy-start | bytes 24580
  133.8 16.1 %collective-permute-start.19 = (bf16[128,1280]{1,0:T(8,128)(2,1)S(1)}, bf16[128,1280]{1,0:T(8,128)(2,1)S(1)}, u32[]{:S(2)}, u32[]{:S(2)}) collective-permute-start(bf16[128,1280]{1,0:T(8,128)(2,1)S(1)} %multiply_convert_fusion.1), channel_id=1, source_target_pairs={{0,4},{1,5},{2,6},{3,7},{4,8},{5,9},{6,10},{7,11},{8,12},{9,13},{1... | collective-permute-start | bytes 983048 | tf_op jit(solution)/shard_map/ppermute | solution.py:93
  138.2 10.6 %collective-permute-start.15 = (bf16[128,1280]{1,0:T(8,128)(2,1)S(1)}, bf16[128,1280]{1,0:T(8,128)(2,1)S(1)}, u32[]{:S(2)}, u32[]{:S(2)}) collective-permute-start(bf16[128,1280]{1,0:T(8,128)(2,1)S(1)} %multiply_convert_fusion.1), channel_id=1, source_target_pairs={{0,2},{1,3},{2,0},{3,1},{4,6},{5,7},{6,4},{7,5},{8,10},{9,11},{10,... | collective-permute-start | bytes 983048 | tf_op jit(solution)/shard_map/ppermute | solution.py:93
  150.0 11.5 %collective-permute-start.20 = (bf16[128,1280]{1,0:T(8,128)(2,1)S(1)}, bf16[128,1280]{1,0:T(8,128)(2,1)S(1)}, u32[]{:S(2)}, u32[]{:S(2)}) collective-permute-start(bf16[128,1280]{1,0:T(8,128)(2,1)S(1)} %add_convert_fusion), channel_id=1, source_target_pairs={{0,4},{1,5},{2,6},{3,7},{4,8},{5,9},{6,10},{7,11},{8,12},{9,13},{1... | collective-permute-start | bytes 983048 | tf_op jit(solution)/shard_map/ppermute | solution.py:93
  150.9 12.1 %collective-permute-start.30 = (bf16[128,1280]{1,0:T(8,128)(2,1)S(1)}, bf16[128,1280]{1,0:T(8,128)(2,1)S(1)}, u32[]{:S(2)}, u32[]{:S(2)}) collective-permute-start(bf16[128,1280]{1,0:T(8,128)(2,1)S(1)} %collective-permute-done.19), channel_id=1, source_target_pairs={{0,2},{1,3},{2,0},{3,1},{4,6},{5,7},{6,4},{7,5},{8,10},{9,11},{10,... | collective-permute-start | bytes 983048 | tf_op jit(solution)/shard_map/ppermute | solution.py:93
  152.2 18.4 %collective-permute-start.16 = (bf16[2,128,1280]{2,1,0:T(8,128)(2,1)S(1)}, bf16[2,128,1280]{2,1,0:T(8,128)(2,1)S(1)}, u32[]{:S(2)}, u32[]{:S(2)}) collective-permute-start(bf16[2,128,1280]{2,1,0:T(8,128)(2,1)S(1)} %get-tuple-element.28), channel_id=1, source_target_pairs={{0,1},{1,0},{2,3},{3,2},{4,5},{5,4},{6,7},{7,6},{8,9},{9,8},{10,11... | collective-permute-start | bytes 1966088 | tf_op jit(solution)/shard_map/ppermute | solution.py:93
  161.5 8.8 %collective-permute-start.26 = (bf16[128,1280]{1,0:T(8,128)(2,1)S(1)}, bf16[128,1280]{1,0:T(8,128)(2,1)S(1)}, u32[]{:S(2)}, u32[]{:S(2)}) collective-permute-start(bf16[128,1280]{1,0:T(8,128)(2,1)S(1)} %collective-permute-done.20), channel_id=1, source_target_pairs={{0,2},{1,3},{2,0},{3,1},{4,6},{5,7},{6,4},{7,5},{8,10},{9,11},{10,... | collective-permute-start | bytes 983048 | tf_op jit(solution)/shard_map/ppermute | solution.py:93
  163.1 14.0 %collective-permute-start.31 = (bf16[2,128,1280]{2,1,0:T(8,128)(2,1)S(1)}, bf16[2,128,1280]{2,1,0:T(8,128)(2,1)S(1)}, u32[]{:S(2)}, u32[]{:S(2)}) collective-permute-start(bf16[2,128,1280]{2,1,0:T(8,128)(2,1)S(1)} %get-tuple-element.22), channel_id=1, source_target_pairs={{0,1},{1,0},{2,3},{3,2},{4,5},{5,4},{6,7},{7,6},{8,9},{9,8},{10,11... | collective-permute-start | bytes 1966088 | tf_op jit(solution)/shard_map/ppermute | solution.py:93
  163.2 12.4 %collective-permute-start.21 = (bf16[128,1280]{1,0:T(8,128)(2,1)S(1)}, bf16[128,1280]{1,0:T(8,128)(2,1)S(1)}, u32[]{:S(2)}, u32[]{:S(2)}) collective-permute-start(bf16[128,1280]{1,0:T(8,128)(2,1)S(1)} %collective-permute-done.20), channel_id=1, source_target_pairs={{0,4},{1,5},{2,6},{3,7},{4,8},{5,9},{6,10},{7,11},{8,12},{9,13},{1... | collective-permute-start | bytes 983048 | tf_op jit(solution)/shard_map/ppermute | solution.py:93
  170.5 15.1 %collective-permute-start.27 = (bf16[2,128,1280]{2,1,0:T(8,128)(2,1)S(1)}, bf16[2,128,1280]{2,1,0:T(8,128)(2,1)S(1)}, u32[]{:S(2)}, u32[]{:S(2)}) collective-permute-start(bf16[2,128,1280]{2,1,0:T(8,128)(2,1)S(1)} %get-tuple-element.24), channel_id=1, source_target_pairs={{0,1},{1,0},{2,3},{3,2},{4,5},{5,4},{6,7},{7,6},{8,9},{9,8},{10,11... | collective-permute-start | bytes 1966088 | tf_op jit(solution)/shard_map/ppermute | solution.py:93
  175.1 51.0 %collective-permute-start.17 = (bf16[2,128,2048]{2,1,0:T(8,128)(2,1)S(1)}, bf16[2,128,2048]{2,1,0:T(8,128)(2,1)S(1)}, u32[]{:S(2)}, u32[]{:S(2)}) collective-permute-start(bf16[2,128,2048]{2,1,0:T(8,128)(2,1)S(1)} %bitcast.182), channel_id=1, source_target_pairs={{0,1},{1,0},{2,3},{3,2},{4,5},{5,4},{6,7},{7,6},{8,9},{9,8},{10,11... | collective-permute-start | bytes 3145736 | tf_op jit(solution)/shard_map/ppermute | solution.py:93
  175.6 9.7 %collective-permute-start.22 = (bf16[128,1280]{1,0:T(8,128)(2,1)S(1)}, bf16[128,1280]{1,0:T(8,128)(2,1)S(1)}, u32[]{:S(2)}, u32[]{:S(2)}) collective-permute-start(bf16[128,1280]{1,0:T(8,128)(2,1)S(1)} %collective-permute-done.21), channel_id=1, source_target_pairs={{0,2},{1,3},{2,0},{3,1},{4,6},{5,7},{6,4},{7,5},{8,10},{9,11},{10,... | collective-permute-start | bytes 983048 | tf_op jit(solution)/shard_map/ppermute | solution.py:93
  181.6 13.9 %collective-permute-start.32 = (bf16[2,128,2048]{2,1,0:T(8,128)(2,1)S(1)}, bf16[2,128,2048]{2,1,0:T(8,128)(2,1)S(1)}, u32[]{:S(2)}, u32[]{:S(2)}) collective-permute-start(bf16[2,128,2048]{2,1,0:T(8,128)(2,1)S(1)} %bitcast.183), channel_id=1, source_target_pairs={{0,1},{1,0},{2,3},{3,2},{4,5},{5,4},{6,7},{7,6},{8,9},{9,8},{10,11... | collective-permute-start | bytes 3145736 | tf_op jit(solution)/shard_map/ppermute | solution.py:93
  185.4 5.2 %collective-permute-start.23 = (bf16[2,128,1280]{2,1,0:T(8,128)(2,1)S(1)}, bf16[2,128,1280]{2,1,0:T(8,128)(2,1)S(1)}, u32[]{:S(2)}, u32[]{:S(2)}) collective-permute-start(bf16[2,128,1280]{2,1,0:T(8,128)(2,1)S(1)} %get-tuple-element.26), channel_id=1, source_target_pairs={{0,1},{1,0},{2,3},{3,2},{4,5},{5,4},{6,7},{7,6},{8,9},{9,8},{10,11... | collective-permute-start | bytes 1966088 | tf_op jit(solution)/shard_map/ppermute | solution.py:93
  190.1 7.3 %collective-permute-start.28 = (bf16[2,128,2048]{2,1,0:T(8,128)(2,1)S(1)}, bf16[2,128,2048]{2,1,0:T(8,128)(2,1)S(1)}, u32[]{:S(2)}, u32[]{:S(2)}) collective-permute-start(bf16[2,128,2048]{2,1,0:T(8,128)(2,1)S(1)} %bitcast.185), channel_id=1, source_target_pairs={{0,1},{1,0},{2,3},{3,2},{4,5},{5,4},{6,7},{7,6},{8,9},{9,8},{10,11... | collective-permute-start | bytes 3145736 | tf_op jit(solution)/shard_map/ppermute | solution.py:93
  195.4 16.2 %collective-permute-start.24 = (bf16[2,128,2048]{2,1,0:T(8,128)(2,1)S(1)}, bf16[2,128,2048]{2,1,0:T(8,128)(2,1)S(1)}, u32[]{:S(2)}, u32[]{:S(2)}) collective-permute-start(bf16[2,128,2048]{2,1,0:T(8,128)(2,1)S(1)} %bitcast.184), channel_id=1, source_target_pairs={{0,1},{1,0},{2,3},{3,2},{4,5},{5,4},{6,7},{7,6},{8,9},{9,8},{10,11... | collective-permute-start | bytes 3145736 | tf_op jit(solution)/shard_map/ppermute | solution.py:93
  195.9 14.8 %collective-permute-start.33 = (bf16[128,2048]{1,0:T(8,128)(2,1)S(1)}, bf16[128,2048]{1,0:T(8,128)(2,1)S(1)}, u32[]{:S(2)}, u32[]{:S(2)}) collective-permute-start(bf16[128,2048]{1,0:T(8,128)(2,1)S(1)} %fusion.59), channel_id=1, source_target_pairs={{0,2},{1,3},{2,0},{3,1},{4,6},{5,7},{6,4},{7,5},{8,10},{9,11},{10,... | collective-permute-start | bytes 1572872 | tf_op jit(solution)/shard_map/ppermute | solution.py:93
  197.8 24.1 %collective-permute-start.29 = (bf16[128,2048]{1,0:T(8,128)(2,1)S(1)}, bf16[128,2048]{1,0:T(8,128)(2,1)S(1)}, u32[]{:S(2)}, u32[]{:S(2)}) collective-permute-start(bf16[128,2048]{1,0:T(8,128)(2,1)S(1)} %fusion.58), channel_id=1, source_target_pairs={{0,2},{1,3},{2,0},{3,1},{4,6},{5,7},{6,4},{7,5},{8,10},{9,11},{10,... | collective-permute-start | bytes 1572872 | tf_op jit(solution)/shard_map/ppermute | solution.py:93
  210.8 15.0 %collective-permute-start.34 = (bf16[128,2048]{1,0:T(8,128)(2,1)S(1)}, bf16[128,2048]{1,0:T(8,128)(2,1)S(1)}, u32[]{:S(2)}, u32[]{:S(2)}) collective-permute-start(bf16[128,2048]{1,0:T(8,128)(2,1)S(1)} %fusion.33), channel_id=1, source_target_pairs={{0,4},{1,5},{2,6},{3,7},{4,8},{5,9},{6,10},{7,11},{8,12},{9,13},{1... | collective-permute-start | bytes 1572872 | tf_op jit(solution)/shard_map/ppermute | solution.py:93
  212.0 21.1 %collective-permute-start.25 = (bf16[128,2048]{1,0:T(8,128)(2,1)S(1)}, bf16[128,2048]{1,0:T(8,128)(2,1)S(1)}, u32[]{:S(2)}, u32[]{:S(2)}) collective-permute-start(bf16[128,2048]{1,0:T(8,128)(2,1)S(1)} %fusion.57), channel_id=1, source_target_pairs={{0,2},{1,3},{2,0},{3,1},{4,6},{5,7},{6,4},{7,5},{8,10},{9,11},{10,... | collective-permute-start | bytes 1572872 | tf_op jit(solution)/shard_map/ppermute | solution.py:93
  226.0 14.0 %collective-permute-start.35 = (bf16[128,2048]{1,0:T(8,128)(2,1)S(1)}, bf16[128,2048]{1,0:T(8,128)(2,1)S(1)}, u32[]{:S(2)}, u32[]{:S(2)}) collective-permute-start(bf16[128,2048]{1,0:T(8,128)(2,1)S(1)} %fusion.36), channel_id=1, source_target_pairs={{0,4},{1,5},{2,6},{3,7},{4,8},{5,9},{6,10},{7,11},{8,12},{9,13},{1... | collective-permute-start | bytes 1572872 | tf_op jit(solution)/shard_map/ppermute | solution.py:93
  226.5 17.5 %collective-permute-start.18 = (bf16[128,2048]{1,0:T(8,128)(2,1)S(1)}, bf16[128,2048]{1,0:T(8,128)(2,1)S(1)}, u32[]{:S(2)}, u32[]{:S(2)}) collective-permute-start(bf16[128,2048]{1,0:T(8,128)(2,1)S(1)} %fusion.56), channel_id=1, source_target_pairs={{0,2},{1,3},{2,0},{3,1},{4,6},{5,7},{6,4},{7,5},{8,10},{9,11},{10,... | collective-permute-start | bytes 1572872 | tf_op jit(solution)/shard_map/ppermute | solution.py:93
  240.2 13.1 %collective-permute-start.36 = (bf16[128,2048]{1,0:T(8,128)(2,1)S(1)}, bf16[128,2048]{1,0:T(8,128)(2,1)S(1)}, u32[]{:S(2)}, u32[]{:S(2)}) collective-permute-start(bf16[128,2048]{1,0:T(8,128)(2,1)S(1)} %fusion.39), channel_id=1, source_target_pairs={{0,4},{1,5},{2,6},{3,7},{4,8},{5,9},{6,10},{7,11},{8,12},{9,13},{1... | collective-permute-start | bytes 1572872 | tf_op jit(solution)/shard_map/ppermute | solution.py:93
Sparse Core Ops, SparseCore 0:
  10.7 99.8 all-gather.2
